TPU v7x, 128 devices: a whole 4x4x4 slice. The times are simulated.
128 devices in a mesh: face: 16 (over y, z_hi, core), sample: 8 (over x, z_lo).
Axes of the slice: x: 4, y: 4, z: 4 (z_hi: 2, z_lo: 2; z = z_hi * 2 + z_lo), core: 2. Of those that a mesh axis runs over, the one named last changes fastest.
Arguments:
- fields: bfloat16 [24, 48, 128, 256], P('sample', 'face'), may hold values from -6 to 6
- sample_index: int32 [16], P('sample'), may hold values from 0 to 2
- halo_index: int32 [48, 68], P('face'), may hold values from 0 to 3071, as said below
- channel_mask: int32 [128], replicated, may hold values 0 or 1
- weight: bfloat16 [1152, 256], replicated, may hold values from -0.1875 to 0.1875
Outputs:
- moments: float32 [1152, 1408], P(('face', 'sample'))
Inputs may be any that keep to these rules, and one draw needn't show every extreme that they name: `halo_index`: every cycle pixel names an edge-table entry; the four sides of a subface each follow one edge of some subface, in one of the two directions.
All inputs are finite; a program needn't handle non-finite values.
Results may differ from a plain program's by a relative error of at most 0.0005.
Values may be sent and summed in bfloat16 or wider, within the bound.
No kernel may reach another device: no remote copies, remote signals or barrier semaphores. Data moves between devices by JAX's collectives and lax.ppermute only.
A program may use at most 64 MiB of HBM per device.

v0:
```python
import jax
import jax.numpy as jnp
from jax import lax
from jax.sharding import PartitionSpec as P

P_SIZE = 16


def strip_edges(selected, side):
    grid = selected.reshape(selected.shape[0], selected.shape[1], selected.shape[2], side, side)
    edges = jnp.concatenate(
        [grid[..., 0, :], grid[..., side - 1, :], grid[..., :, 0], grid[..., :, side - 1]], axis=-1
    )
    edges = jnp.transpose(edges, (0, 2, 1, 3))
    return edges.reshape(edges.shape[0], edges.shape[1], -1)


def build_patches(selected, table, halo_index, side):
    count = selected.shape[0]
    subs = selected.shape[1]
    chans = selected.shape[2]
    flat = halo_index.reshape(-1)
    cycle = jnp.take(table, flat, axis=2).reshape(count, chans, subs, 4 * side + 4)
    cycle = jnp.transpose(cycle, (0, 2, 1, 3))
    grid = selected.reshape(count, subs, chans, side, side)
    top = cycle[..., 0 : side + 2]
    bottom = cycle[..., side + 2 : 2 * side + 4]
    left = cycle[..., 2 * side + 4 : 3 * side + 4]
    right = cycle[..., 3 * side + 4 : 4 * side + 4]
    middle = jnp.concatenate([left[..., :, None], grid, right[..., :, None]], axis=-1)
    padded = jnp.concatenate([top[..., None, :], middle, bottom[..., None, :]], axis=-2)
    taps = [padded[..., dy : dy + side, dx : dx + side] for dy in range(3) for dx in range(3)]
    stacked = jnp.stack(taps, axis=2)
    stacked = jnp.transpose(stacked, (0, 1, 4, 5, 2, 3))
    return stacked.reshape(count * subs * side * side, 9 * chans)


def per_device(fields, sample_index, halo_index, channel_mask, weight):
    selected = jnp.take(fields, sample_index, axis=0)
    edges = strip_edges(selected, P_SIZE)
    table = lax.all_gather(edges, "face", axis=2, tiled=True)
    patches = build_patches(selected, table, halo_index, P_SIZE)
    target = jnp.dot(patches, weight, preferred_element_type=jnp.float32).astype(jnp.bfloat16)
    column_mask = jnp.tile(channel_mask, 9).astype(patches.dtype)
    kept = patches * column_mask[None, :]
    right_side = jnp.concatenate([kept, target], axis=1)
    face_count = lax.axis_size("face")
    sample_count = lax.axis_size("sample")
    summed = lax.psum_scatter(
        lax.dot_general(
            kept, right_side, (((0,), (0,)), ((), ())), preferred_element_type=jnp.float32
        ),
        ("face", "sample"),
        scatter_dimension=0,
        tiled=True,
    )
    pixels = selected.shape[0] * selected.shape[1] * P_SIZE * P_SIZE * face_count * sample_count
    return summed / pixels


def solution(mesh):
    placed = (P("sample", "face", None, None), P("sample"), P("face", None), P(), P())
    return jax.shard_map(
        per_device,
        mesh=mesh,
        in_specs=placed,
        out_specs=P(("face", "sample"), None),
        check_vma=False,
    )
```

profile of v0, /device:TPU:1, one launch (start us, length us, event | category | flops | bytes accessed | tf_op | source)
XLA Modules:
  0.0 251.0 jit_solution(16624494259656536826)
XLA Ops:
  6.5 0.7 compare_select_fusion.2
  7.3 0.7 compare_and_fusion
  7.9 1.6 gather_fusion
  9.6 0.2 copy.38
  9.8 0.1 broadcast_select_fusion
  9.9 0.1 fusion.22
  10.1 0.8 copy.40
  10.8 0.0 all-gather.2.cloned.1.call-update
  10.8 0.0 all-reduce.3.cloned.1.call-start
  10.9 0.8 reshape.72
  11.7 0.7 convert_element_type.14
  12.3 0.7 compare_and_fusion.1
  13.0 48.4 %all-gather.2.cloned.1.call-done = bf16[2,128,3072]{1,0,2:T(2,128)(2,1)} async-done(((bf16[2,128,192]{1,0,2:T(2,128)(2,1)}), bf16[2,128,3072]{1,0,2:T(2,128)(2,1)}) %all-gather.2.cloned.1.call-update) | async-done | bytes 1572880 | tf_op jit(solution)/shard_map/all_gather | solution.py:41
  61.5 2.3 gather_fusion.1
  63.7 0.1 fusion.20
  64.0 0.5 pad_maximum_fusion
  64.6 0.2 fusion.18
  64.8 0.2 fusion.17
  65.0 0.2 fusion.16
  65.2 0.2 select_dynamic-update-slice_fusion
  65.4 0.3 fusion.14
  65.6 0.1 fusion.12
  65.7 0.2 fusion.11
  65.9 0.2 fusion.10
  66.1 4.5 %copy.49 = bf16[2,3,16,16,9,128]{5,4,3,2,1,0:T(8,128)(2,1)S(1)} copy(bf16[2,3,16,16,9,128]{5,3,2,1,0,4:T(8,128)(2,1)S(1)} %bitcast.78) | data formatting | bytes 7077888 | tf_op jit(solution)/shard_map/transpose | solution.py:34
  70.6 2.6 %bitcast_multiply_fusion = bf16[1536,1152]{1,0:T(8,128)(2,1)} fusion(bf16[1152]{0:T(1024)(128)(2,1)S(1)} %broadcast_bitcast_fusion, bf16[192,8,9,128]{3,2,1,0:T(8,128)(2,1)S(1)} %bitcast.76), kind=kLoop, calls=%fused_computation.8 | loop fusion | flops 1769472 | bytes 7080192 | tf_op jit(solution)/shard_map/mul | solution.py:45
  73.2 1.3 fusion.6
  74.6 0.3 copy.50
  74.9 11.7 %fusion = f32[1152,1408]{1,0:T(8,128)} fusion(bf16[1536,1152]{1,0:T(8,128)(2,1)} %bitcast_multiply_fusion, bf16[1536,256]{1,0:T(8,128)(2,1)S(1)} %copy.50), kind=kOutput, calls=%fused_computation.2 | convolution fusion | flops 4991483904 | bytes 10813440 | tf_op jit(solution)/shard_map/dot_general | solution.py:50
  86.6 0.0 all-reduce.3.cloned.1.call-update
  86.6 156.0 %all-reduce.3.cloned.1.call-done = f32[1152,1408]{1,0:T(8,128)} async-done(((f32[1152,1408]{1,0:T(8,128)}), f32[1152,1408]{1,0:T(8,128)}) %all-reduce.3.cloned.1.call-update) | async-done | bytes 6488080
  242.6 1.6 dynamic-slice_multiply_fusion
  (15 shorter events, 0.2 us)
Async XLA Ops:
  6.5 66.7 %copy-start = (bf16[1152,256]{1,0:T(8,128)(2,1)S(1)}, bf16[1152,256]{1,0:T(8,128)(2,1)}, u32[]{:S(2)}) copy-start(bf16[1152,256]{1,0:T(8,128)(2,1)} %param.9) | copy-start | bytes 1769476
  6.5 54.9 %all-gather.2.cloned.1.call-start = ((), (), s32[]{:S(2)}) async-start(), calls=%async_computation | async-start | bytes 1671168 | tf_op jit(solution)/shard_map/all_gather | solution.py:41
  10.8 231.8 %all-reduce.3.cloned.1.call-start = ((), (), s32[]{:S(2)}) async-start(), calls=%async_computation.1 | async-start | bytes 12976128
Sparse Core Ops, SparseCore 0:
  11.0 50.4 all-gather.1
  86.7 155.8 all-reduce.2
where the time goes:
time: 251 us
  waiting for transfers between devices  205 us (82%)
  between operations  13.6 us (5%)
  matrix products  13.1 us (5%)
  local copies, waits for them, and re-layouts  11.5 us (5%)
  other arithmetic  8.31 us (3%)
    unnamed x3, waiting for transfers between devices  156 us
    all_gather x1, waiting for transfers between devices, per_device(): table = lax.all_gather(edges, 'face', axis=2, tiled=True)  48.4 us
    dot_general x1, matrix products, per_device(): lax.dot_general(kept, right_side, (((0,), (0,)), ((), ())), preferred_ele...  11.7 us
  transfers between devices with their start and end apart: 2, of which 2 were waited for; matrix products, arithmetic and copies ran while one was open for 1% of the time, Pallas kernels for 0%

commit v1 on v0

v1 whole, which is shorter than its diff:
```python
import functools

import jax
import jax.numpy as jnp
import ml_dtypes
import numpy as np
from jax import lax
from jax.experimental import pallas as pl
from jax.experimental.pallas import tpu as pltpu
from jax.sharding import PartitionSpec as P

SIDE = 16
PIX = SIDE * SIDE
CH = 128
TAPS = 9
K = TAPS * CH
HALF = K // 2
CYCLE = 4 * SIDE + 4
ROWS = 88
AXES = ("face", "sample")
NT = (((1,), (1,)), ((), ()))
SIDE_AT = (1, 19, 36, 52)
CORNER_AT = (0, 17, 18, 35)


def edge_picker():
    out = np.zeros((4 * SIDE, PIX), np.float32)
    for i in range(SIDE):
        out[i, i] = 1
        out[SIDE + i, (SIDE - 1) * SIDE + i] = 1
        out[2 * SIDE + i, i * SIDE] = 1
        out[3 * SIDE + i, i * SIDE + SIDE - 1] = 1
    return out.astype(ml_dtypes.bfloat16)


def tap_matrices():
    out = np.zeros((TAPS, PIX + CH, PIX), np.float32)
    for t in range(TAPS):
        for y in range(SIDE):
            for x in range(SIDE):
                u, v = y + t // 3, x + t % 3
                if u == 0:
                    k = PIX + v
                elif u == SIDE + 1:
                    k = PIX + SIDE + 2 + v
                elif v == 0:
                    k = PIX + 2 * SIDE + 4 + u - 1
                elif v == SIDE + 1:
                    k = PIX + 3 * SIDE + 4 + u - 1
                else:
                    k = (u - 1) * SIDE + v - 1
                out[t, k, y * SIDE + x] = 1
    return out.astype(ml_dtypes.bfloat16)


def source_base():
    out = np.full((1, CH), -1000, np.int32)
    for e, at in enumerate(SIDE_AT):
        out[0, at : at + SIDE] = e * SIDE
    for e, at in enumerate(CORNER_AT):
        out[0, at] = (4 + e) * SIDE
    return out


def edges_kernel(index_ref, fields_ref, pick_ref, copies_ref, own_ref):
    subs = fields_ref.shape[1]
    for s in range(2):
        for f in range(subs):
            x = fields_ref[index_ref[s], f]
            u = s * subs + f
            own_ref[u * CH : (u + 1) * CH, :] = x
            edges = lax.dot_general(pick_ref[...], x, NT, preferred_element_type=jnp.float32)
            edges = edges.astype(jnp.bfloat16)
            for d in range(copies_ref.shape[0]):
                copies_ref[d, u * 4 * SIDE : (u + 1) * 4 * SIDE, :] = edges


def moments_kernel(
    subs,
    core_ref,
    halo_own_ref,
    halo_other_ref,
    own_ref,
    other_ref,
    table_own_ref,
    table_other_ref,
    position_ref,
    base_ref,
    taps_ref,
    kept_row_ref,
    kept_lane_ref,
    message_ref,
    tiles,
    grid,
    patches,
    gram,
):
    core = core_ref[0]
    units = 4 * subs
    half = units // 2

    for side, halo_ref in enumerate((halo_own_ref, halo_other_ref)):
        for f in range(subs):
            for n, at in enumerate(SIDE_AT + CORNER_AT):
                index = halo_ref[f, at]
                sub = index // (4 * SIDE)
                edge = lax.rem(index // SIDE, 4)
                device = sub // subs
                local = sub - device * subs
                near = lax.rem(device, 2) == core
                for s in range(2):
                    row = pl.multiple_of((s * subs + local) * 4 * SIDE + edge * SIDE, SIDE)
                    mine = table_own_ref[device // 2, pl.ds(row, SIDE), :]
                    theirs = table_other_ref[device // 2, pl.ds(row, SIDE), :]
                    u = side * half + s * subs + f
                    tiles[u * CH + n * SIDE : u * CH + (n + 1) * SIDE, :] = jnp.where(near, mine, theirs)

    row_at = lax.broadcasted_iota(jnp.int32, (CH, CH), 0)
    col_at = lax.broadcasted_iota(jnp.int32, (CH, CH), 1)
    eye = jnp.where(row_at == col_at, 1.0, 0.0).astype(jnp.bfloat16)
    turned = lax.dot_general(eye, tiles[...], NT, preferred_element_type=jnp.float32).astype(jnp.bfloat16)
    largest = jnp.zeros((CH, CH), jnp.float32)
    for u in range(units):
        side, f = u // half, u % half % subs
        source = position_ref[side * subs + f : side * subs + f + 1, :] + base_ref[...]
        pick = jnp.where(row_at == source, 1.0, 0.0).astype(jnp.bfloat16)
        cycle = jnp.dot(turned[:, u * CH : (u + 1) * CH], pick, preferred_element_type=jnp.float32)
        x = (own_ref if side == 0 else other_ref)[(u % half) * CH : (u % half + 1) * CH, :]
        grid[u * CH : (u + 1) * CH, :PIX] = x
        grid[u * CH : (u + 1) * CH, PIX:] = cycle.astype(jnp.bfloat16)
        size = jnp.abs(x.astype(jnp.float32))
        largest = jnp.maximum(largest, jnp.maximum(size[:, :CH], size[:, CH:]))
        largest = jnp.maximum(largest, jnp.abs(cycle))

    kept_row = kept_row_ref[...]

    def exponent(values):
        top = jnp.maximum(jnp.max(values), 2.0**-60)
        return jnp.ceil(jnp.log2(jnp.full((8, CH), top, jnp.float32)))

    kept_exp = exponent(jnp.where(kept_row > 0, largest, 0.0))
    any_exp = exponent(largest)
    row_scale = jnp.where(kept_row > 0, jnp.exp2(-kept_exp[0:1, :]), 0.0)
    lane_exps = jnp.where(kept_lane_ref[...] > 0, kept_exp, any_exp)
    lane_scale = jnp.exp2(-lane_exps)

    chunk = units * CH // 3
    for t in range(TAPS):
        for m in range(0, units * CH, chunk):
            if t == TAPS // 2:
                values = grid[m : m + chunk, :PIX]
            else:
                values = jnp.dot(grid[m : m + chunk, :], taps_ref[t], preferred_element_type=jnp.float32)
                values = values.astype(jnp.bfloat16)
            for n in range(chunk // CH):
                u = m // CH + n
                patches[t * CH : (t + 1) * CH, u * PIX : (u + 1) * PIX] = values[n * CH : (n + 1) * CH, :]

    right = patches[pl.ds(pl.multiple_of(core * HALF, HALF), HALF), :]
    for t in range(0, TAPS, 3):
        block = lax.dot_general(
            patches[t * CH : (t + 3) * CH, :], right, NT, preferred_element_type=jnp.float32
        )
        for n in range(3):
            rows = block[n * CH : (n + 1) * CH, :]
            for l in range(4):
                part = rows[:, l * CH : (l + 1) * CH] * row_scale * lane_scale[0:1, :]
                gram[l, (t + n) * CH : (t + n + 1) * CH, :] = part
            part = rows[:, 4 * CH :] * row_scale[:, : CH // 2] * lane_scale[1:2, : CH // 2]
            gram[4, (t + n) * CH : (t + n + 1) * CH, : CH // 2] = part

    for g in range(8):
        for s in range(8):
            j = g * 8 + s
            at = g * 144 + s * 9
            for c in range(2):
                for l in range(4):
                    to = (c * 4 + l) * 9
                    message_ref[j, to : to + 9, :] = gram[l, at + c * 72 : at + c * 72 + 9, :]
                message_ref[j, 72:81, c * 64 : (c + 1) * 64] = gram[4, at + c * 72 : at + c * 72 + 9, : CH // 2]
            message_ref[j, 81:88, :] = (lane_exps + kept_exp)[0:7, :]


def rows_kernel(place_ref, mask_ref, near_ref, far_ref, weight_ref, kept_ref, out_ref, rows):
    core, owner = place_ref[0], place_ref[1]
    near, far = near_ref[...], far_ref[...]
    low = jnp.where(core == 0, near, far)
    high = jnp.where(core == 0, far, near)

    def mine(values, l):
        return jnp.where(core == 0, values[l * 9 : l * 9 + 9, :], values[(4 + l) * 9 : (4 + l) * 9 + 9, :])

    def middle(values):
        return jnp.where(core == 0, values[72:81, : CH // 2], values[72:81, CH // 2 :])

    for l in range(4):
        rows[0:9, l * CH : (l + 1) * CH] = mine(low, l)
        rows[0:9, HALF + l * CH : HALF + (l + 1) * CH] = mine(high, l)
    rows[0:9, 4 * CH : HALF] = middle(low)
    rows[0:9, HALF + 4 * CH :] = middle(high)

    at = lax.broadcasted_iota(jnp.int32, (9, CH), 0)
    keep = jnp.zeros((9, CH), jnp.float32)
    for k in range(9):
        bit = mask_ref[lax.rem(owner * 9 + k, CH)]
        keep = jnp.where(at == k, bit.astype(jnp.float32), keep)
    whole = rows[0:9, :]
    head = whole.astype(jnp.bfloat16)
    left = whole - head.astype(jnp.float32)
    tail = left.astype(jnp.bfloat16)
    rest = (left - tail.astype(jnp.float32)).astype(jnp.bfloat16)
    weight = weight_ref[...]
    product = jnp.dot(rest, weight, preferred_element_type=jnp.float32)
    product += jnp.dot(tail, weight, preferred_element_type=jnp.float32)
    product += jnp.dot(head, weight, preferred_element_type=jnp.float32)
    count = place_ref[2].astype(jnp.float32)
    kept = kept_ref[...]
    for t in range(TAPS):
        part = whole[:, t * CH : (t + 1) * CH]
        out_ref[:, t * CH : (t + 1) * CH] = jnp.where((keep > 0) & (kept > 0), part / count, 0.0)
    for n in range(2):
        part = product[:, n * CH : (n + 1) * CH]
        out_ref[:, K + n * CH : K + (n + 1) * CH] = jnp.where(keep > 0, part / count, 0.0)


VMEM = pl.BlockSpec(memory_space=pltpu.VMEM)
SMEM = pl.BlockSpec(memory_space=pltpu.SMEM)


def shape(dims, kind):
    return jax.ShapeDtypeStruct(dims, kind)


def per_device(fields, sample_index, halo_index, channel_mask, weight):
    faces, samples = lax.axis_size("face"), lax.axis_size("sample")
    face, sample = lax.axis_index("face"), lax.axis_index("sample")
    core = lax.rem(face, 2)
    subs = fields.shape[1]
    units = 4 * subs
    swap = [(f, f ^ 1) for f in range(faces)]
    bf16, f32 = jnp.bfloat16, jnp.float32

    copies, own = pl.pallas_call(
        edges_kernel,
        out_shape=(shape((faces // 2, 8 * subs * SIDE, CH), bf16), shape((units // 2 * CH, PIX), bf16)),
        in_specs=[SMEM, VMEM, VMEM],
        out_specs=(VMEM, VMEM),
        name="edges",
    )(sample_index, fields, jnp.asarray(edge_picker()))

    other = lax.ppermute(own, "face", swap)
    halo_other = lax.ppermute(halo_index, "face", swap)
    same_core = [[f for f in range(c, faces, 2)] for c in range(2)]
    table = lax.all_to_all(copies, "face", 0, 0, axis_index_groups=same_core)
    table_other = lax.ppermute(table, "face", swap)

    both = jnp.concatenate([halo_index, halo_other], axis=0)
    position = jnp.pad(lax.rem(both, SIDE), ((0, 0), (0, CH - CYCLE)))
    keep = channel_mask.astype(f32)
    kept_row = jnp.broadcast_to(keep[:, None], (CH, CH))
    rolled = jnp.where(core == 0, keep, jnp.roll(keep, CH // 2))
    folded = jnp.concatenate([rolled[: CH // 2], rolled[: CH // 2]])
    kept_lane = jnp.concatenate([rolled[None], jnp.broadcast_to(folded[None], (7, CH))], axis=0)

    message = pl.pallas_call(
        functools.partial(moments_kernel, subs),
        out_shape=shape((64, ROWS, CH), f32),
        in_specs=[SMEM] * 3 + [VMEM] * 9,
        out_specs=VMEM,
        scratch_shapes=[
            pltpu.VMEM((units * CH, CH), bf16),
            pltpu.VMEM((units * CH, PIX + CH), bf16),
            pltpu.VMEM((K, units * PIX), bf16),
            pltpu.VMEM((5, K, CH), f32),
        ],
        compiler_params=pltpu.CompilerParams(vmem_limit_bytes=56 * 2**20),
        name="moments",
    )(
        core[None],
        halo_index,
        halo_other,
        own,
        other,
        table,
        table_other,
        position,
        jnp.asarray(source_base()),
        jnp.asarray(tap_matrices()),
        kept_row,
        kept_lane,
    )

    groups = [[f * samples + s for f in range(c, faces, 2) for s in range(samples)] for c in range(2)]
    landed = lax.all_to_all(message.astype(jnp.float16), AXES, 0, 0, axis_index_groups=groups)
    landed = landed.astype(f32)
    exps = jnp.where(jnp.arange(ROWS)[None, :, None] < 72, landed[:, 81:82, :], landed[:, 82:83, :])
    near = jnp.sum(landed * jnp.exp2(exps), axis=0)
    far = lax.ppermute(near, "face", swap)

    pixels = 2 * subs * PIX * faces * samples
    place = jnp.stack([core, face * samples + sample, jnp.int32(pixels)])
    return pl.pallas_call(
        rows_kernel,
        out_shape=shape((TAPS, K + weight.shape[1]), f32),
        in_specs=[SMEM] * 2 + [VMEM] * 4,
        out_specs=VMEM,
        scratch_shapes=[pltpu.VMEM((16, K), f32)],
        name="rows",
    )(place, channel_mask, near, far, weight, keep[None])


def solution(mesh):
    placed = (P("sample", "face", None, None), P("sample"), P("face", None), P(), P())
    return jax.shard_map(
        per_device,
        mesh=mesh,
        in_specs=placed,
        out_specs=P(("face", "sample"), None),
        check_vma=False,
    )
```

time: 251 us -> 85.6 us (0.34)
  waiting for transfers between devices: 205 us -> 34.9 us
  Pallas kernels: 0 us -> 20.6 us
  starting transfers between devices: 0.04 us -> 19.3 us
  between operations: 13.6 us -> 0.07 us
  matrix products: 13.1 us -> 0 us
  local copies, waits for them, and re-layouts: 11.5 us -> 2.41 us
    unnamed x3 -> x0, waiting for transfers between devices: 156 us -> none
    all_gather x1 -> x0, waiting for transfers between devices: 48.4 us -> none  [per_device(): table = lax.all_gather(edges, 'face', axis=2, tiled=True)]
    all_to_all x0 -> x2, waiting for transfers between devices: none -> 34.7 us  [the longest x1 22.6 us: per_device(): lax.all_to_all(message.astype(jnp.float16), AXES, 0, 0, axis_index_groups...]
    pallas_call x0 -> x3, Pallas kernels: none -> 20.6 us  [the longest x1 16.1 us: per_device(): pl.pallas_call(functools.partial(moments_kernel, subs), out_shape=shape((...]
    all_to_all x0 -> x2, starting transfers between devices: none -> 15.5 us  [the longest x1 8.33 us: per_device(): table = lax.all_to_all(copies, 'face', 0, 0, axis_index_groups=same_core)]
    dot_general x2 -> x0, matrix products: 13.1 us -> none  [the longest x1 11.7 us: per_device(): lax.dot_general(kept, right_side, (((0,), (0,)), ((), ())), preferred_ele...]
    transpose x1 -> x0, local copies, waits for them, and re-layouts: 4.54 us -> none  [build_patches(): stacked = jnp.transpose(stacked, (0, 1, 4, 5, 2, 3))]
    gather x3 -> x0, local copies, waits for them, and re-layouts: 4.14 us -> none  [the longest x1 2.27 us: build_patches(): jnp.take(table, flat, axis=2).reshape(count, chans, subs, 4 * side + 4)]
  transfers between devices with their start and end apart: 2 -> 6, of which waited for: 2 -> 3; matrix products, arithmetic and copies ran while one was open for 1% -> 5% of each run, Pallas kernels for 0% -> 0%
where the time goes in v1:
time: 85.6 us; the launch traced here: 85.2 us
  waiting for transfers between devices  34.9 us (41%)
  Pallas kernels  20.6 us (24%)
  starting transfers between devices  19.3 us (23%)
  other arithmetic  7.98 us (9%)
  local copies, waits for them, and re-layouts  2.41 us (3%)
    all_to_all x1, waiting for transfers between devices, per_device(): lax.all_to_all(message.astype(jnp.float16), AXES, 0, 0, axis_index_groups...  22.6 us
    pallas_call x1, Pallas kernels, per_device(): pl.pallas_call(functools.partial(moments_kernel, subs), out_shape=shape((...  16.1 us
    all_to_all x1, waiting for transfers between devices, per_device(): table = lax.all_to_all(copies, 'face', 0, 0, axis_index_groups=same_core)  12 us
    all_to_all x1, starting transfers between devices, per_device(): table = lax.all_to_all(copies, 'face', 0, 0, axis_index_groups=same_core)  8.33 us
    all_to_all x1, starting transfers between devices, per_device(): lax.all_to_all(message.astype(jnp.float16), AXES, 0, 0, axis_index_groups...  7.18 us
    convert_element_type x1, other arithmetic, per_device(): message.astype(jnp.float16)  3.1 us
    pallas_call x1, Pallas kernels, per_device(): pl.pallas_call(edges_kernel, out_shape=(shape((faces // 2, 8 * subs * SID...  2.26 us
    pallas_call x1, Pallas kernels, per_device(): pl.pallas_call(rows_kernel, out_shape=shape((TAPS, K + weight.shape[1]),...  2.21 us
  transfers between devices with their start and end apart: 6, of which 3 were waited for; matrix products, arithmetic and copies ran while one was open for 5% of the time, Pallas kernels for 0%

profile of v1, /device:TPU:1, one launch (start us, length us, event | category | flops | bytes accessed | tf_op | source)
XLA Modules:
  0.0 85.2 jit_solution(18067365966467176550)
XLA Ops:
  0.0 2.3 %edges.1 = (bf16[8,384,128]{2,1,0:T(8,128)(2,1)}, bf16[768,256]{1,0:T(8,128)(2,1)}) custom-call(s32[2]{0:T(128)} %index_ref.1, bf16[3,3,128,256]{3,2,1,0:T(8,128)(2,1)} %fields_ref.1, bf16[64,256]{1,0:T(8,128)(2,1)} %constant.35.clone.pick_ref), custom_call_target="tpu_custom_call" | custom-call | tf_op jit(solution)/shard_map/edges/pallas_call | solution.py:243
  2.3 8.3 %all-to-all-start = ((bf16[8,384,128]{2,1,0:T(8,128)(2,1)}), bf16[8,384,128]{2,1,0:T(8,128)(2,1)S(1)}, u32[]{:S(2)}, u32[]{:S(2)}) async-start(bf16[8,384,128]{2,1,0:T(8,128)(2,1)} %get-tuple-element.8), calls=%async_computation | async-start | bytes 1572864 | tf_op jit(solution)/shard_map/all_to_all | solution.py:254
  10.6 1.0 %collective-permute-start = (s32[3,68]{1,0:T(4,128)}, s32[3,68]{1,0:T(4,128)S(1)}, u32[]{:S(2)}, u32[]{:S(2)}) collective-permute-start(s32[3,68]{1,0:T(4,128)} %halo_own_ref.1), channel_id=1, source_target_pairs={{0,8},{8,0},{16,24},{24,16},{32,40},{40,32},{48,56},{56,48},{64,72... | collective-permute-start | bytes 2456 | tf_op jit(solution)/shard_map/ppermute | solution.py:252
  11.5 0.1 collective-permute-start.1
  11.6 12.0 %all-to-all-done.table_own_ref = bf16[8,384,128]{2,1,0:T(8,128)(2,1)S(1)} async-done(((bf16[8,384,128]{2,1,0:T(8,128)(2,1)}), bf16[8,384,128]{2,1,0:T(8,128)(2,1)S(1)}, u32[]{:S(2)}, u32[]{:S(2)}) %all-to-all-start) | async-done | bytes 786464 | tf_op jit(solution)/shard_map/all_to_all | solution.py:254
  23.7 1.2 %collective-permute-start.2 = (bf16[8,384,128]{2,1,0:T(8,128)(2,1)S(1)}, bf16[8,384,128]{2,1,0:T(8,128)(2,1)S(1)}, u32[]{:S(2)}, u32[]{:S(2)}) collective-permute-start(bf16[8,384,128]{2,1,0:T(8,128)(2,1)S(1)} %all-to-all-done.table_own_ref), channel_id=1, source_target_pairs={{0,8},{8,0},{16,24},{24,16},{32,40},{40,32},{48,56},{56,48},{64,72... | collective-permute-start | bytes 2359304 | tf_op jit(solution)/shard_map/ppermute | solution.py:255
  24.9 1.2 %convert_bitcast_fusion = (f32[1,128]{1,0:T(1,128)}, f32[128]{0:T(128)S(1)}) fusion(s32[128]{0:T(128)} %mask_ref.1), kind=kLoop, calls=%fused_computation.9 | loop fusion | flops 128 | bytes 1536 | tf_op jit(solution)/shard_map/broadcast_in_dim | solution.py:309
  26.1 0.1 fusion.2
  26.2 0.7 broadcast_select_fusion
  26.9 0.1 pad_maximum_fusion.1
  27.0 0.6 pad_maximum_fusion.kept_lane_ref
  27.6 0.0 collective-permute-done.halo_other_ref
  27.6 0.7 negate_select_fusion
  28.3 0.6 pad.4.position_ref
  28.9 0.0 collective-permute-done.1.other_ref
  28.9 0.0 collective-permute-done.2.table_other_ref
  28.9 0.9 %broadcast_in_dim.48.kept_row_ref = f32[128,128]{1,0:T(8,128)} broadcast(f32[128]{0:T(128)S(1)} %get-tuple-element.12), dimensions={0} | broadcast | bytes 66048 | tf_op jit(solution)/shard_map/broadcast_in_dim | solution.py:260
  29.8 0.0 copy-done
  29.8 0.2 copy-done.1
  30.0 16.1 %moments.1 = f32[64,88,128]{2,1,0:T(8,128)} custom-call(s32[1]{0:T(128)} %bitcast.core_ref, s32[3,68]{1,0:T(4,128)} %halo_own_ref.1, s32[3,68]{1,0:T(4,128)} %copy-done.5, bf16[768,256]{1,0:T(8,128)(2,1)} %get-tuple-element.7.own_ref, bf16[768,256]{1,0:T(8,128)(2,1)} %copy-done.2, bf16[8,384,128]{2,1,0:T(8,128)(2,1)} %copy-done, ...), custom_call_target="tpu_custom_call" | custom-call | tf_op jit(solution)/shard_map/moments/pallas_call | solution.py:265
  46.1 3.1 %convert_element_type.10 = f16[64,88,128]{2,1,0:T(8,128)(2,1)} convert(f32[64,88,128]{2,1,0:T(8,128)} %moments.1) | non-fusion elementwise | flops 720896 | bytes 4325376 | tf_op jit(solution)/shard_map/convert_element_type | solution.py:294
  49.2 7.2 %all-to-all-start.1 = ((f16[64,88,128]{2,1,0:T(8,128)(2,1)}), f16[64,88,128]{2,1,0:T(8,128)(2,1)S(1)}, u32[]{:S(2)}, u32[]{:S(2)}) async-start(f16[64,88,128]{2,1,0:T(8,128)(2,1)} %convert_element_type.10), calls=%async_computation.1 | async-start | bytes 2883584 | tf_op jit(solution)/shard_map/all_to_all | solution.py:294
  56.4 22.6 %all-to-all-done.1 = f16[64,88,128]{2,1,0:T(8,128)(2,1)S(1)} async-done(((f16[64,88,128]{2,1,0:T(8,128)(2,1)}), f16[64,88,128]{2,1,0:T(8,128)(2,1)S(1)}, u32[]{:S(2)}, u32[]{:S(2)}) %all-to-all-start.1) | async-done | bytes 1441824 | tf_op jit(solution)/shard_map/all_to_all | solution.py:294
  79.0 0.2 convert_element_type.11
  79.2 0.1 fusion.1
  79.3 0.8 multiply_reduce_fusion.near_ref
  80.0 1.5 %collective-permute-start.3 = (f32[88,128]{1,0:T(8,128)S(1)}, f32[88,128]{1,0:T(8,128)S(1)}, u32[]{:S(2)}, u32[]{:S(2)}) collective-permute-start(f32[88,128]{1,0:T(8,128)S(1)} %multiply_reduce_fusion.near_ref), channel_id=1, source_target_pairs={{0,8},{8,0},{16,24},{24,16},{32,40},{40,32},{48,56},{56,48},{64,72... | collective-permute-start | bytes 135176 | tf_op jit(solution)/shard_map/ppermute | solution.py:298
  81.5 0.6 pad_add_fusion.place_ref
  82.1 0.3 collective-permute-done.3.far_ref
  82.4 0.0 copy-done.3
  82.4 0.6 copy-done.4
  83.0 2.2 %rows.1 = f32[9,1408]{1,0:T(8,128)} custom-call(s32[3]{0:T(128)} %pad_add_fusion.place_ref, s32[128]{0:T(128)} %mask_ref.1, f32[88,128]{1,0:T(8,128)} %copy-done.3, f32[88,128]{1,0:T(8,128)} %copy-done.4, bf16[1152,256]{1,0:T(8,128)(2,1)} %weight_ref.1, f32[1,128]{1,0:T(1,128)} %get-tuple-element.11.kept_ref), custom_call_target="tpu_custom_call" | custom-call | tf_op jit(solution)/shard_map/rows/pallas_call | solution.py:302
  (10 shorter events, 0.0 us)
Async XLA Ops:
  2.3 21.4 %all-to-all-start = ((bf16[8,384,128]{2,1,0:T(8,128)(2,1)}), bf16[8,384,128]{2,1,0:T(8,128)(2,1)S(1)}, u32[]{:S(2)}, u32[]{:S(2)}) async-start(bf16[8,384,128]{2,1,0:T(8,128)(2,1)} %get-tuple-element.8), calls=%async_computation | async-start | bytes 1572864 | tf_op jit(solution)/shard_map/all_to_all | solution.py:254
  10.6 17.0 %collective-permute-start = (s32[3,68]{1,0:T(4,128)}, s32[3,68]{1,0:T(4,128)S(1)}, u32[]{:S(2)}, u32[]{:S(2)}) collective-permute-start(s32[3,68]{1,0:T(4,128)} %halo_own_ref.1), channel_id=1, source_target_pairs={{0,8},{8,0},{16,24},{24,16},{32,40},{40,32},{48,56},{56,48},{64,72... | collective-permute-start | bytes 2456 | tf_op jit(solution)/shard_map/ppermute | solution.py:252
  11.5 17.4 %collective-permute-start.1 = (bf16[768,256]{1,0:T(8,128)(2,1)}, bf16[768,256]{1,0:T(8,128)(2,1)S(1)}, u32[]{:S(2)}, u32[]{:S(2)}) collective-permute-start(bf16[768,256]{1,0:T(8,128)(2,1)} %get-tuple-element.7.own_ref), channel_id=1, source_target_pairs={{0,8},{8,0},{16,24},{24,16},{32,40},{40,32},{48,56},{56,48},{64,72... | collective-permute-start | bytes 1179656 | tf_op jit(solution)/shard_map/ppermute | solution.py:251
  23.7 6.1 %copy-start = (bf16[8,384,128]{2,1,0:T(8,128)(2,1)}, bf16[8,384,128]{2,1,0:T(8,128)(2,1)S(1)}, u32[]{:S(2)}) copy-start(bf16[8,384,128]{2,1,0:T(8,128)(2,1)S(1)} %all-to-all-done.table_own_ref) | copy-start | bytes 2359300
  23.7 5.2 %collective-permute-start.2 = (bf16[8,384,128]{2,1,0:T(8,128)(2,1)S(1)}, bf16[8,384,128]{2,1,0:T(8,128)(2,1)S(1)}, u32[]{:S(2)}, u32[]{:S(2)}) collective-permute-start(bf16[8,384,128]{2,1,0:T(8,128)(2,1)S(1)} %all-to-all-done.table_own_ref), channel_id=1, source_target_pairs={{0,8},{8,0},{16,24},{24,16},{32,40},{40,32},{48,56},{56,48},{64,72... | collective-permute-start | bytes 2359304 | tf_op jit(solution)/shard_map/ppermute | solution.py:255
  27.6 2.2 %copy-start.5 = (s32[3,68]{1,0:T(4,128)}, s32[3,68]{1,0:T(4,128)S(1)}, u32[]{:S(2)}) copy-start(s32[3,68]{1,0:T(4,128)S(1)} %collective-permute-done.halo_other_ref) | copy-start | bytes 2452
  28.9 0.9 %copy-start.2 = (bf16[768,256]{1,0:T(8,128)(2,1)}, bf16[768,256]{1,0:T(8,128)(2,1)S(1)}, u32[]{:S(2)}) copy-start(bf16[768,256]{1,0:T(8,128)(2,1)S(1)} %collective-permute-done.1.other_ref) | copy-start | bytes 1179652
  28.9 1.1 %copy-start.1 = (bf16[8,384,128]{2,1,0:T(8,128)(2,1)}, bf16[8,384,128]{2,1,0:T(8,128)(2,1)S(1)}, u32[]{:S(2)}) copy-start(bf16[8,384,128]{2,1,0:T(8,128)(2,1)S(1)} %collective-permute-done.2.table_other_ref) | copy-start | bytes 2359300
  49.2 29.8 %all-to-all-start.1 = ((f16[64,88,128]{2,1,0:T(8,128)(2,1)}), f16[64,88,128]{2,1,0:T(8,128)(2,1)S(1)}, u32[]{:S(2)}, u32[]{:S(2)}) async-start(f16[64,88,128]{2,1,0:T(8,128)(2,1)} %convert_element_type.10), calls=%async_computation.1 | async-start | bytes 2883584 | tf_op jit(solution)/shard_map/all_to_all | solution.py:294
  80.0 2.4 %copy-start.3 = (f32[88,128]{1,0:T(8,128)}, f32[88,128]{1,0:T(8,128)S(1)}, u32[]{:S(2)}) copy-start(f32[88,128]{1,0:T(8,128)S(1)} %multiply_reduce_fusion.near_ref) | copy-start | bytes 135172
  80.0 2.4 %collective-permute-start.3 = (f32[88,128]{1,0:T(8,128)S(1)}, f32[88,128]{1,0:T(8,128)S(1)}, u32[]{:S(2)}, u32[]{:S(2)}) collective-permute-start(f32[88,128]{1,0:T(8,128)S(1)} %multiply_reduce_fusion.near_ref), channel_id=1, source_target_pairs={{0,8},{8,0},{16,24},{24,16},{32,40},{40,32},{48,56},{56,48},{64,72... | collective-permute-start | bytes 135176 | tf_op jit(solution)/shard_map/ppermute | solution.py:298
  82.4 0.6 copy-start.4

commit v2 on v1

--- a/solution.py
+++ b/solution.py
@@ -16,6 +16,7 @@
 K = TAPS * CH
 HALF = K // 2
 CYCLE = 4 * SIDE + 4
+RIM = 64
 ROWS = 88
 AXES = ("face", "sample")
 NT = (((1,), (1,)), ((), ()))
@@ -34,7 +35,7 @@
 
 
 def tap_matrices():
-    out = np.zeros((TAPS, PIX + CH, PIX), np.float32)
+    whole = np.zeros((TAPS, PIX + CH, PIX), np.float32)
     for t in range(TAPS):
         for y in range(SIDE):
             for x in range(SIDE):
@@ -49,17 +50,14 @@
                     k = PIX + 3 * SIDE + 4 + u - 1
                 else:
                     k = (u - 1) * SIDE + v - 1
-                out[t, k, y * SIDE + x] = 1
-    return out.astype(ml_dtypes.bfloat16)
-
-
-def source_base():
-    out = np.full((1, CH), -1000, np.int32)
-    for e, at in enumerate(SIDE_AT):
-        out[0, at : at + SIDE] = e * SIDE
-    for e, at in enumerate(CORNER_AT):
-        out[0, at] = (4 + e) * SIDE
-    return out
+                whole[t, k, y * SIDE + x] = 1
+    rim = [p for p in range(PIX) if p // SIDE in (0, SIDE - 1) or p % SIDE in (0, SIDE - 1)]
+    inner = whole[:, :PIX].copy()
+    inner[:, :, rim] = 0
+    outer = np.zeros((PIX + CH, 640), np.float32)
+    for t in range(TAPS):
+        outer[:, t * RIM : t * RIM + len(rim)] = whole[t][:, rim]
+    return inner.astype(ml_dtypes.bfloat16), outer.astype(ml_dtypes.bfloat16)
 
 
 def edges_kernel(index_ref, fields_ref, pick_ref, copies_ref, own_ref):
@@ -75,7 +73,25 @@
                 copies_ref[d, u * 4 * SIDE : (u + 1) * 4 * SIDE, :] = edges
 
 
-def moments_kernel(
+def inner_kernel(core_ref, own_ref, other_ref, taps_ref, gram_ref, patches):
+    half = own_ref.shape[0] // CH
+    for t in range(TAPS):
+        for n, ref in enumerate((own_ref, other_ref)):
+            values = jnp.dot(ref[...], taps_ref[t], preferred_element_type=jnp.float32)
+            values = values.astype(jnp.bfloat16)
+            for m in range(half):
+                u = n * half + m
+                patches[t * CH : (t + 1) * CH, u * PIX : (u + 1) * PIX] = values[m * CH : (m + 1) * CH, :]
+    right = patches[pl.ds(pl.multiple_of(core_ref[0] * HALF, HALF), HALF), :]
+    for t in range(0, TAPS, 3):
+        rows = slice(t * CH, (t + 3) * CH)
+        block = lax.dot_general(patches[rows, :], right, NT, preferred_element_type=jnp.float32)
+        for l in range(4):
+            gram_ref[l, rows, :] = block[:, l * CH : (l + 1) * CH]
+        gram_ref[4, rows, : CH // 2] = block[:, 4 * CH :]
+
+
+def outer_kernel(
     subs,
     core_ref,
     halo_own_ref,
@@ -84,16 +100,17 @@
     other_ref,
     table_own_ref,
     table_other_ref,
-    position_ref,
-    base_ref,
+    halo_rows_own_ref,
+    halo_rows_other_ref,
     taps_ref,
-    kept_row_ref,
-    kept_lane_ref,
+    mask_ref,
+    inner_ref,
     message_ref,
     tiles,
     grid,
     patches,
     gram,
+    position,
 ):
     core = core_ref[0]
     units = 4 * subs
@@ -115,15 +132,27 @@
                     u = side * half + s * subs + f
                     tiles[u * CH + n * SIDE : u * CH + (n + 1) * SIDE, :] = jnp.where(near, mine, theirs)
 
+    lane = lax.broadcasted_iota(jnp.int32, (8, CH), 1)
+    base = jnp.full((8, CH), -1000, jnp.int32)
+    for e, at in enumerate(SIDE_AT):
+        base = jnp.where((lane >= at) & (lane < at + SIDE), e * SIDE, base)
+    for e, at in enumerate(CORNER_AT):
+        base = jnp.where(lane == at, (4 + e) * SIDE, base)
+    position[...] = jnp.zeros((8, CH), jnp.int32)
+    position[0:subs, 0:CYCLE] = lax.rem(halo_rows_own_ref[...], SIDE)
+    position[subs : 2 * subs, 0:CYCLE] = lax.rem(halo_rows_other_ref[...], SIDE)
+    source = position[...] + base
+
     row_at = lax.broadcasted_iota(jnp.int32, (CH, CH), 0)
     col_at = lax.broadcasted_iota(jnp.int32, (CH, CH), 1)
-    eye = jnp.where(row_at == col_at, 1.0, 0.0).astype(jnp.bfloat16)
+    diagonal = row_at == col_at
+    eye = jnp.where(diagonal, 1.0, 0.0).astype(jnp.bfloat16)
     turned = lax.dot_general(eye, tiles[...], NT, preferred_element_type=jnp.float32).astype(jnp.bfloat16)
     largest = jnp.zeros((CH, CH), jnp.float32)
     for u in range(units):
         side, f = u // half, u % half % subs
-        source = position_ref[side * subs + f : side * subs + f + 1, :] + base_ref[...]
-        pick = jnp.where(row_at == source, 1.0, 0.0).astype(jnp.bfloat16)
+        at = side * subs + f
+        pick = jnp.where(row_at == source[at : at + 1, :], 1.0, 0.0).astype(jnp.bfloat16)
         cycle = jnp.dot(turned[:, u * CH : (u + 1) * CH], pick, preferred_element_type=jnp.float32)
         x = (own_ref if side == 0 else other_ref)[(u % half) * CH : (u % half + 1) * CH, :]
         grid[u * CH : (u + 1) * CH, :PIX] = x
@@ -132,7 +161,13 @@
         largest = jnp.maximum(largest, jnp.maximum(size[:, :CH], size[:, CH:]))
         largest = jnp.maximum(largest, jnp.abs(cycle))
 
-    kept_row = kept_row_ref[...]
+    kept = mask_ref[...].astype(jnp.float32)
+    kept_row = jnp.sum(jnp.where(diagonal, kept, 0.0), axis=1, keepdims=True)
+    turned_kept = pltpu.roll(jnp.broadcast_to(kept, (8, CH)), CH // 2, 1)
+    kept = jnp.broadcast_to(kept, (8, CH))
+    first, second = jnp.where(core == 0, kept, turned_kept), jnp.where(core == 0, turned_kept, kept)
+    folded = jnp.where(lane < CH // 2, first, second)
+    kept_lane = jnp.where(lax.broadcasted_iota(jnp.int32, (8, CH), 0) == 0, first, folded)
 
     def exponent(values):
         top = jnp.maximum(jnp.max(values), 2.0**-60)
@@ -141,20 +176,18 @@
     kept_exp = exponent(jnp.where(kept_row > 0, largest, 0.0))
     any_exp = exponent(largest)
     row_scale = jnp.where(kept_row > 0, jnp.exp2(-kept_exp[0:1, :]), 0.0)
-    lane_exps = jnp.where(kept_lane_ref[...] > 0, kept_exp, any_exp)
+    lane_exps = jnp.where(kept_lane > 0, kept_exp, any_exp)
     lane_scale = jnp.exp2(-lane_exps)
 
     chunk = units * CH // 3
-    for t in range(TAPS):
-        for m in range(0, units * CH, chunk):
-            if t == TAPS // 2:
-                values = grid[m : m + chunk, :PIX]
-            else:
-                values = jnp.dot(grid[m : m + chunk, :], taps_ref[t], preferred_element_type=jnp.float32)
-                values = values.astype(jnp.bfloat16)
-            for n in range(chunk // CH):
-                u = m // CH + n
-                patches[t * CH : (t + 1) * CH, u * PIX : (u + 1) * PIX] = values[n * CH : (n + 1) * CH, :]
+    for m in range(0, units * CH, chunk):
+        values = jnp.dot(grid[m : m + chunk, :], taps_ref[...], preferred_element_type=jnp.float32)
+        values = values.astype(jnp.bfloat16)
+        for n in range(chunk // CH):
+            u = m // CH + n
+            for t in range(TAPS):
+                part = values[n * CH : (n + 1) * CH, t * RIM : (t + 1) * RIM]
+                patches[t * CH : (t + 1) * CH, u * RIM : (u + 1) * RIM] = part
 
     right = patches[pl.ds(pl.multiple_of(core * HALF, HALF), HALF), :]
     for t in range(0, TAPS, 3):
@@ -163,11 +196,12 @@
         )
         for n in range(3):
             rows = block[n * CH : (n + 1) * CH, :]
+            at = slice((t + n) * CH, (t + n + 1) * CH)
             for l in range(4):
-                part = rows[:, l * CH : (l + 1) * CH] * row_scale * lane_scale[0:1, :]
-                gram[l, (t + n) * CH : (t + n + 1) * CH, :] = part
-            part = rows[:, 4 * CH :] * row_scale[:, : CH // 2] * lane_scale[1:2, : CH // 2]
-            gram[4, (t + n) * CH : (t + n + 1) * CH, : CH // 2] = part
+                part = rows[:, l * CH : (l + 1) * CH] + inner_ref[l, at, :]
+                gram[l, at, :] = part * row_scale * lane_scale[0:1, :]
+            part = rows[:, 4 * CH :] + inner_ref[4, at, : CH // 2]
+            gram[4, at, : CH // 2] = part * row_scale[:, : CH // 2] * lane_scale[1:2, : CH // 2]
 
     for g in range(8):
         for s in range(8):
@@ -181,7 +215,7 @@
             message_ref[j, 81:88, :] = (lane_exps + kept_exp)[0:7, :]
 
 
-def rows_kernel(place_ref, mask_ref, near_ref, far_ref, weight_ref, kept_ref, out_ref, rows):
+def rows_kernel(place_ref, mask_ref, near_ref, far_ref, weight_ref, kept_ref, out_ref, rows, split):
     core, owner = place_ref[0], place_ref[1]
     near, far = near_ref[...], far_ref[...]
     low = jnp.where(core == 0, near, far)
@@ -193,34 +227,37 @@
     def middle(values):
         return jnp.where(core == 0, values[72:81, : CH // 2], values[72:81, CH // 2 :])
 
+    rows[...] = jnp.zeros_like(rows)
     for l in range(4):
         rows[0:9, l * CH : (l + 1) * CH] = mine(low, l)
         rows[0:9, HALF + l * CH : HALF + (l + 1) * CH] = mine(high, l)
     rows[0:9, 4 * CH : HALF] = middle(low)
     rows[0:9, HALF + 4 * CH :] = middle(high)
 
-    at = lax.broadcasted_iota(jnp.int32, (9, CH), 0)
-    keep = jnp.zeros((9, CH), jnp.float32)
+    at = lax.broadcasted_iota(jnp.int32, (16, CH), 0)
+    keep = jnp.zeros((16, CH), jnp.float32)
     for k in range(9):
         bit = mask_ref[lax.rem(owner * 9 + k, CH)]
         keep = jnp.where(at == k, bit.astype(jnp.float32), keep)
-    whole = rows[0:9, :]
+    whole = rows[...]
     head = whole.astype(jnp.bfloat16)
     left = whole - head.astype(jnp.float32)
     tail = left.astype(jnp.bfloat16)
-    rest = (left - tail.astype(jnp.float32)).astype(jnp.bfloat16)
-    weight = weight_ref[...]
-    product = jnp.dot(rest, weight, preferred_element_type=jnp.float32)
-    product += jnp.dot(tail, weight, preferred_element_type=jnp.float32)
-    product += jnp.dot(head, weight, preferred_element_type=jnp.float32)
+    split[0:16, :] = head
+    split[16:32, :] = tail
+    split[32:48, :] = (left - tail.astype(jnp.float32)).astype(jnp.bfloat16)
+    product = jnp.dot(split[...], weight_ref[...], preferred_element_type=jnp.float32)
+    product = product[32:48, :] + product[16:32, :] + product[0:16, :]
     count = place_ref[2].astype(jnp.float32)
-    kept = kept_ref[...]
+    kept = kept_ref[...] > 0
     for t in range(TAPS):
         part = whole[:, t * CH : (t + 1) * CH]
-        out_ref[:, t * CH : (t + 1) * CH] = jnp.where((keep > 0) & (kept > 0), part / count, 0.0)
+        part = jnp.where((keep > 0) & kept, part / count, 0.0)
+        out_ref[:, t * CH : (t + 1) * CH] = part[0:9, :]
     for n in range(2):
         part = product[:, n * CH : (n + 1) * CH]
-        out_ref[:, K + n * CH : K + (n + 1) * CH] = jnp.where(keep > 0, part / count, 0.0)
+        part = jnp.where(keep > 0, part / count, 0.0)
+        out_ref[:, K + n * CH : K + (n + 1) * CH] = part[0:9, :]
 
 
 VMEM = pl.BlockSpec(memory_space=pltpu.VMEM)
@@ -254,40 +291,49 @@
     table = lax.all_to_all(copies, "face", 0, 0, axis_index_groups=same_core)
     table_other = lax.ppermute(table, "face", swap)
 
-    both = jnp.concatenate([halo_index, halo_other], axis=0)
-    position = jnp.pad(lax.rem(both, SIDE), ((0, 0), (0, CH - CYCLE)))
-    keep = channel_mask.astype(f32)
-    kept_row = jnp.broadcast_to(keep[:, None], (CH, CH))
-    rolled = jnp.where(core == 0, keep, jnp.roll(keep, CH // 2))
-    folded = jnp.concatenate([rolled[: CH // 2], rolled[: CH // 2]])
-    kept_lane = jnp.concatenate([rolled[None], jnp.broadcast_to(folded[None], (7, CH))], axis=0)
+    mask_row = channel_mask[None]
+    place = jnp.stack([core, face * samples + sample, jnp.int32(2 * subs * PIX * faces * samples)])
+    inner_taps, outer_taps = tap_matrices()
+    limit = pltpu.CompilerParams(vmem_limit_bytes=56 * 2**20)
+
+    inner = pl.pallas_call(
+        inner_kernel,
+        out_shape=shape((5, K, CH), f32),
+        in_specs=[SMEM] + [VMEM] * 3,
+        out_specs=VMEM,
+        scratch_shapes=[pltpu.VMEM((K, units * PIX), bf16)],
+        compiler_params=limit,
+        cost_estimate=pl.CostEstimate(flops=6 * 10**9, bytes_accessed=5 * 10**6, transcendentals=0),
+        name="inner",
+    )(place, own, other, jnp.asarray(inner_taps))
 
     message = pl.pallas_call(
-        functools.partial(moments_kernel, subs),
+        functools.partial(outer_kernel, subs),
         out_shape=shape((64, ROWS, CH), f32),
         in_specs=[SMEM] * 3 + [VMEM] * 9,
         out_specs=VMEM,
         scratch_shapes=[
             pltpu.VMEM((units * CH, CH), bf16),
             pltpu.VMEM((units * CH, PIX + CH), bf16),
-            pltpu.VMEM((K, units * PIX), bf16),
+            pltpu.VMEM((K, units * RIM), bf16),
             pltpu.VMEM((5, K, CH), f32),
+            pltpu.VMEM((8, CH), jnp.int32),
         ],
-        compiler_params=pltpu.CompilerParams(vmem_limit_bytes=56 * 2**20),
-        name="moments",
+        compiler_params=limit,
+        name="outer",
     )(
-        core[None],
+        place,
         halo_index,
         halo_other,
         own,
         other,
         table,
         table_other,
-        position,
-        jnp.asarray(source_base()),
-        jnp.asarray(tap_matrices()),
-        kept_row,
-        kept_lane,
+        halo_index,
+        halo_other,
+        jnp.asarray(outer_taps),
+        mask_row,
+        inner,
     )
 
     groups = [[f * samples + s for f in range(c, faces, 2) for s in range(samples)] for c in range(2)]
@@ -297,16 +343,14 @@
     near = jnp.sum(landed * jnp.exp2(exps), axis=0)
     far = lax.ppermute(near, "face", swap)
 
-    pixels = 2 * subs * PIX * faces * samples
-    place = jnp.stack([core, face * samples + sample, jnp.int32(pixels)])
     return pl.pallas_call(
         rows_kernel,
         out_shape=shape((TAPS, K + weight.shape[1]), f32),
         in_specs=[SMEM] * 2 + [VMEM] * 4,
         out_specs=VMEM,
-        scratch_shapes=[pltpu.VMEM((16, K), f32)],
+        scratch_shapes=[pltpu.VMEM((16, K), f32), pltpu.VMEM((48, K), bf16)],
         name="rows",
-    )(place, channel_mask, near, far, weight, keep[None])
+    )(place, channel_mask, near, far, weight, mask_row)
 
 
 def solution(mesh):

time: 85.6 us -> 87.8 us (1.026)
  Pallas kernels: 20.6 us -> 25.6 us
  other arithmetic: 7.98 us -> 4.67 us
    pallas_call x1 -> x2, Pallas kernels: 16.1 us -> 21.3 us  [the longest x1 12 us: per_device(): pl.pallas_call(inner_kernel, out_shape=shape((5, K, CH), f32), in_specs=[...]
    unnamed x12, local copies, waits for them, and re-layouts: 0.81 us -> 2.26 us
    broadcast_in_dim x1 -> x0, other arithmetic: 1.22 us -> none  [per_device(): keep[None]]
    ppermute x1, starting transfers between devices: 0.96 us -> 0.01 us  [per_device(): halo_other = lax.ppermute(halo_index, 'face', swap)]
  transfers between devices with their start and end apart: 6 -> 6, of which waited for: 3 -> 3; matrix products, arithmetic and copies ran while one was open for 5% -> 1% of each run, Pallas kernels for 0% -> 14%
where the time goes in v2:
time: 87.8 us; the launch traced here: 87.4 us
  waiting for transfers between devices  35 us (40%)
  Pallas kernels  25.6 us (29%)
  starting transfers between devices  19.8 us (23%)
  other arithmetic  4.67 us (5%)
  local copies, waits for them, and re-layouts  2.32 us (3%)
    all_to_all x1, waiting for transfers between devices, per_device(): lax.all_to_all(message.astype(jnp.float16), AXES, 0, 0, axis_index_groups...  22 us
    all_to_all x1, waiting for transfers between devices, per_device(): table = lax.all_to_all(copies, 'face', 0, 0, axis_index_groups=same_core)  12.1 us
    pallas_call x1, Pallas kernels, per_device(): pl.pallas_call(inner_kernel, out_shape=shape((5, K, CH), f32), in_specs=[...  12 us
    pallas_call x1, Pallas kernels, per_device(): pl.pallas_call(functools.partial(outer_kernel, subs), out_shape=shape((64...  9.26 us
    all_to_all x1, starting transfers between devices, per_device(): table = lax.all_to_all(copies, 'face', 0, 0, axis_index_groups=same_core)  8.33 us
    all_to_all x1, starting transfers between devices, per_device(): lax.all_to_all(message.astype(jnp.float16), AXES, 0, 0, axis_index_groups...  7.18 us
    convert_element_type x1, other arithmetic, per_device(): message.astype(jnp.float16)  3.12 us
    unnamed x12, local copies, waits for them, and re-layouts  2.26 us
  transfers between devices with their start and end apart: 6, of which 3 were waited for; matrix products, arithmetic and copies ran while one was open for 1% of the time, Pallas kernels for 14%

profile of v2, /device:TPU:1, one launch (start us, length us, event | category | flops | bytes accessed | tf_op | source)
XLA Modules:
  0.0 87.4 jit_solution(17985258161885113799)
XLA Ops:
  0.0 2.2 %edges.1 = (bf16[8,384,128]{2,1,0:T(8,128)(2,1)}, bf16[768,256]{1,0:T(8,128)(2,1)}) custom-call(s32[2]{0:T(128)} %index_ref.1, bf16[3,3,128,256]{3,2,1,0:T(8,128)(2,1)} %fields_ref.1, bf16[64,256]{1,0:T(8,128)(2,1)} %constant.30.clone.pick_ref), custom_call_target="tpu_custom_call" | custom-call | tf_op jit(solution)/shard_map/edges/pallas_call | solution.py:280
  2.3 8.3 %all-to-all-start = ((bf16[8,384,128]{2,1,0:T(8,128)(2,1)}), bf16[8,384,128]{2,1,0:T(8,128)(2,1)S(1)}, u32[]{:S(2)}, u32[]{:S(2)}) async-start(bf16[8,384,128]{2,1,0:T(8,128)(2,1)} %get-tuple-element.8), calls=%async_computation | async-start | bytes 1572864 | tf_op jit(solution)/shard_map/all_to_all | solution.py:291
  10.6 1.0 %collective-permute-start.1 = (bf16[768,256]{1,0:T(8,128)(2,1)}, bf16[768,256]{1,0:T(8,128)(2,1)S(1)}, u32[]{:S(2)}, u32[]{:S(2)}) collective-permute-start(bf16[768,256]{1,0:T(8,128)(2,1)} %get-tuple-element.7.own_ref), channel_id=1, source_target_pairs={{0,8},{8,0},{16,24},{24,16},{32,40},{40,32},{48,56},{56,48},{64,72... | collective-permute-start | bytes 1179656 | tf_op jit(solution)/shard_map/ppermute | solution.py:288
  11.5 12.1 %all-to-all-done.table_own_ref = bf16[8,384,128]{2,1,0:T(8,128)(2,1)S(1)} async-done(((bf16[8,384,128]{2,1,0:T(8,128)(2,1)}), bf16[8,384,128]{2,1,0:T(8,128)(2,1)S(1)}, u32[]{:S(2)}, u32[]{:S(2)}) %all-to-all-start) | async-done | bytes 786464 | tf_op jit(solution)/shard_map/all_to_all | solution.py:291
  23.6 0.0 copy-start
  23.7 1.2 %collective-permute-start.2 = (bf16[8,384,128]{2,1,0:T(8,128)(2,1)S(1)}, bf16[8,384,128]{2,1,0:T(8,128)(2,1)S(1)}, u32[]{:S(2)}, u32[]{:S(2)}) collective-permute-start(bf16[8,384,128]{2,1,0:T(8,128)(2,1)S(1)} %all-to-all-done.table_own_ref), channel_id=1, source_target_pairs={{0,8},{8,0},{16,24},{24,16},{32,40},{40,32},{48,56},{56,48},{64,72... | collective-permute-start | bytes 2359304 | tf_op jit(solution)/shard_map/ppermute | solution.py:292
  24.9 0.0 collective-permute-start
  24.9 0.6 pad_add_fusion.core_ref.place_ref
  25.5 0.0 collective-permute-done.1.other_ref
  25.5 0.0 copy-start.2
  25.5 0.8 copy-done.2
  26.3 12.0 %inner.1.inner_ref = f32[5,1152,128]{2,1,0:T(8,128)} custom-call(s32[3]{0:T(128)} %pad_add_fusion.core_ref.place_ref, bf16[768,256]{1,0:T(8,128)(2,1)} %get-tuple-element.7.own_ref, bf16[768,256]{1,0:T(8,128)(2,1)} %copy-done.2, bf16[9,256,256]{2,1,0:T(8,128)(2,1)} %constant.31.clone.taps_ref), custom_call_target="tpu_custom_call" | custom-call | flops 6000000000 | bytes 5000000 | tf_op jit(solution)/shard_map/inner/pallas_call | solution.py:299
  38.3 0.0 copy-done
  38.3 0.0 collective-permute-done.halo_other_ref.halo_rows_other_ref
  38.3 0.0 copy-start.5
  38.3 0.0 collective-permute-done.2.table_other_ref
  38.3 0.0 copy-start.1
  38.3 0.6 copy-done.5
  38.9 0.3 copy-done.1
  39.2 9.3 %outer.1 = f32[64,88,128]{2,1,0:T(8,128)} custom-call(s32[3]{0:T(128)} %pad_add_fusion.core_ref.place_ref, s32[3,68]{1,0:T(4,128)} %halo_rows_own_ref.1, s32[3,68]{1,0:T(4,128)} %copy-done.5, bf16[768,256]{1,0:T(8,128)(2,1)} %get-tuple-element.7.own_ref, bf16[768,256]{1,0:T(8,128)(2,1)} %copy-done.2, bf16[8,384,128]{2,1,0:T(8,128)(2,1)} %copy-done, ...), custom_call_target="tpu_custom_call" | custom-call | tf_op jit(solution)/shard_map/outer/pallas_call | solution.py:310
  48.4 3.1 %convert_element_type.6 = f16[64,88,128]{2,1,0:T(8,128)(2,1)} convert(f32[64,88,128]{2,1,0:T(8,128)} %outer.1) | non-fusion elementwise | flops 720896 | bytes 4325376 | tf_op jit(solution)/shard_map/convert_element_type | solution.py:340
  51.6 7.2 %all-to-all-start.1 = ((f16[64,88,128]{2,1,0:T(8,128)(2,1)}), f16[64,88,128]{2,1,0:T(8,128)(2,1)S(1)}, u32[]{:S(2)}, u32[]{:S(2)}) async-start(f16[64,88,128]{2,1,0:T(8,128)(2,1)} %convert_element_type.6), calls=%async_computation.1 | async-start | bytes 2883584 | tf_op jit(solution)/shard_map/all_to_all | solution.py:340
  58.8 22.0 %all-to-all-done.1 = f16[64,88,128]{2,1,0:T(8,128)(2,1)S(1)} async-done(((f16[64,88,128]{2,1,0:T(8,128)(2,1)}), f16[64,88,128]{2,1,0:T(8,128)(2,1)S(1)}, u32[]{:S(2)}, u32[]{:S(2)}) %all-to-all-start.1) | async-done | bytes 1441824 | tf_op jit(solution)/shard_map/all_to_all | solution.py:340
  80.8 0.2 convert_element_type.7
  80.9 0.1 fusion
  81.0 0.8 multiply_reduce_fusion.near_ref
  81.8 0.0 copy-start.3
  81.8 2.1 %collective-permute-start.3 = (f32[88,128]{1,0:T(8,128)S(1)}, f32[88,128]{1,0:T(8,128)S(1)}, u32[]{:S(2)}, u32[]{:S(2)}) collective-permute-start(f32[88,128]{1,0:T(8,128)S(1)} %multiply_reduce_fusion.near_ref), channel_id=1, source_target_pairs={{0,8},{8,0},{16,24},{24,16},{32,40},{40,32},{48,56},{56,48},{64,72... | collective-permute-start | bytes 135176 | tf_op jit(solution)/shard_map/ppermute | solution.py:344
  83.9 0.9 %collective-permute-done.3.far_ref = f32[88,128]{1,0:T(8,128)S(1)} collective-permute-done((f32[88,128]{1,0:T(8,128)S(1)}, f32[88,128]{1,0:T(8,128)S(1)}, u32[]{:S(2)}, u32[]{:S(2)}) %collective-permute-start.3) | collective-permute-done | bytes 45088 | tf_op jit(solution)/shard_map/ppermute | solution.py:344
  84.7 0.0 copy-done.3
  84.7 0.6 copy-done.4
  85.3 2.1 %rows.1 = f32[9,1408]{1,0:T(8,128)} custom-call(s32[3]{0:T(128)} %pad_add_fusion.core_ref.place_ref, s32[128]{0:T(128)} %mask_ref.1, f32[88,128]{1,0:T(8,128)} %copy-done.3, f32[88,128]{1,0:T(8,128)} %copy-done.4, bf16[1152,256]{1,0:T(8,128)(2,1)} %weight_ref.1, s32[1,128]{1,0:T(1,128)} %bitcast.8), custom_call_target="tpu_custom_call" | custom-call | tf_op jit(solution)/shard_map/rows/pallas_call | solution.py:346
  (2 shorter events, 0.0 us)
Async XLA Ops:
  2.3 21.4 %all-to-all-start = ((bf16[8,384,128]{2,1,0:T(8,128)(2,1)}), bf16[8,384,128]{2,1,0:T(8,128)(2,1)S(1)}, u32[]{:S(2)}, u32[]{:S(2)}) async-start(bf16[8,384,128]{2,1,0:T(8,128)(2,1)} %get-tuple-element.8), calls=%async_computation | async-start | bytes 1572864 | tf_op jit(solution)/shard_map/all_to_all | solution.py:291
  10.6 14.9 %collective-permute-start.1 = (bf16[768,256]{1,0:T(8,128)(2,1)}, bf16[768,256]{1,0:T(8,128)(2,1)S(1)}, u32[]{:S(2)}, u32[]{:S(2)}) collective-permute-start(bf16[768,256]{1,0:T(8,128)(2,1)} %get-tuple-element.7.own_ref), channel_id=1, source_target_pairs={{0,8},{8,0},{16,24},{24,16},{32,40},{40,32},{48,56},{56,48},{64,72... | collective-permute-start | bytes 1179656 | tf_op jit(solution)/shard_map/ppermute | solution.py:288
  23.6 14.6 %copy-start = (bf16[8,384,128]{2,1,0:T(8,128)(2,1)}, bf16[8,384,128]{2,1,0:T(8,128)(2,1)S(1)}, u32[]{:S(2)}) copy-start(bf16[8,384,128]{2,1,0:T(8,128)(2,1)S(1)} %all-to-all-done.table_own_ref) | copy-start | bytes 2359300
  23.7 14.6 %collective-permute-start.2 = (bf16[8,384,128]{2,1,0:T(8,128)(2,1)S(1)}, bf16[8,384,128]{2,1,0:T(8,128)(2,1)S(1)}, u32[]{:S(2)}, u32[]{:S(2)}) collective-permute-start(bf16[8,384,128]{2,1,0:T(8,128)(2,1)S(1)} %all-to-all-done.table_own_ref), channel_id=1, source_target_pairs={{0,8},{8,0},{16,24},{24,16},{32,40},{40,32},{48,56},{56,48},{64,72... | collective-permute-start | bytes 2359304 | tf_op jit(solution)/shard_map/ppermute | solution.py:292
  24.9 13.4 %collective-permute-start = (s32[3,68]{1,0:T(4,128)}, s32[3,68]{1,0:T(4,128)S(1)}, u32[]{:S(2)}, u32[]{:S(2)}) collective-permute-start(s32[3,68]{1,0:T(4,128)} %halo_rows_own_ref.1), channel_id=1, source_target_pairs={{0,8},{8,0},{16,24},{24,16},{32,40},{40,32},{48,56},{56,48},{64,72... | collective-permute-start | bytes 2456 | tf_op jit(solution)/shard_map/ppermute | solution.py:289
  25.5 0.8 copy-start.2
  38.3 0.6 copy-start.5
  38.3 0.9 %copy-start.1 = (bf16[8,384,128]{2,1,0:T(8,128)(2,1)}, bf16[8,384,128]{2,1,0:T(8,128)(2,1)S(1)}, u32[]{:S(2)}) copy-start(bf16[8,384,128]{2,1,0:T(8,128)(2,1)S(1)} %collective-permute-done.2.table_other_ref) | copy-start | bytes 2359300
  51.6 29.2 %all-to-all-start.1 = ((f16[64,88,128]{2,1,0:T(8,128)(2,1)}), f16[64,88,128]{2,1,0:T(8,128)(2,1)S(1)}, u32[]{:S(2)}, u32[]{:S(2)}) async-start(f16[64,88,128]{2,1,0:T(8,128)(2,1)} %convert_element_type.6), calls=%async_computation.1 | async-start | bytes 2883584 | tf_op jit(solution)/shard_map/all_to_all | solution.py:340
  81.8 3.0 %copy-start.3 = (f32[88,128]{1,0:T(8,128)}, f32[88,128]{1,0:T(8,128)S(1)}, u32[]{:S(2)}) copy-start(f32[88,128]{1,0:T(8,128)S(1)} %multiply_reduce_fusion.near_ref) | copy-start | bytes 135172
  81.8 2.9 %collective-permute-start.3 = (f32[88,128]{1,0:T(8,128)S(1)}, f32[88,128]{1,0:T(8,128)S(1)}, u32[]{:S(2)}, u32[]{:S(2)}) collective-permute-start(f32[88,128]{1,0:T(8,128)S(1)} %multiply_reduce_fusion.near_ref), channel_id=1, source_target_pairs={{0,8},{8,0},{16,24},{24,16},{32,40},{40,32},{48,56},{56,48},{64,72... | collective-permute-start | bytes 135176 | tf_op jit(solution)/shard_map/ppermute | solution.py:344
  84.7 0.6 copy-start.4

commit v3 on v2

--- a/solution.py
+++ b/solution.py
@@ -18,6 +18,8 @@
 CYCLE = 4 * SIDE + 4
 RIM = 64
 ROWS = 88
+STEPS = 16
+TOP = 32700.0
 AXES = ("face", "sample")
 NT = (((1,), (1,)), ((), ()))
 SIDE_AT = (1, 19, 36, 52)
@@ -60,28 +62,29 @@
     return inner.astype(ml_dtypes.bfloat16), outer.astype(ml_dtypes.bfloat16)
 
 
-def edges_kernel(index_ref, fields_ref, pick_ref, copies_ref, own_ref):
+def edges_kernel(index_ref, fields_ref, pick_ref, copies_ref):
     subs = fields_ref.shape[1]
     for s in range(2):
         for f in range(subs):
             x = fields_ref[index_ref[s], f]
             u = s * subs + f
-            own_ref[u * CH : (u + 1) * CH, :] = x
             edges = lax.dot_general(pick_ref[...], x, NT, preferred_element_type=jnp.float32)
             edges = edges.astype(jnp.bfloat16)
             for d in range(copies_ref.shape[0]):
                 copies_ref[d, u * 4 * SIDE : (u + 1) * 4 * SIDE, :] = edges
 
 
-def inner_kernel(core_ref, own_ref, other_ref, taps_ref, gram_ref, patches):
-    half = own_ref.shape[0] // CH
+def inner_kernel(core_ref, index_ref, own_ref, other_ref, taps_ref, gram_ref, patches):
+    subs = own_ref.shape[1]
     for t in range(TAPS):
         for n, ref in enumerate((own_ref, other_ref)):
-            values = jnp.dot(ref[...], taps_ref[t], preferred_element_type=jnp.float32)
-            values = values.astype(jnp.bfloat16)
-            for m in range(half):
-                u = n * half + m
-                patches[t * CH : (t + 1) * CH, u * PIX : (u + 1) * PIX] = values[m * CH : (m + 1) * CH, :]
+            for s in range(2):
+                x = ref[index_ref[s]].reshape(subs * CH, PIX)
+                values = jnp.dot(x, taps_ref[t], preferred_element_type=jnp.float32)
+                values = values.astype(jnp.bfloat16)
+                for f in range(subs):
+                    u = (n * 2 + s) * subs + f
+                    patches[t * CH : (t + 1) * CH, u * PIX : (u + 1) * PIX] = values[f * CH : (f + 1) * CH, :]
     right = patches[pl.ds(pl.multiple_of(core_ref[0] * HALF, HALF), HALF), :]
     for t in range(0, TAPS, 3):
         rows = slice(t * CH, (t + 3) * CH)
@@ -94,6 +97,7 @@
 def outer_kernel(
     subs,
     core_ref,
+    index_ref,
     halo_own_ref,
     halo_other_ref,
     own_ref,
@@ -111,6 +115,7 @@
     patches,
     gram,
     position,
+    stage,
 ):
     core = core_ref[0]
     units = 4 * subs
@@ -148,19 +153,17 @@
     diagonal = row_at == col_at
     eye = jnp.where(diagonal, 1.0, 0.0).astype(jnp.bfloat16)
     turned = lax.dot_general(eye, tiles[...], NT, preferred_element_type=jnp.float32).astype(jnp.bfloat16)
-    largest = jnp.zeros((CH, CH), jnp.float32)
+    energy = jnp.zeros((CH, CH), jnp.float32)
     for u in range(units):
         side, f = u // half, u % half % subs
         at = side * subs + f
         pick = jnp.where(row_at == source[at : at + 1, :], 1.0, 0.0).astype(jnp.bfloat16)
         cycle = jnp.dot(turned[:, u * CH : (u + 1) * CH], pick, preferred_element_type=jnp.float32)
-        x = (own_ref if side == 0 else other_ref)[(u % half) * CH : (u % half + 1) * CH, :]
+        x = (own_ref if side == 0 else other_ref)[index_ref[u % half // subs], f]
         grid[u * CH : (u + 1) * CH, :PIX] = x
         grid[u * CH : (u + 1) * CH, PIX:] = cycle.astype(jnp.bfloat16)
-        size = jnp.abs(x.astype(jnp.float32))
-        largest = jnp.maximum(largest, jnp.maximum(size[:, :CH], size[:, CH:]))
-        largest = jnp.maximum(largest, jnp.abs(cycle))
-
+        x = x.astype(jnp.float32)
+        energy += x[:, :CH] * x[:, :CH] + x[:, CH:] * x[:, CH:] + cycle * cycle
     kept = mask_ref[...].astype(jnp.float32)
     kept_row = jnp.sum(jnp.where(diagonal, kept, 0.0), axis=1, keepdims=True)
     turned_kept = pltpu.roll(jnp.broadcast_to(kept, (8, CH)), CH // 2, 1)
@@ -169,15 +172,20 @@
     folded = jnp.where(lane < CH // 2, first, second)
     kept_lane = jnp.where(lax.broadcasted_iota(jnp.int32, (8, CH), 0) == 0, first, folded)
 
+    energy = jnp.sum(energy, axis=1, keepdims=True)
+
     def exponent(values):
-        top = jnp.maximum(jnp.max(values), 2.0**-60)
-        return jnp.ceil(jnp.log2(jnp.full((8, CH), top, jnp.float32)))
-
-    kept_exp = exponent(jnp.where(kept_row > 0, largest, 0.0))
-    any_exp = exponent(largest)
-    row_scale = jnp.where(kept_row > 0, jnp.exp2(-kept_exp[0:1, :]), 0.0)
+        top = jnp.full((8, CH), jnp.maximum(jnp.max(values), 2.0**-120), jnp.float32)
+        return jnp.ceil(jnp.log2(top) * (STEPS / 2) + 0.1)
+
+    kept_exp = exponent(jnp.where(kept_row > 0, energy, 0.0))
+    any_exp = exponent(energy)
+    row_scale = jnp.where(kept_row > 0, jnp.exp2(kept_exp[0:1, :] * (-1 / STEPS)), 0.0)
     lane_exps = jnp.where(kept_lane > 0, kept_exp, any_exp)
-    lane_scale = jnp.exp2(-lane_exps)
+    lane_scale = jnp.exp2(lane_exps * (-1 / STEPS))
+
+    def coded(values):
+        return jnp.round(TOP * values * lax.rsqrt(jnp.maximum(jnp.abs(values), 1e-30)))
 
     chunk = units * CH // 3
     for m in range(0, units * CH, chunk):
@@ -199,20 +207,21 @@
             at = slice((t + n) * CH, (t + n + 1) * CH)
             for l in range(4):
                 part = rows[:, l * CH : (l + 1) * CH] + inner_ref[l, at, :]
-                gram[l, at, :] = part * row_scale * lane_scale[0:1, :]
+                gram[l, at, :] = coded(part * row_scale * lane_scale[0:1, :])
             part = rows[:, 4 * CH :] + inner_ref[4, at, : CH // 2]
-            gram[4, at, : CH // 2] = part * row_scale[:, : CH // 2] * lane_scale[1:2, : CH // 2]
-
-    for g in range(8):
-        for s in range(8):
-            j = g * 8 + s
-            at = g * 144 + s * 9
-            for c in range(2):
-                for l in range(4):
-                    to = (c * 4 + l) * 9
-                    message_ref[j, to : to + 9, :] = gram[l, at + c * 72 : at + c * 72 + 9, :]
-                message_ref[j, 72:81, c * 64 : (c + 1) * 64] = gram[4, at + c * 72 : at + c * 72 + 9, : CH // 2]
-            message_ref[j, 81:88, :] = (lane_exps + kept_exp)[0:7, :]
+            gram[4, at, : CH // 2] = coded(part * row_scale[:, : CH // 2] * lane_scale[1:2, : CH // 2])
+
+    for j in range(64):
+        at = j // 8 * 144 + j % 8 * 9
+        block = stage.at[j % 4]
+        for c in range(2):
+            rows = slice(at + c * 72, at + c * 72 + 9)
+            for l in range(4):
+                to = (c * 4 + l) * 9
+                block[to : to + 9, :] = gram[l, rows, :]
+            block[72:81, c * 64 : (c + 1) * 64] = gram[4, rows, : CH // 2]
+        block[81:88, :] = (lane_exps + kept_exp)[0:7, :]
+        message_ref[j] = block[...].astype(jnp.int32).astype(jnp.int16)
 
 
 def rows_kernel(place_ref, mask_ref, near_ref, far_ref, weight_ref, kept_ref, out_ref, rows, split):
@@ -277,40 +286,42 @@
     swap = [(f, f ^ 1) for f in range(faces)]
     bf16, f32 = jnp.bfloat16, jnp.float32
 
-    copies, own = pl.pallas_call(
+    other = lax.ppermute(fields, "face", swap)
+    halo_other = lax.ppermute(halo_index, "face", swap)
+    copies = pl.pallas_call(
         edges_kernel,
-        out_shape=(shape((faces // 2, 8 * subs * SIDE, CH), bf16), shape((units // 2 * CH, PIX), bf16)),
+        out_shape=shape((faces // 2, 8 * subs * SIDE, CH), bf16),
         in_specs=[SMEM, VMEM, VMEM],
-        out_specs=(VMEM, VMEM),
+        out_specs=VMEM,
         name="edges",
     )(sample_index, fields, jnp.asarray(edge_picker()))
 
-    other = lax.ppermute(own, "face", swap)
-    halo_other = lax.ppermute(halo_index, "face", swap)
+    copies, other, halo_other = lax.optimization_barrier((copies, other, halo_other))
     same_core = [[f for f in range(c, faces, 2)] for c in range(2)]
     table = lax.all_to_all(copies, "face", 0, 0, axis_index_groups=same_core)
-    table_other = lax.ppermute(table, "face", swap)
 
     mask_row = channel_mask[None]
     place = jnp.stack([core, face * samples + sample, jnp.int32(2 * subs * PIX * faces * samples)])
     inner_taps, outer_taps = tap_matrices()
-    limit = pltpu.CompilerParams(vmem_limit_bytes=56 * 2**20)
+    limit = pltpu.CompilerParams(vmem_limit_bytes=28 * 2**20)
 
     inner = pl.pallas_call(
         inner_kernel,
         out_shape=shape((5, K, CH), f32),
-        in_specs=[SMEM] + [VMEM] * 3,
+        in_specs=[SMEM] * 2 + [VMEM] * 3,
         out_specs=VMEM,
         scratch_shapes=[pltpu.VMEM((K, units * PIX), bf16)],
         compiler_params=limit,
         cost_estimate=pl.CostEstimate(flops=6 * 10**9, bytes_accessed=5 * 10**6, transcendentals=0),
         name="inner",
-    )(place, own, other, jnp.asarray(inner_taps))
-
+    )(place, sample_index, fields, other, jnp.asarray(inner_taps))
+
+    table, inner = lax.optimization_barrier((table, inner))
+    table_other = lax.ppermute(table, "face", swap)
     message = pl.pallas_call(
         functools.partial(outer_kernel, subs),
-        out_shape=shape((64, ROWS, CH), f32),
-        in_specs=[SMEM] * 3 + [VMEM] * 9,
+        out_shape=shape((64, ROWS, CH), jnp.int16),
+        in_specs=[SMEM] * 4 + [VMEM] * 9,
         out_specs=VMEM,
         scratch_shapes=[
             pltpu.VMEM((units * CH, CH), bf16),
@@ -318,14 +329,16 @@
             pltpu.VMEM((K, units * RIM), bf16),
             pltpu.VMEM((5, K, CH), f32),
             pltpu.VMEM((8, CH), jnp.int32),
+            pltpu.VMEM((4, ROWS, CH), f32),
         ],
         compiler_params=limit,
         name="outer",
     )(
         place,
+        sample_index,
         halo_index,
         halo_other,
-        own,
+        fields,
         other,
         table,
         table_other,
@@ -337,10 +350,10 @@
     )
 
     groups = [[f * samples + s for f in range(c, faces, 2) for s in range(samples)] for c in range(2)]
-    landed = lax.all_to_all(message.astype(jnp.float16), AXES, 0, 0, axis_index_groups=groups)
+    landed = lax.all_to_all(message, AXES, 0, 0, axis_index_groups=groups)
     landed = landed.astype(f32)
     exps = jnp.where(jnp.arange(ROWS)[None, :, None] < 72, landed[:, 81:82, :], landed[:, 82:83, :])
-    near = jnp.sum(landed * jnp.exp2(exps), axis=0)
+    near = jnp.sum(landed * jnp.abs(landed) * jnp.exp2(exps * (1 / STEPS)), axis=0) * TOP**-2
     far = lax.ppermute(near, "face", swap)
 
     return pl.pallas_call(

time: 87.8 us -> 75.6 us (0.86)
  waiting for transfers between devices: 35 us -> 25.7 us
  Pallas kernels: 25.6 us -> 20.8 us
  local copies, waits for them, and re-layouts: 2.32 us -> 5.38 us
  other arithmetic: 4.67 us -> 1.62 us
  starting transfers between devices: 19.8 us -> 21.6 us
    all_to_all x1, waiting for transfers between devices: 12.1 us -> 0.54 us  [per_device(): table = lax.all_to_all(copies, 'face', 0, 0, axis_index_groups=same_core)]
    convert_element_type x1 -> x0, other arithmetic: 3.12 us -> none  [per_device(): message.astype(jnp.float16)]
    unnamed x12 -> x22, local copies, waits for them, and re-layouts: 2.26 us -> 5.32 us
    pallas_call x1, Pallas kernels: 12 us -> 9.45 us  [per_device(): pl.pallas_call(inner_kernel, out_shape=shape((5, K, CH), f32), in_specs=[...]
    all_to_all x1, starting transfers between devices: 7.18 us -> 9.61 us  [per_device(): landed = lax.all_to_all(message, AXES, 0, 0, axis_index_groups=groups)]
    pallas_call x1, Pallas kernels: 9.26 us -> 7.09 us  [per_device(): pl.pallas_call(functools.partial(outer_kernel, subs), out_shape=shape((64...]
    ppermute x1, waiting for transfers between devices: 0.01 us -> 1.91 us  [per_device(): table_other = lax.ppermute(table, 'face', swap)]
  transfers between devices with their start and end apart: 6 -> 6, of which waited for: 3 -> 4; matrix products, arithmetic and copies ran while one was open for 1% -> 0% of each run, Pallas kernels for 14% -> 16%
where the time goes in v3:
time: 75.6 us; the launch traced here: 75.2 us
  waiting for transfers between devices  25.7 us (34%)
  starting transfers between devices  21.6 us (29%)
  Pallas kernels  20.8 us (28%)
  local copies, waits for them, and re-layouts  5.38 us (7%)
  other arithmetic  1.62 us (2%)
    all_to_all x1, waiting for transfers between devices, per_device(): landed = lax.all_to_all(message, AXES, 0, 0, axis_index_groups=groups)  22.3 us
    all_to_all x1, starting transfers between devices, per_device(): landed = lax.all_to_all(message, AXES, 0, 0, axis_index_groups=groups)  9.61 us
    pallas_call x1, Pallas kernels, per_device(): pl.pallas_call(inner_kernel, out_shape=shape((5, K, CH), f32), in_specs=[...  9.45 us
    all_to_all x1, starting transfers between devices, per_device(): table = lax.all_to_all(copies, 'face', 0, 0, axis_index_groups=same_core)  7.68 us
    pallas_call x1, Pallas kernels, per_device(): pl.pallas_call(functools.partial(outer_kernel, subs), out_shape=shape((64...  7.09 us
    unnamed x22, local copies, waits for them, and re-layouts  5.32 us
    pallas_call x1, Pallas kernels, per_device(): pl.pallas_call(edges_kernel, out_shape=shape((faces // 2, 8 * subs * SIDE...  2.21 us
    pallas_call x1, Pallas kernels, per_device(): pl.pallas_call(rows_kernel, out_shape=shape((TAPS, K + weight.shape[1]),...  2.06 us
  transfers between devices with their start and end apart: 6, of which 4 were waited for; matrix products, arithmetic and copies ran while one was open for 0% of the time, Pallas kernels for 16%

profile of v3, /device:TPU:1, one launch (start us, length us, event | category | flops | bytes accessed | tf_op | source)
XLA Modules:
  0.0 75.2 jit_solution(6466667000580089235)
XLA Ops:
  0.0 1.4 %collective-permute-start = (bf16[3,3,128,256]{3,2,1,0:T(8,128)(2,1)}, bf16[3,3,128,256]{3,2,1,0:T(8,128)(2,1)S(1)}, u32[]{:S(2)}, u32[]{:S(2)}) collective-permute-start(bf16[3,3,128,256]{3,2,1,0:T(8,128)(2,1)} %own_ref.3), channel_id=1, source_target_pairs={{0,8},{8,0},{16,24},{24,16},{32,40},{40,32},{48,56},{56,48},{64,72... | collective-permute-start | bytes 1769480 | tf_op jit(solution)/shard_map/ppermute | solution.py:289
  1.4 0.0 collective-permute-start.1
  1.4 2.2 %edges.1 = bf16[8,384,128]{2,1,0:T(8,128)(2,1)} custom-call(s32[2]{0:T(128)} %index_ref.5, bf16[3,3,128,256]{3,2,1,0:T(8,128)(2,1)} %own_ref.3, bf16[64,256]{1,0:T(8,128)(2,1)} %constant.34.clone.pick_ref), custom_call_target="tpu_custom_call" | custom-call | tf_op jit(solution)/shard_map/edges/pallas_call | solution.py:291
  3.6 0.0 collective-permute-done.1.halo_other_ref.halo_rows_other_ref
  3.6 0.0 collective-permute-done.other_ref
  3.6 7.7 %all-to-all-start = ((bf16[8,384,128]{2,1,0:T(8,128)(2,1)}), bf16[8,384,128]{2,1,0:T(8,128)(2,1)S(1)}, u32[]{:S(2)}, u32[]{:S(2)}) async-start(bf16[8,384,128]{2,1,0:T(8,128)(2,1)} %edges.1), calls=%async_computation | async-start | bytes 1572864 | tf_op jit(solution)/shard_map/all_to_all | solution.py:301
  11.3 0.1 pad_add_fusion.core_ref.place_ref
  11.4 0.0 copy-done.2
  11.4 0.0 copy-done.7
  11.4 1.3 %copy-done.8 = bf16[9,256,256]{2,1,0:T(8,128)(2,1)S(1)} copy-done((bf16[9,256,256]{2,1,0:T(8,128)(2,1)S(1)}, bf16[9,256,256]{2,1,0:T(8,128)(2,1)}, u32[]{:S(2)}) %copy-start.8) | copy-done | bytes 1179672
  12.7 9.4 %inner.1.inner_ref = f32[5,1152,128]{2,1,0:T(8,128)S(1)} custom-call(s32[3]{0:T(128)S(1)} %pad_add_fusion.core_ref.place_ref, s32[2]{0:T(128)S(1)} %copy-done.7, bf16[3,3,128,256]{3,2,1,0:T(8,128)(2,1)S(1)} %copy-done.2, bf16[3,3,128,256]{3,2,1,0:T(8,128)(2,1)S(1)} %collective-permute-done.other_ref, bf16[9,256,256]{2,1,0:T(8,128)(2,1)S(1)} %copy-done.8), custom_call_target="tpu_custom_call" | custom-call | flops 6000000000 | bytes 5000000 | tf_op jit(solution)/shard_map/inner/pallas_call | solution.py:308
  22.2 0.0 copy-start
  22.2 1.6 %copy-done = f32[5,1152,128]{2,1,0:T(8,128)} copy-done((f32[5,1152,128]{2,1,0:T(8,128)}, f32[5,1152,128]{2,1,0:T(8,128)S(1)}, u32[]{:S(2)}) %copy-start) | copy-done | bytes 2949144
  23.8 0.5 all-to-all-done.table_own_ref
  24.3 1.1 %collective-permute-start.2 = (bf16[8,384,128]{2,1,0:T(8,128)(2,1)S(1)}, bf16[8,384,128]{2,1,0:T(8,128)(2,1)S(1)}, u32[]{:S(2)}, u32[]{:S(2)}) collective-permute-start(bf16[8,384,128]{2,1,0:T(8,128)(2,1)S(1)} %all-to-all-done.table_own_ref), channel_id=1, source_target_pairs={{0,8},{8,0},{16,24},{24,16},{32,40},{40,32},{48,56},{56,48},{64,72... | collective-permute-start | bytes 2359304 | tf_op jit(solution)/shard_map/ppermute | solution.py:320
  25.4 1.9 %collective-permute-done.2.table_other_ref = bf16[8,384,128]{2,1,0:T(8,128)(2,1)S(1)} collective-permute-done((bf16[8,384,128]{2,1,0:T(8,128)(2,1)S(1)}, bf16[8,384,128]{2,1,0:T(8,128)(2,1)S(1)}, u32[]{:S(2)}, u32[]{:S(2)}) %collective-permute-start.2) | collective-permute-done | bytes 786464 | tf_op jit(solution)/shard_map/ppermute | solution.py:320
  27.3 0.0 copy-done.5
  27.3 0.0 copy-done.3
  27.3 0.0 copy-done.4
  27.3 0.0 copy-done.6
  27.3 0.0 copy-start.1
  27.3 1.8 %copy-done.1 = f32[5,1152,128]{2,1,0:T(8,128)S(1)} copy-done((f32[5,1152,128]{2,1,0:T(8,128)S(1)}, f32[5,1152,128]{2,1,0:T(8,128)}, u32[]{:S(2)}) %copy-start.1) | copy-done | bytes 2949144
  29.2 7.1 %outer.1 = s16[64,88,128]{2,1,0:T(8,128)(2,1)} custom-call(s32[3]{0:T(128)S(1)} %pad_add_fusion.core_ref.place_ref, s32[2]{0:T(128)S(1)} %copy-done.7, s32[3,68]{1,0:T(4,128)S(1)} %copy-done.4, s32[3,68]{1,0:T(4,128)S(1)} %collective-permute-done.1.halo_other_ref.halo_rows_other_ref, bf16[3,3,128,256]{3,2,1,0:T(8,128)(2,1)S(1)} %copy-done.2, ...), custom_call_target="tpu_custom_call" | custom-call | tf_op jit(solution)/shard_map/outer/pallas_call | solution.py:321
  36.3 9.6 %all-to-all-start.1 = ((s16[64,88,128]{2,1,0:T(8,128)(2,1)}), s16[64,88,128]{2,1,0:T(8,128)(2,1)S(1)}, u32[]{:S(2)}, u32[]{:S(2)}) async-start(s16[64,88,128]{2,1,0:T(8,128)(2,1)} %outer.1), calls=%async_computation.1 | async-start | bytes 2883584 | tf_op jit(solution)/shard_map/all_to_all | solution.py:353
  45.9 22.3 %all-to-all-done.1 = s16[64,88,128]{2,1,0:T(8,128)(2,1)S(1)} async-done(((s16[64,88,128]{2,1,0:T(8,128)(2,1)}), s16[64,88,128]{2,1,0:T(8,128)(2,1)S(1)}, u32[]{:S(2)}, u32[]{:S(2)}) %all-to-all-start.1) | async-done | bytes 1441824 | tf_op jit(solution)/shard_map/all_to_all | solution.py:353
  68.2 0.4 convert_element_type.3
  68.6 0.1 fusion.2
  68.7 1.2 %fusion.1 = f32[88,128]{1,0:T(8,128)S(1)} fusion(f32[64,128]{1,0:T(8,128)S(1)} %bitcast.8, f32[64,128]{1,0:T(8,128)S(1)} %bitcast.7, pred[88]{0:T(512)(128)(4,1)S(1)} %iota_compare_fusion, s16[64,88,128]{2,1,0:T(8,128)(2,1)S(1)} %all-to-all-done.1), kind=kLoop, calls=%fused_computation.2 | loop fusion | flops 5035008 | bytes 1552472 | tf_op jit(solution)/shard_map/reduce_sum | solution.py:356
  69.9 1.8 %collective-permute-start.3 = (f32[88,128]{1,0:T(8,128)S(1)}, f32[88,128]{1,0:T(8,128)S(1)}, u32[]{:S(2)}, u32[]{:S(2)}) collective-permute-start(f32[88,128]{1,0:T(8,128)S(1)} %broadcast_multiply_fusion.near_ref), channel_id=1, source_target_pairs={{0,8},{8,0},{16,24},{24,16},{32,40},{40,32},{48,56},{56,48},{64,72... | collective-permute-start | bytes 135176 | tf_op jit(solution)/shard_map/ppermute | solution.py:357
  71.7 0.9 %collective-permute-done.3.far_ref = f32[88,128]{1,0:T(8,128)S(1)} collective-permute-done((f32[88,128]{1,0:T(8,128)S(1)}, f32[88,128]{1,0:T(8,128)S(1)}, u32[]{:S(2)}, u32[]{:S(2)}) %collective-permute-start.3) | collective-permute-done | bytes 45088 | tf_op jit(solution)/shard_map/ppermute | solution.py:357
  72.5 0.6 copy-done.10
  73.1 2.1 %rows.1 = f32[9,1408]{1,0:T(8,128)} custom-call(s32[3]{0:T(128)} %copy-done.5, s32[128]{0:T(128)} %mask_ref.1, f32[88,128]{1,0:T(8,128)} %copy-done.9, f32[88,128]{1,0:T(8,128)} %copy-done.10, bf16[1152,256]{1,0:T(8,128)(2,1)} %weight_ref.1, s32[1,128]{1,0:T(1,128)} %bitcast.5), custom_call_target="tpu_custom_call" | custom-call | tf_op jit(solution)/shard_map/rows/pallas_call | solution.py:359
  (12 shorter events, 0.0 us)
Async XLA Ops:
  0.0 11.4 %copy-start.2 = (bf16[3,3,128,256]{3,2,1,0:T(8,128)(2,1)S(1)}, bf16[3,3,128,256]{3,2,1,0:T(8,128)(2,1)}, u32[]{:S(2)}) copy-start(bf16[3,3,128,256]{3,2,1,0:T(8,128)(2,1)} %own_ref.3) | copy-start | bytes 1769476
  0.0 11.4 %copy-start.7 = (s32[2]{0:T(128)S(1)}, s32[2]{0:T(128)}, u32[]{:S(2)}) copy-start(s32[2]{0:T(128)} %index_ref.5) | copy-start | bytes 28
  0.0 3.6 %collective-permute-start = (bf16[3,3,128,256]{3,2,1,0:T(8,128)(2,1)}, bf16[3,3,128,256]{3,2,1,0:T(8,128)(2,1)S(1)}, u32[]{:S(2)}, u32[]{:S(2)}) collective-permute-start(bf16[3,3,128,256]{3,2,1,0:T(8,128)(2,1)} %own_ref.3), channel_id=1, source_target_pairs={{0,8},{8,0},{16,24},{24,16},{32,40},{40,32},{48,56},{56,48},{64,72... | collective-permute-start | bytes 1769480 | tf_op jit(solution)/shard_map/ppermute | solution.py:289
  1.4 2.2 %collective-permute-start.1 = (s32[3,68]{1,0:T(4,128)}, s32[3,68]{1,0:T(4,128)S(1)}, u32[]{:S(2)}, u32[]{:S(2)}) collective-permute-start(s32[3,68]{1,0:T(4,128)} %halo_rows_own_ref.1), channel_id=1, source_target_pairs={{0,8},{8,0},{16,24},{24,16},{32,40},{40,32},{48,56},{56,48},{64,72... | collective-permute-start | bytes 2456 | tf_op jit(solution)/shard_map/ppermute | solution.py:290
  3.6 20.6 %all-to-all-start = ((bf16[8,384,128]{2,1,0:T(8,128)(2,1)}), bf16[8,384,128]{2,1,0:T(8,128)(2,1)S(1)}, u32[]{:S(2)}, u32[]{:S(2)}) async-start(bf16[8,384,128]{2,1,0:T(8,128)(2,1)} %edges.1), calls=%async_computation | async-start | bytes 1572864 | tf_op jit(solution)/shard_map/all_to_all | solution.py:301
  11.4 1.3 %copy-start.8 = (bf16[9,256,256]{2,1,0:T(8,128)(2,1)S(1)}, bf16[9,256,256]{2,1,0:T(8,128)(2,1)}, u32[]{:S(2)}) copy-start(bf16[9,256,256]{2,1,0:T(8,128)(2,1)} %constant.35.clone.taps_ref) | copy-start | bytes 3538948
  12.7 14.6 %copy-start.5 = (s32[3]{0:T(128)}, s32[3]{0:T(128)S(1)}, u32[]{:S(2)}) copy-start(s32[3]{0:T(128)S(1)} %pad_add_fusion.core_ref.place_ref) | copy-start | bytes 40
  12.7 14.6 %copy-start.3 = (bf16[384,640]{1,0:T(8,128)(2,1)S(1)}, bf16[384,640]{1,0:T(8,128)(2,1)}, u32[]{:S(2)}) copy-start(bf16[384,640]{1,0:T(8,128)(2,1)} %constant.36.clone.taps_ref) | copy-start | bytes 1474564
  12.7 14.6 %copy-start.4 = (s32[3,68]{1,0:T(4,128)S(1)}, s32[3,68]{1,0:T(4,128)}, u32[]{:S(2)}) copy-start(s32[3,68]{1,0:T(4,128)} %halo_rows_own_ref.1) | copy-start | bytes 2452
  12.7 14.6 %copy-start.6 = (s32[128]{0:T(128)S(1)}, s32[128]{0:T(128)}, u32[]{:S(2)}) copy-start(s32[128]{0:T(128)} %mask_ref.1) | copy-start | bytes 1540
  22.2 1.6 %copy-start = (f32[5,1152,128]{2,1,0:T(8,128)}, f32[5,1152,128]{2,1,0:T(8,128)S(1)}, u32[]{:S(2)}) copy-start(f32[5,1152,128]{2,1,0:T(8,128)S(1)} %inner.1.inner_ref) | copy-start | bytes 8847364
  24.3 3.0 %collective-permute-start.2 = (bf16[8,384,128]{2,1,0:T(8,128)(2,1)S(1)}, bf16[8,384,128]{2,1,0:T(8,128)(2,1)S(1)}, u32[]{:S(2)}, u32[]{:S(2)}) collective-permute-start(bf16[8,384,128]{2,1,0:T(8,128)(2,1)S(1)} %all-to-all-done.table_own_ref), channel_id=1, source_target_pairs={{0,8},{8,0},{16,24},{24,16},{32,40},{40,32},{48,56},{56,48},{64,72... | collective-permute-start | bytes 2359304 | tf_op jit(solution)/shard_map/ppermute | solution.py:320
  27.3 1.8 %copy-start.1 = (f32[5,1152,128]{2,1,0:T(8,128)S(1)}, f32[5,1152,128]{2,1,0:T(8,128)}, u32[]{:S(2)}) copy-start(f32[5,1152,128]{2,1,0:T(8,128)} %copy-done) | copy-start | bytes 8847364
  36.3 32.0 %all-to-all-start.1 = ((s16[64,88,128]{2,1,0:T(8,128)(2,1)}), s16[64,88,128]{2,1,0:T(8,128)(2,1)S(1)}, u32[]{:S(2)}, u32[]{:S(2)}) async-start(s16[64,88,128]{2,1,0:T(8,128)(2,1)} %outer.1), calls=%async_computation.1 | async-start | bytes 2883584 | tf_op jit(solution)/shard_map/all_to_all | solution.py:353
  69.8 2.7 %copy-start.9 = (f32[88,128]{1,0:T(8,128)}, f32[88,128]{1,0:T(8,128)S(1)}, u32[]{:S(2)}) copy-start(f32[88,128]{1,0:T(8,128)S(1)} %broadcast_multiply_fusion.near_ref) | copy-start | bytes 135172
  69.9 2.7 %collective-permute-start.3 = (f32[88,128]{1,0:T(8,128)S(1)}, f32[88,128]{1,0:T(8,128)S(1)}, u32[]{:S(2)}, u32[]{:S(2)}) collective-permute-start(f32[88,128]{1,0:T(8,128)S(1)} %broadcast_multiply_fusion.near_ref), channel_id=1, source_target_pairs={{0,8},{8,0},{16,24},{24,16},{32,40},{40,32},{48,56},{56,48},{64,72... | collective-permute-start | bytes 135176 | tf_op jit(solution)/shard_map/ppermute | solution.py:357
  72.5 0.6 copy-start.10

commit v4 on v3

--- a/solution.py
+++ b/solution.py
@@ -36,7 +36,7 @@
     return out.astype(ml_dtypes.bfloat16)
 
 
-def tap_matrices():
+def rim_matrix():
     whole = np.zeros((TAPS, PIX + CH, PIX), np.float32)
     for t in range(TAPS):
         for y in range(SIDE):
@@ -54,12 +54,10 @@
                     k = (u - 1) * SIDE + v - 1
                 whole[t, k, y * SIDE + x] = 1
     rim = [p for p in range(PIX) if p // SIDE in (0, SIDE - 1) or p % SIDE in (0, SIDE - 1)]
-    inner = whole[:, :PIX].copy()
-    inner[:, :, rim] = 0
     outer = np.zeros((PIX + CH, 640), np.float32)
     for t in range(TAPS):
         outer[:, t * RIM : t * RIM + len(rim)] = whole[t][:, rim]
-    return inner.astype(ml_dtypes.bfloat16), outer.astype(ml_dtypes.bfloat16)
+    return outer.astype(ml_dtypes.bfloat16)
 
 
 def edges_kernel(index_ref, fields_ref, pick_ref, copies_ref):
@@ -74,53 +72,45 @@
                 copies_ref[d, u * 4 * SIDE : (u + 1) * 4 * SIDE, :] = edges
 
 
-def inner_kernel(core_ref, index_ref, own_ref, other_ref, taps_ref, gram_ref, patches):
+def row_blocks():
+    return [slice(t * CH, (t + 3) * CH) for t in range(0, TAPS, 3)]
+
+
+def inner_kernel(core_ref, index_ref, own_ref, other_ref, gram_ref, done_ref, patches, gram, sems):
     subs = own_ref.shape[1]
+    done_ref[...] = jnp.zeros_like(done_ref)
+    pixel = lax.broadcasted_iota(jnp.int32, (PIX, PIX), 1)
+    ahead = lax.broadcasted_iota(jnp.int32, (PIX, PIX), 0) - pixel
+    y, x = pixel // SIDE, pixel % SIDE
+    inside = (y > 0) & (y < SIDE - 1) & (x > 0) & (x < SIDE - 1)
+    ahead = jnp.where(inside, ahead, PIX)
     for t in range(TAPS):
+        shift = (t // 3 - 1) * SIDE + t % 3 - 1
+        tap = jnp.where(ahead == shift, 1.0, 0.0).astype(jnp.bfloat16)
         for n, ref in enumerate((own_ref, other_ref)):
             for s in range(2):
                 x = ref[index_ref[s]].reshape(subs * CH, PIX)
-                values = jnp.dot(x, taps_ref[t], preferred_element_type=jnp.float32)
+                values = jnp.dot(x, tap, preferred_element_type=jnp.float32)
                 values = values.astype(jnp.bfloat16)
                 for f in range(subs):
                     u = (n * 2 + s) * subs + f
                     patches[t * CH : (t + 1) * CH, u * PIX : (u + 1) * PIX] = values[f * CH : (f + 1) * CH, :]
     right = patches[pl.ds(pl.multiple_of(core_ref[0] * HALF, HALF), HALF), :]
-    for t in range(0, TAPS, 3):
-        rows = slice(t * CH, (t + 3) * CH)
+    copies = []
+    for n, rows in enumerate(row_blocks()):
         block = lax.dot_general(patches[rows, :], right, NT, preferred_element_type=jnp.float32)
         for l in range(4):
-            gram_ref[l, rows, :] = block[:, l * CH : (l + 1) * CH]
-        gram_ref[4, rows, : CH // 2] = block[:, 4 * CH :]
-
-
-def outer_kernel(
-    subs,
-    core_ref,
-    index_ref,
-    halo_own_ref,
-    halo_other_ref,
-    own_ref,
-    other_ref,
-    table_own_ref,
-    table_other_ref,
-    halo_rows_own_ref,
-    halo_rows_other_ref,
-    taps_ref,
-    mask_ref,
-    inner_ref,
-    message_ref,
-    tiles,
-    grid,
-    patches,
-    gram,
-    position,
-    stage,
-):
+            gram[l, rows, :] = block[:, l * CH : (l + 1) * CH]
+        gram[4, rows, : CH // 2] = block[:, 4 * CH :]
+        gram[4, rows, CH // 2 :] = jnp.zeros((3 * CH, CH // 2), jnp.float32)
+        copies.append(pltpu.make_async_copy(gram.at[:, rows, :], gram_ref.at[:, rows, :], sems.at[n]))
+        copies[-1].start()
+    for copy in copies:
+        copy.wait()
+
+
+def gather_kernel(subs, core_ref, halo_own_ref, halo_other_ref, table_ref, after_ref, tiles_ref):
     core = core_ref[0]
-    units = 4 * subs
-    half = units // 2
-
     for side, halo_ref in enumerate((halo_own_ref, halo_other_ref)):
         for f in range(subs):
             for n, at in enumerate(SIDE_AT + CORNER_AT):
@@ -132,10 +122,40 @@
                 near = lax.rem(device, 2) == core
                 for s in range(2):
                     row = pl.multiple_of((s * subs + local) * 4 * SIDE + edge * SIDE, SIDE)
-                    mine = table_own_ref[device // 2, pl.ds(row, SIDE), :]
-                    theirs = table_other_ref[device // 2, pl.ds(row, SIDE), :]
-                    u = side * half + s * subs + f
-                    tiles[u * CH + n * SIDE : u * CH + (n + 1) * SIDE, :] = jnp.where(near, mine, theirs)
+                    tile = table_ref[device // 2, pl.ds(row, SIDE), :]
+                    u = (side * 2 + s) * subs + f
+                    tiles_ref[u * CH + n * SIDE : u * CH + (n + 1) * SIDE, :] = jnp.where(near, tile, jnp.zeros_like(tile))
+
+
+def outer_kernel(
+    subs,
+    core_ref,
+    index_ref,
+    own_ref,
+    other_ref,
+    tiles_own_ref,
+    tiles_other_ref,
+    halo_rows_own_ref,
+    halo_rows_other_ref,
+    taps_ref,
+    mask_ref,
+    inner_ref,
+    message_ref,
+    grid,
+    patches,
+    gram,
+    position,
+    stage,
+    inner,
+    sems,
+):
+    core = core_ref[0]
+    units = 4 * subs
+    half = units // 2
+    copies = []
+    for n, rows in enumerate(row_blocks()):
+        copies.append(pltpu.make_async_copy(inner_ref.at[:, rows, :], inner.at[:, rows, :], sems.at[n]))
+        copies[-1].start()
 
     lane = lax.broadcasted_iota(jnp.int32, (8, CH), 1)
     base = jnp.full((8, CH), -1000, jnp.int32)
@@ -152,13 +172,18 @@
     col_at = lax.broadcasted_iota(jnp.int32, (CH, CH), 1)
     diagonal = row_at == col_at
     eye = jnp.where(diagonal, 1.0, 0.0).astype(jnp.bfloat16)
-    turned = lax.dot_general(eye, tiles[...], NT, preferred_element_type=jnp.float32).astype(jnp.bfloat16)
+    split = units * CH // 2
+    turned = []
+    for mine, theirs in ((0, split), (split, 0)):
+        tiles = tiles_own_ref[mine : mine + split, :] + tiles_other_ref[theirs : theirs + split, :]
+        tiles = lax.dot_general(eye, tiles, NT, preferred_element_type=jnp.float32)
+        turned.append(tiles.astype(jnp.bfloat16))
     energy = jnp.zeros((CH, CH), jnp.float32)
     for u in range(units):
         side, f = u // half, u % half % subs
         at = side * subs + f
         pick = jnp.where(row_at == source[at : at + 1, :], 1.0, 0.0).astype(jnp.bfloat16)
-        cycle = jnp.dot(turned[:, u * CH : (u + 1) * CH], pick, preferred_element_type=jnp.float32)
+        cycle = jnp.dot(turned[side][:, u % half * CH : (u % half + 1) * CH], pick, preferred_element_type=jnp.float32)
         x = (own_ref if side == 0 else other_ref)[index_ref[u % half // subs], f]
         grid[u * CH : (u + 1) * CH, :PIX] = x
         grid[u * CH : (u + 1) * CH, PIX:] = cycle.astype(jnp.bfloat16)
@@ -202,13 +227,14 @@
         block = lax.dot_general(
             patches[t * CH : (t + 3) * CH, :], right, NT, preferred_element_type=jnp.float32
         )
+        copies[t // 3].wait()
         for n in range(3):
             rows = block[n * CH : (n + 1) * CH, :]
             at = slice((t + n) * CH, (t + n + 1) * CH)
             for l in range(4):
-                part = rows[:, l * CH : (l + 1) * CH] + inner_ref[l, at, :]
+                part = rows[:, l * CH : (l + 1) * CH] + inner[l, at, :]
                 gram[l, at, :] = coded(part * row_scale * lane_scale[0:1, :])
-            part = rows[:, 4 * CH :] + inner_ref[4, at, : CH // 2]
+            part = rows[:, 4 * CH :] + inner[4, at, : CH // 2]
             gram[4, at, : CH // 2] = coded(part * row_scale[:, : CH // 2] * lane_scale[1:2, : CH // 2])
 
     for j in range(64):
@@ -222,6 +248,18 @@
             block[72:81, c * 64 : (c + 1) * 64] = gram[4, rows, : CH // 2]
         block[81:88, :] = (lane_exps + kept_exp)[0:7, :]
         message_ref[j] = block[...].astype(jnp.int32).astype(jnp.int16)
+
+
+def sum_kernel(landed_ref, sum_ref):
+    whole = jnp.zeros((72, CH), jnp.float32)
+    folded = jnp.zeros((ROWS - 72, CH), jnp.float32)
+    for j in range(landed_ref.shape[0]):
+        codes = landed_ref[j].astype(jnp.int32).astype(jnp.float32)
+        scale = jnp.exp2(codes[80:88, :] * (1 / STEPS))
+        whole += codes[:72, :] * jnp.abs(codes[:72, :]) * scale[1:2, :]
+        folded += codes[72:, :] * jnp.abs(codes[72:, :]) * scale[2:3, :]
+    sum_ref[:72, :] = whole * TOP**-2
+    sum_ref[72:, :] = folded * TOP**-2
 
 
 def rows_kernel(place_ref, mask_ref, near_ref, far_ref, weight_ref, kept_ref, out_ref, rows, split):
@@ -271,6 +309,7 @@
 
 VMEM = pl.BlockSpec(memory_space=pltpu.VMEM)
 SMEM = pl.BlockSpec(memory_space=pltpu.SMEM)
+HBM = pl.BlockSpec(memory_space=pltpu.HBM)
 
 
 def shape(dims, kind):
@@ -302,58 +341,72 @@
 
     mask_row = channel_mask[None]
     place = jnp.stack([core, face * samples + sample, jnp.int32(2 * subs * PIX * faces * samples)])
-    inner_taps, outer_taps = tap_matrices()
-    limit = pltpu.CompilerParams(vmem_limit_bytes=28 * 2**20)
-
-    inner = pl.pallas_call(
+
+    inner, done = pl.pallas_call(
         inner_kernel,
-        out_shape=shape((5, K, CH), f32),
-        in_specs=[SMEM] * 2 + [VMEM] * 3,
-        out_specs=VMEM,
-        scratch_shapes=[pltpu.VMEM((K, units * PIX), bf16)],
-        compiler_params=limit,
+        out_shape=(pltpu.HBM((5, K, CH), f32), shape((8, CH), f32)),
+        in_specs=[SMEM] * 2 + [VMEM] * 2,
+        out_specs=(HBM, VMEM),
+        scratch_shapes=[
+            pltpu.VMEM((K, units * PIX), bf16),
+            pltpu.VMEM((5, K, CH), f32),
+            pltpu.SemaphoreType.DMA((3,)),
+        ],
+        compiler_params=pltpu.CompilerParams(vmem_limit_bytes=28 * 2**20),
         cost_estimate=pl.CostEstimate(flops=6 * 10**9, bytes_accessed=5 * 10**6, transcendentals=0),
         name="inner",
-    )(place, sample_index, fields, other, jnp.asarray(inner_taps))
-
-    table, inner = lax.optimization_barrier((table, inner))
-    table_other = lax.ppermute(table, "face", swap)
+    )(place, sample_index, fields, other)
+
+    tiles = pl.pallas_call(
+        functools.partial(gather_kernel, subs),
+        out_shape=shape((units * CH, CH), bf16),
+        in_specs=[SMEM] * 3 + [VMEM] * 2,
+        out_specs=VMEM,
+        compiler_params=pltpu.CompilerParams(vmem_limit_bytes=4 * 2**20),
+        name="gather",
+    )(place, halo_index, halo_other, table, done)
+    tiles_other = lax.ppermute(tiles, "face", swap)
+
     message = pl.pallas_call(
         functools.partial(outer_kernel, subs),
         out_shape=shape((64, ROWS, CH), jnp.int16),
-        in_specs=[SMEM] * 4 + [VMEM] * 9,
+        in_specs=[SMEM] * 2 + [VMEM] * 8 + [HBM],
         out_specs=VMEM,
         scratch_shapes=[
-            pltpu.VMEM((units * CH, CH), bf16),
             pltpu.VMEM((units * CH, PIX + CH), bf16),
             pltpu.VMEM((K, units * RIM), bf16),
             pltpu.VMEM((5, K, CH), f32),
             pltpu.VMEM((8, CH), jnp.int32),
             pltpu.VMEM((4, ROWS, CH), f32),
+            pltpu.VMEM((5, K, CH), f32),
+            pltpu.SemaphoreType.DMA((3,)),
         ],
-        compiler_params=limit,
+        compiler_params=pltpu.CompilerParams(vmem_limit_bytes=28 * 2**20),
         name="outer",
     )(
         place,
         sample_index,
+        fields,
+        other,
+        tiles,
+        tiles_other,
         halo_index,
         halo_other,
-        fields,
-        other,
-        table,
-        table_other,
-        halo_index,
-        halo_other,
-        jnp.asarray(outer_taps),
+        jnp.asarray(rim_matrix()),
         mask_row,
-        inner,
+        pltpu.with_memory_space_constraint(inner, pltpu.HBM),
     )
 
     groups = [[f * samples + s for f in range(c, faces, 2) for s in range(samples)] for c in range(2)]
     landed = lax.all_to_all(message, AXES, 0, 0, axis_index_groups=groups)
-    landed = landed.astype(f32)
-    exps = jnp.where(jnp.arange(ROWS)[None, :, None] < 72, landed[:, 81:82, :], landed[:, 82:83, :])
-    near = jnp.sum(landed * jnp.abs(landed) * jnp.exp2(exps * (1 / STEPS)), axis=0) * TOP**-2
+    near = pl.pallas_call(
+        sum_kernel,
+        out_shape=shape((ROWS, CH), f32),
+        in_specs=[VMEM],
+        out_specs=VMEM,
+        compiler_params=pltpu.CompilerParams(vmem_limit_bytes=8 * 2**20),
+        name="total",
+    )(landed)
     far = lax.ppermute(near, "face", swap)
 
     return pl.pallas_call(
@@ -362,6 +415,7 @@
         in_specs=[SMEM] * 2 + [VMEM] * 4,
         out_specs=VMEM,
         scratch_shapes=[pltpu.VMEM((16, K), f32), pltpu.VMEM((48, K), bf16)],
+        compiler_params=pltpu.CompilerParams(vmem_limit_bytes=8 * 2**20),
         name="rows",
     )(place, channel_mask, near, far, weight, mask_row)
 

time: 75.6 us -> 69.4 us (0.918)
  blocking collectives: 0 us -> 30 us
  waiting for transfers between devices: 25.7 us -> 4.59 us
  starting transfers between devices: 21.6 us -> 12.2 us
  local copies, waits for them, and re-layouts: 5.38 us -> 0.03 us
  other arithmetic: 1.62 us -> 0.08 us
  Pallas kernels: 20.8 us -> 22.1 us
    all_to_all x0 -> x1, blocking collectives: none -> 30 us  [per_device(): landed = lax.all_to_all(message, AXES, 0, 0, axis_index_groups=groups)]
    all_to_all x1 -> x0, waiting for transfers between devices: 22.3 us -> none  [per_device(): landed = lax.all_to_all(message, AXES, 0, 0, axis_index_groups=groups)]
    all_to_all x1 -> x0, starting transfers between devices: 9.61 us -> none  [per_device(): landed = lax.all_to_all(message, AXES, 0, 0, axis_index_groups=groups)]
    unnamed x22 -> x12, local copies, waits for them, and re-layouts: 5.32 us -> 0.03 us
    pallas_call x1 -> x3, Pallas kernels: 9.45 us -> 12.9 us  [the longest x1 10.5 us: per_device(): pl.pallas_call(inner_kernel, out_shape=(pltpu.HBM((5, K, CH), f32), shape...]
    all_to_all x1, waiting for transfers between devices: 0.54 us -> 2.36 us  [per_device(): table = lax.all_to_all(copies, 'face', 0, 0, axis_index_groups=same_core)]
    pallas_call x1, Pallas kernels: 7.09 us -> 5.55 us  [per_device(): pl.pallas_call(functools.partial(outer_kernel, subs), out_shape=shape((64...]
    reduce_sum x1 -> x0, other arithmetic: 1.16 us -> none  [per_device(): jnp.sum(landed * jnp.abs(landed) * jnp.exp2(exps * (1 / STEPS)), axis=0)]
  transfers between devices with their start and end apart: 6 -> 5, of which waited for: 4 -> 3; matrix products, arithmetic and copies ran while one was open for 0% -> 0% of each run, Pallas kernels for 16% -> 18%
where the time goes in v4:
time: 69.4 us; the launch traced here: 69.1 us
  blocking collectives  30 us (43%)
  Pallas kernels  22.1 us (32%)
  starting transfers between devices  12.2 us (18%)
  waiting for transfers between devices  4.59 us (7%)
    all_to_all x1, blocking collectives, per_device(): landed = lax.all_to_all(message, AXES, 0, 0, axis_index_groups=groups)  30 us
    pallas_call x1, Pallas kernels, per_device(): pl.pallas_call(inner_kernel, out_shape=(pltpu.HBM((5, K, CH), f32), shape...  10.5 us
    all_to_all x1, starting transfers between devices, per_device(): table = lax.all_to_all(copies, 'face', 0, 0, axis_index_groups=same_core)  7.68 us
    pallas_call x1, Pallas kernels, per_device(): pl.pallas_call(functools.partial(outer_kernel, subs), out_shape=shape((64...  5.55 us
    all_to_all x1, waiting for transfers between devices, per_device(): table = lax.all_to_all(copies, 'face', 0, 0, axis_index_groups=same_core)  2.36 us
    pallas_call x1, Pallas kernels, per_device(): pl.pallas_call(edges_kernel, out_shape=shape((faces // 2, 8 * subs * SIDE...  2.22 us
    pallas_call x1, Pallas kernels, per_device(): pl.pallas_call(functools.partial(gather_kernel, subs), out_shape=shape((u...  1.74 us
    ppermute x1, starting transfers between devices, per_device(): far = lax.ppermute(near, 'face', swap)  1.74 us
  transfers between devices with their start and end apart: 5, of which 3 were waited for; matrix products, arithmetic and copies ran while one was open for 0% of the time, Pallas kernels for 18%

profile of v4, /device:TPU:1, one launch (start us, length us, event | category | flops | bytes accessed | tf_op | source)
XLA Modules:
  0.0 69.1 jit_solution(13904669475211887342)
XLA Ops:
  0.0 0.0 copy-start
  0.0 0.0 copy-start.5
  0.0 1.4 %collective-permute-start = (bf16[3,3,128,256]{3,2,1,0:T(8,128)(2,1)}, bf16[3,3,128,256]{3,2,1,0:T(8,128)(2,1)S(1)}, u32[]{:S(2)}, u32[]{:S(2)}) collective-permute-start(bf16[3,3,128,256]{3,2,1,0:T(8,128)(2,1)} %own_ref.3), channel_id=1, source_target_pairs={{0,8},{8,0},{16,24},{24,16},{32,40},{40,32},{48,56},{56,48},{64,72... | collective-permute-start | bytes 1769480 | tf_op jit(solution)/shard_map/ppermute | solution.py:328
  1.4 0.0 collective-permute-start.1
  1.4 2.2 %edges.1 = bf16[8,384,128]{2,1,0:T(8,128)(2,1)} custom-call(s32[2]{0:T(128)} %index_ref.5, bf16[3,3,128,256]{3,2,1,0:T(8,128)(2,1)} %own_ref.3, bf16[64,256]{1,0:T(8,128)(2,1)} %constant.22.clone.pick_ref), custom_call_target="tpu_custom_call" | custom-call | tf_op jit(solution)/shard_map/edges/pallas_call | solution.py:330
  3.7 0.0 collective-permute-done.1.halo_other_ref.halo_rows_other_ref
  3.7 0.0 collective-permute-done.other_ref
  3.7 7.7 %all-to-all-start = ((bf16[8,384,128]{2,1,0:T(8,128)(2,1)}), bf16[8,384,128]{2,1,0:T(8,128)(2,1)S(1)}, u32[]{:S(2)}, u32[]{:S(2)}) async-start(bf16[8,384,128]{2,1,0:T(8,128)(2,1)} %edges.1), calls=%async_computation | async-start | bytes 1572864 | tf_op jit(solution)/shard_map/all_to_all | solution.py:340
  11.3 0.1 pad_add_fusion.core_ref.place_ref
  11.4 0.0 copy-done
  11.4 0.0 copy-done.5
  11.4 0.0 copy-start.3
  11.4 0.0 copy-start.4
  11.4 10.5 %inner.1 = (f32[5,1152,128]{2,1,0:T(8,128)}, f32[8,128]{1,0:T(8,128)S(1)}) custom-call(s32[3]{0:T(128)S(1)} %pad_add_fusion.core_ref.place_ref, s32[2]{0:T(128)S(1)} %copy-done.5, bf16[3,3,128,256]{3,2,1,0:T(8,128)(2,1)S(1)} %copy-done, bf16[3,3,128,256]{3,2,1,0:T(8,128)(2,1)S(1)} %collective-permute-done.other_ref), custom_call_target="tpu_custom_call" | custom-call | flops 6000000000 | bytes 5000000 | tf_op jit(solution)/shard_map/inner/pallas_call | solution.py:345
  21.9 0.0 copy-start.2
  22.0 2.4 %all-to-all-done.table_ref = bf16[8,384,128]{2,1,0:T(8,128)(2,1)S(1)} async-done(((bf16[8,384,128]{2,1,0:T(8,128)(2,1)}), bf16[8,384,128]{2,1,0:T(8,128)(2,1)S(1)}, u32[]{:S(2)}, u32[]{:S(2)}) %all-to-all-start) | async-done | bytes 786464 | tf_op jit(solution)/shard_map/all_to_all | solution.py:340
  24.3 0.0 copy-done.3
  24.3 1.7 %gather.1.tiles_own_ref = bf16[1536,128]{1,0:T(8,128)(2,1)S(1)} custom-call(s32[3]{0:T(128)S(1)} %pad_add_fusion.core_ref.place_ref, s32[3,68]{1,0:T(4,128)S(1)} %copy-done.3, s32[3,68]{1,0:T(4,128)S(1)} %collective-permute-done.1.halo_other_ref.halo_rows_other_ref, bf16[8,384,128]{2,1,0:T(8,128)(2,1)S(1)} %all-to-all-done.table_ref, ...), custom_call_target="tpu_custom_call" | custom-call | tf_op jit(solution)/shard_map/gather/pallas_call | solution.py:360
  26.1 1.4 %collective-permute-start.2 = (bf16[1536,128]{1,0:T(8,128)(2,1)S(1)}, bf16[1536,128]{1,0:T(8,128)(2,1)S(1)}, u32[]{:S(2)}, u32[]{:S(2)}) collective-permute-start(bf16[1536,128]{1,0:T(8,128)(2,1)S(1)} %gather.1.tiles_own_ref), channel_id=1, source_target_pairs={{0,8},{8,0},{16,24},{24,16},{32,40},{40,32},{48,56},{56,48},{64,72... | collective-permute-start | bytes 1179656 | tf_op jit(solution)/shard_map/ppermute | solution.py:368
  27.4 1.3 %collective-permute-done.2.tiles_other_ref = bf16[1536,128]{1,0:T(8,128)(2,1)S(1)} collective-permute-done((bf16[1536,128]{1,0:T(8,128)(2,1)S(1)}, bf16[1536,128]{1,0:T(8,128)(2,1)S(1)}, u32[]{:S(2)}, u32[]{:S(2)}) %collective-permute-start.2) | collective-permute-done | bytes 393248 | tf_op jit(solution)/shard_map/ppermute | solution.py:368
  28.8 0.0 copy-done.4
  28.8 0.0 copy-done.2
  28.8 5.6 %outer.1 = s16[64,88,128]{2,1,0:T(8,128)(2,1)S(1)} custom-call(s32[3]{0:T(128)S(1)} %pad_add_fusion.core_ref.place_ref, s32[2]{0:T(128)S(1)} %copy-done.5, bf16[3,3,128,256]{3,2,1,0:T(8,128)(2,1)S(1)} %copy-done, bf16[3,3,128,256]{3,2,1,0:T(8,128)(2,1)S(1)} %collective-permute-done.other_ref, bf16[1536,128]{1,0:T(8,128)(2,1)S(1)} %gather.1.tiles_own_ref, ...), custom_call_target="tpu_custom_call" | custom-call | tf_op jit(solution)/shard_map/outer/pallas_call | solution.py:370
  34.3 30.0 %all_to_all.10.landed_ref = s16[64,88,128]{2,1,0:T(8,128)(2,1)S(1)} all-to-all(s16[64,88,128]{2,1,0:T(8,128)(2,1)S(1)} %outer.1), channel_id=1, replica_groups={{0,1,2,3,4,5,6,7,16,17,18,19,20,21,22,23,32,33,34,35,36,37,38,39,48,49,..., dimensions={0} | all-to-all | bytes 2883584 | tf_op jit(solution)/shard_map/all_to_all | solution.py:401
  64.4 0.0 copy-start.1
  64.4 0.7 total.1.near_ref
  65.0 1.7 %collective-permute-start.3 = (f32[88,128]{1,0:T(8,128)S(1)}, f32[88,128]{1,0:T(8,128)S(1)}, u32[]{:S(2)}, u32[]{:S(2)}) collective-permute-start(f32[88,128]{1,0:T(8,128)S(1)} %total.1.near_ref), channel_id=1, source_target_pairs={{0,8},{8,0},{16,24},{24,16},{32,40},{40,32},{48,56},{56,48},{64,72... | collective-permute-start | bytes 135176 | tf_op jit(solution)/shard_map/ppermute | solution.py:410
  66.8 0.9 %collective-permute-done.3.far_ref = f32[88,128]{1,0:T(8,128)S(1)} collective-permute-done((f32[88,128]{1,0:T(8,128)S(1)}, f32[88,128]{1,0:T(8,128)S(1)}, u32[]{:S(2)}, u32[]{:S(2)}) %collective-permute-start.3) | collective-permute-done | bytes 45088 | tf_op jit(solution)/shard_map/ppermute | solution.py:410
  67.7 0.0 copy-done.1
  67.7 1.5 %rows.1 = f32[9,1408]{1,0:T(8,128)} custom-call(s32[3]{0:T(128)S(1)} %pad_add_fusion.core_ref.place_ref, s32[128]{0:T(128)S(1)} %copy-done.4, f32[88,128]{1,0:T(8,128)S(1)} %total.1.near_ref, f32[88,128]{1,0:T(8,128)S(1)} %collective-permute-done.3.far_ref, bf16[1152,256]{1,0:T(8,128)(2,1)S(1)} %copy-done.1, s32[1,128]{1,0:T(1,128)S(1)} %bitcast.4), custom_call_target="tpu_custom_call" | custom-call | tf_op jit(solution)/shard_map/rows/pallas_call | solution.py:412
Async XLA Ops:
  0.0 11.4 %copy-start = (bf16[3,3,128,256]{3,2,1,0:T(8,128)(2,1)S(1)}, bf16[3,3,128,256]{3,2,1,0:T(8,128)(2,1)}, u32[]{:S(2)}) copy-start(bf16[3,3,128,256]{3,2,1,0:T(8,128)(2,1)} %own_ref.3) | copy-start | bytes 1769476
  0.0 11.4 %copy-start.5 = (s32[2]{0:T(128)S(1)}, s32[2]{0:T(128)}, u32[]{:S(2)}) copy-start(s32[2]{0:T(128)} %index_ref.5) | copy-start | bytes 28
  0.0 3.7 %collective-permute-start = (bf16[3,3,128,256]{3,2,1,0:T(8,128)(2,1)}, bf16[3,3,128,256]{3,2,1,0:T(8,128)(2,1)S(1)}, u32[]{:S(2)}, u32[]{:S(2)}) collective-permute-start(bf16[3,3,128,256]{3,2,1,0:T(8,128)(2,1)} %own_ref.3), channel_id=1, source_target_pairs={{0,8},{8,0},{16,24},{24,16},{32,40},{40,32},{48,56},{56,48},{64,72... | collective-permute-start | bytes 1769480 | tf_op jit(solution)/shard_map/ppermute | solution.py:328
  1.4 2.2 %collective-permute-start.1 = (s32[3,68]{1,0:T(4,128)}, s32[3,68]{1,0:T(4,128)S(1)}, u32[]{:S(2)}, u32[]{:S(2)}) collective-permute-start(s32[3,68]{1,0:T(4,128)} %halo_rows_own_ref.1), channel_id=1, source_target_pairs={{0,8},{8,0},{16,24},{24,16},{32,40},{40,32},{48,56},{56,48},{64,72... | collective-permute-start | bytes 2456 | tf_op jit(solution)/shard_map/ppermute | solution.py:329
  3.7 20.6 %all-to-all-start = ((bf16[8,384,128]{2,1,0:T(8,128)(2,1)}), bf16[8,384,128]{2,1,0:T(8,128)(2,1)S(1)}, u32[]{:S(2)}, u32[]{:S(2)}) async-start(bf16[8,384,128]{2,1,0:T(8,128)(2,1)} %edges.1), calls=%async_computation | async-start | bytes 1572864 | tf_op jit(solution)/shard_map/all_to_all | solution.py:340
  11.4 12.9 %copy-start.3 = (s32[3,68]{1,0:T(4,128)S(1)}, s32[3,68]{1,0:T(4,128)}, u32[]{:S(2)}) copy-start(s32[3,68]{1,0:T(4,128)} %halo_rows_own_ref.1) | copy-start | bytes 2452
  11.4 17.4 %copy-start.4 = (s32[128]{0:T(128)S(1)}, s32[128]{0:T(128)}, u32[]{:S(2)}) copy-start(s32[128]{0:T(128)} %mask_ref.1) | copy-start | bytes 1540
  21.9 6.8 %copy-start.2 = (bf16[384,640]{1,0:T(8,128)(2,1)S(1)}, bf16[384,640]{1,0:T(8,128)(2,1)}, u32[]{:S(2)}) copy-start(bf16[384,640]{1,0:T(8,128)(2,1)} %constant.23.clone.taps_ref) | copy-start | bytes 1474564
  26.1 2.7 %collective-permute-start.2 = (bf16[1536,128]{1,0:T(8,128)(2,1)S(1)}, bf16[1536,128]{1,0:T(8,128)(2,1)S(1)}, u32[]{:S(2)}, u32[]{:S(2)}) collective-permute-start(bf16[1536,128]{1,0:T(8,128)(2,1)S(1)} %gather.1.tiles_own_ref), channel_id=1, source_target_pairs={{0,8},{8,0},{16,24},{24,16},{32,40},{40,32},{48,56},{56,48},{64,72... | collective-permute-start | bytes 1179656 | tf_op jit(solution)/shard_map/ppermute | solution.py:368
  64.4 3.3 %copy-start.1 = (bf16[1152,256]{1,0:T(8,128)(2,1)S(1)}, bf16[1152,256]{1,0:T(8,128)(2,1)}, u32[]{:S(2)}) copy-start(bf16[1152,256]{1,0:T(8,128)(2,1)} %weight_ref.1) | copy-start | bytes 1769476
  65.0 2.6 %collective-permute-start.3 = (f32[88,128]{1,0:T(8,128)S(1)}, f32[88,128]{1,0:T(8,128)S(1)}, u32[]{:S(2)}, u32[]{:S(2)}) collective-permute-start(f32[88,128]{1,0:T(8,128)S(1)} %total.1.near_ref), channel_id=1, source_target_pairs={{0,8},{8,0},{16,24},{24,16},{32,40},{40,32},{48,56},{56,48},{64,72... | collective-permute-start | bytes 135176 | tf_op jit(solution)/shard_map/ppermute | solution.py:410

commit v5 on v4

--- a/solution.py
+++ b/solution.py
@@ -72,11 +72,20 @@
                 copies_ref[d, u * 4 * SIDE : (u + 1) * 4 * SIDE, :] = edges
 
 
-def row_blocks():
-    return [slice(t * CH, (t + 3) * CH) for t in range(0, TAPS, 3)]
-
-
-def inner_kernel(core_ref, index_ref, own_ref, other_ref, gram_ref, done_ref, patches, gram, sems):
+def owned_rows(core, patches, owned):
+    for c in range(2):
+
+        @pl.when(core == c)
+        def _():
+            for g in range(K // 144):
+                owned[g * 72 : (g + 1) * 72, :] = patches[g * 144 + c * 72 : g * 144 + c * 72 + 72, :]
+
+
+def tap_blocks():
+    return [slice(t, t + 3) for t in range(0, TAPS, 3)]
+
+
+def inner_kernel(core_ref, index_ref, own_ref, other_ref, gram_ref, done_ref, patches, owned, gram, sems):
     subs = own_ref.shape[1]
     done_ref[...] = jnp.zeros_like(done_ref)
     pixel = lax.broadcasted_iota(jnp.int32, (PIX, PIX), 1)
@@ -95,15 +104,14 @@
                 for f in range(subs):
                     u = (n * 2 + s) * subs + f
                     patches[t * CH : (t + 1) * CH, u * PIX : (u + 1) * PIX] = values[f * CH : (f + 1) * CH, :]
-    right = patches[pl.ds(pl.multiple_of(core_ref[0] * HALF, HALF), HALF), :]
+    owned_rows(core_ref[0], patches, owned)
     copies = []
-    for n, rows in enumerate(row_blocks()):
-        block = lax.dot_general(patches[rows, :], right, NT, preferred_element_type=jnp.float32)
-        for l in range(4):
-            gram[l, rows, :] = block[:, l * CH : (l + 1) * CH]
-        gram[4, rows, : CH // 2] = block[:, 4 * CH :]
-        gram[4, rows, CH // 2 :] = jnp.zeros((3 * CH, CH // 2), jnp.float32)
-        copies.append(pltpu.make_async_copy(gram.at[:, rows, :], gram_ref.at[:, rows, :], sems.at[n]))
+    for n, taps in enumerate(tap_blocks()):
+        right = patches[taps.start * CH : taps.stop * CH, :]
+        block = lax.dot_general(owned[...], right, NT, preferred_element_type=jnp.float32)
+        for l in range(3):
+            gram[taps.start + l, :, :] = block[:, l * CH : (l + 1) * CH]
+        copies.append(pltpu.make_async_copy(gram.at[taps], gram_ref.at[taps], sems.at[n]))
         copies[-1].start()
     for copy in copies:
         copy.wait()
@@ -143,6 +151,7 @@
     message_ref,
     grid,
     patches,
+    owned,
     gram,
     position,
     stage,
@@ -153,8 +162,8 @@
     units = 4 * subs
     half = units // 2
     copies = []
-    for n, rows in enumerate(row_blocks()):
-        copies.append(pltpu.make_async_copy(inner_ref.at[:, rows, :], inner.at[:, rows, :], sems.at[n]))
+    for n, taps in enumerate(tap_blocks()):
+        copies.append(pltpu.make_async_copy(inner_ref.at[taps], inner.at[taps], sems.at[n]))
         copies[-1].start()
 
     lane = lax.broadcasted_iota(jnp.int32, (8, CH), 1)
@@ -191,12 +200,6 @@
         energy += x[:, :CH] * x[:, :CH] + x[:, CH:] * x[:, CH:] + cycle * cycle
     kept = mask_ref[...].astype(jnp.float32)
     kept_row = jnp.sum(jnp.where(diagonal, kept, 0.0), axis=1, keepdims=True)
-    turned_kept = pltpu.roll(jnp.broadcast_to(kept, (8, CH)), CH // 2, 1)
-    kept = jnp.broadcast_to(kept, (8, CH))
-    first, second = jnp.where(core == 0, kept, turned_kept), jnp.where(core == 0, turned_kept, kept)
-    folded = jnp.where(lane < CH // 2, first, second)
-    kept_lane = jnp.where(lax.broadcasted_iota(jnp.int32, (8, CH), 0) == 0, first, folded)
-
     energy = jnp.sum(energy, axis=1, keepdims=True)
 
     def exponent(values):
@@ -205,9 +208,8 @@
 
     kept_exp = exponent(jnp.where(kept_row > 0, energy, 0.0))
     any_exp = exponent(energy)
-    row_scale = jnp.where(kept_row > 0, jnp.exp2(kept_exp[0:1, :] * (-1 / STEPS)), 0.0)
-    lane_exps = jnp.where(kept_lane > 0, kept_exp, any_exp)
-    lane_scale = jnp.exp2(lane_exps * (-1 / STEPS))
+    lane_exps = jnp.where(kept > 0, kept_exp, any_exp) + kept_exp
+    scale = jnp.exp2(lane_exps * (-1 / STEPS))
 
     def coded(values):
         return jnp.round(TOP * values * lax.rsqrt(jnp.maximum(jnp.abs(values), 1e-30)))
@@ -222,64 +224,34 @@
                 part = values[n * CH : (n + 1) * CH, t * RIM : (t + 1) * RIM]
                 patches[t * CH : (t + 1) * CH, u * RIM : (u + 1) * RIM] = part
 
-    right = patches[pl.ds(pl.multiple_of(core * HALF, HALF), HALF), :]
-    for t in range(0, TAPS, 3):
-        block = lax.dot_general(
-            patches[t * CH : (t + 3) * CH, :], right, NT, preferred_element_type=jnp.float32
-        )
-        copies[t // 3].wait()
-        for n in range(3):
-            rows = block[n * CH : (n + 1) * CH, :]
-            at = slice((t + n) * CH, (t + n + 1) * CH)
-            for l in range(4):
-                part = rows[:, l * CH : (l + 1) * CH] + inner[l, at, :]
-                gram[l, at, :] = coded(part * row_scale * lane_scale[0:1, :])
-            part = rows[:, 4 * CH :] + inner[4, at, : CH // 2]
-            gram[4, at, : CH // 2] = coded(part * row_scale[:, : CH // 2] * lane_scale[1:2, : CH // 2])
-
-    for j in range(64):
-        at = j // 8 * 144 + j % 8 * 9
+    owned_rows(core, patches, owned)
+    for n, taps in enumerate(tap_blocks()):
+        right = patches[taps.start * CH : taps.stop * CH, :]
+        block = lax.dot_general(owned[...], right, NT, preferred_element_type=jnp.float32)
+        copies[n].wait()
+        for l in range(3):
+            part = block[:, l * CH : (l + 1) * CH] + inner[taps.start + l, :, :]
+            gram[taps.start + l, :, :] = coded(part * scale[0:1, :])
+
+    for j in range(message_ref.shape[0]):
         block = stage.at[j % 4]
-        for c in range(2):
-            rows = slice(at + c * 72, at + c * 72 + 9)
-            for l in range(4):
-                to = (c * 4 + l) * 9
-                block[to : to + 9, :] = gram[l, rows, :]
-            block[72:81, c * 64 : (c + 1) * 64] = gram[4, rows, : CH // 2]
-        block[81:88, :] = (lane_exps + kept_exp)[0:7, :]
+        for l in range(TAPS):
+            block[l * 9 : (l + 1) * 9, :] = gram[l, j * 9 : (j + 1) * 9, :]
+        block[81:88, :] = lane_exps[0:7, :]
         message_ref[j] = block[...].astype(jnp.int32).astype(jnp.int16)
 
 
-def sum_kernel(landed_ref, sum_ref):
-    whole = jnp.zeros((72, CH), jnp.float32)
-    folded = jnp.zeros((ROWS - 72, CH), jnp.float32)
+def rows_kernel(place_ref, mask_ref, landed_ref, weight_ref, kept_ref, out_ref, rows, split):
+    owner = place_ref[1]
+    total = jnp.zeros((ROWS, CH), jnp.float32)
     for j in range(landed_ref.shape[0]):
         codes = landed_ref[j].astype(jnp.int32).astype(jnp.float32)
         scale = jnp.exp2(codes[80:88, :] * (1 / STEPS))
-        whole += codes[:72, :] * jnp.abs(codes[:72, :]) * scale[1:2, :]
-        folded += codes[72:, :] * jnp.abs(codes[72:, :]) * scale[2:3, :]
-    sum_ref[:72, :] = whole * TOP**-2
-    sum_ref[72:, :] = folded * TOP**-2
-
-
-def rows_kernel(place_ref, mask_ref, near_ref, far_ref, weight_ref, kept_ref, out_ref, rows, split):
-    core, owner = place_ref[0], place_ref[1]
-    near, far = near_ref[...], far_ref[...]
-    low = jnp.where(core == 0, near, far)
-    high = jnp.where(core == 0, far, near)
-
-    def mine(values, l):
-        return jnp.where(core == 0, values[l * 9 : l * 9 + 9, :], values[(4 + l) * 9 : (4 + l) * 9 + 9, :])
-
-    def middle(values):
-        return jnp.where(core == 0, values[72:81, : CH // 2], values[72:81, CH // 2 :])
-
+        total += codes * jnp.abs(codes) * scale[1:2, :]
+    total = total * TOP**-2
     rows[...] = jnp.zeros_like(rows)
-    for l in range(4):
-        rows[0:9, l * CH : (l + 1) * CH] = mine(low, l)
-        rows[0:9, HALF + l * CH : HALF + (l + 1) * CH] = mine(high, l)
-    rows[0:9, 4 * CH : HALF] = middle(low)
-    rows[0:9, HALF + 4 * CH :] = middle(high)
+    for l in range(TAPS):
+        rows[0:9, l * CH : (l + 1) * CH] = total[l * 9 : (l + 1) * 9, :]
 
     at = lax.broadcasted_iota(jnp.int32, (16, CH), 0)
     keep = jnp.zeros((16, CH), jnp.float32)
@@ -344,12 +316,13 @@
 
     inner, done = pl.pallas_call(
         inner_kernel,
-        out_shape=(pltpu.HBM((5, K, CH), f32), shape((8, CH), f32)),
+        out_shape=(pltpu.HBM((TAPS, HALF, CH), f32), shape((8, CH), f32)),
         in_specs=[SMEM] * 2 + [VMEM] * 2,
         out_specs=(HBM, VMEM),
         scratch_shapes=[
             pltpu.VMEM((K, units * PIX), bf16),
-            pltpu.VMEM((5, K, CH), f32),
+            pltpu.VMEM((HALF, units * PIX), bf16),
+            pltpu.VMEM((TAPS, HALF, CH), f32),
             pltpu.SemaphoreType.DMA((3,)),
         ],
         compiler_params=pltpu.CompilerParams(vmem_limit_bytes=28 * 2**20),
@@ -375,10 +348,11 @@
         scratch_shapes=[
             pltpu.VMEM((units * CH, PIX + CH), bf16),
             pltpu.VMEM((K, units * RIM), bf16),
-            pltpu.VMEM((5, K, CH), f32),
+            pltpu.VMEM((HALF, units * RIM), bf16),
+            pltpu.VMEM((TAPS, HALF, CH), f32),
             pltpu.VMEM((8, CH), jnp.int32),
             pltpu.VMEM((4, ROWS, CH), f32),
-            pltpu.VMEM((5, K, CH), f32),
+            pltpu.VMEM((TAPS, HALF, CH), f32),
             pltpu.SemaphoreType.DMA((3,)),
         ],
         compiler_params=pltpu.CompilerParams(vmem_limit_bytes=28 * 2**20),
@@ -399,25 +373,15 @@
 
     groups = [[f * samples + s for f in range(c, faces, 2) for s in range(samples)] for c in range(2)]
     landed = lax.all_to_all(message, AXES, 0, 0, axis_index_groups=groups)
-    near = pl.pallas_call(
-        sum_kernel,
-        out_shape=shape((ROWS, CH), f32),
-        in_specs=[VMEM],
-        out_specs=VMEM,
-        compiler_params=pltpu.CompilerParams(vmem_limit_bytes=8 * 2**20),
-        name="total",
-    )(landed)
-    far = lax.ppermute(near, "face", swap)
-
     return pl.pallas_call(
         rows_kernel,
         out_shape=shape((TAPS, K + weight.shape[1]), f32),
-        in_specs=[SMEM] * 2 + [VMEM] * 4,
+        in_specs=[SMEM] * 2 + [VMEM] * 3,
         out_specs=VMEM,
         scratch_shapes=[pltpu.VMEM((16, K), f32), pltpu.VMEM((48, K), bf16)],
         compiler_params=pltpu.CompilerParams(vmem_limit_bytes=8 * 2**20),
         name="rows",
-    )(place, channel_mask, near, far, weight, mask_row)
+    )(place, channel_mask, landed, weight, mask_row)
 
 
 def solution(mesh):

time: 69.4 us -> 66.4 us (0.957)
  starting transfers between devices: 12.2 us -> 10.3 us
  Pallas kernels: 22.1 us -> 21 us
    ppermute x1 -> x0, starting transfers between devices: 1.74 us -> none  [per_device(): far = lax.ppermute(near, 'face', swap)]
    pallas_call x2 -> x1, Pallas kernels: 11.1 us -> 9.43 us  [per_device(): pl.pallas_call(inner_kernel, out_shape=(pltpu.HBM((TAPS, HALF, CH), f32),...]
    all_to_all x1, waiting for transfers between devices: 2.36 us -> 3.42 us  [per_device(): table = lax.all_to_all(copies, 'face', 0, 0, axis_index_groups=same_core)]
    ppermute x1 -> x0, waiting for transfers between devices: 0.88 us -> none  [per_device(): far = lax.ppermute(near, 'face', swap)]
  transfers between devices with their start and end apart: 5 -> 4, of which waited for: 3 -> 2; matrix products, arithmetic and copies ran while one was open for 0% -> 0% of each run, Pallas kernels for 18% -> 18%
where the time goes in v5:
time: 66.4 us; the launch traced here: 66.1 us
  blocking collectives  29.9 us (45%)
  Pallas kernels  21 us (32%)
  starting transfers between devices  10.3 us (16%)
  waiting for transfers between devices  4.77 us (7%)
    all_to_all x1, blocking collectives, per_device(): landed = lax.all_to_all(message, AXES, 0, 0, axis_index_groups=groups)  29.9 us
    pallas_call x1, Pallas kernels, per_device(): pl.pallas_call(inner_kernel, out_shape=(pltpu.HBM((TAPS, HALF, CH), f32),...  9.43 us
    all_to_all x1, starting transfers between devices, per_device(): table = lax.all_to_all(copies, 'face', 0, 0, axis_index_groups=same_core)  7.68 us
    pallas_call x1, Pallas kernels, per_device(): pl.pallas_call(functools.partial(outer_kernel, subs), out_shape=shape((64...  5.59 us
    all_to_all x1, waiting for transfers between devices, per_device(): table = lax.all_to_all(copies, 'face', 0, 0, axis_index_groups=same_core)  3.42 us
    pallas_call x1, Pallas kernels, per_device(): pl.pallas_call(edges_kernel, out_shape=shape((faces // 2, 8 * subs * SIDE...  2.22 us
    pallas_call x1, Pallas kernels, per_device(): pl.pallas_call(rows_kernel, out_shape=shape((TAPS, K + weight.shape[1]),...  1.97 us
    pallas_call x1, Pallas kernels, per_device(): pl.pallas_call(functools.partial(gather_kernel, subs), out_shape=shape((u...  1.74 us
  transfers between devices with their start and end apart: 4, of which 2 were waited for; matrix products, arithmetic and copies ran while one was open for 0% of the time, Pallas kernels for 18%

profile of v5, /device:TPU:1, one launch (start us, length us, event | category | flops | bytes accessed | tf_op | source)
XLA Modules:
  0.0 66.1 jit_solution(17719118436549671847)
XLA Ops:
  0.0 0.0 copy-start
  0.0 0.0 copy-start.5
  0.0 1.4 %collective-permute-start = (bf16[3,3,128,256]{3,2,1,0:T(8,128)(2,1)}, bf16[3,3,128,256]{3,2,1,0:T(8,128)(2,1)S(1)}, u32[]{:S(2)}, u32[]{:S(2)}) collective-permute-start(bf16[3,3,128,256]{3,2,1,0:T(8,128)(2,1)} %own_ref.3), channel_id=1, source_target_pairs={{0,8},{8,0},{16,24},{24,16},{32,40},{40,32},{48,56},{56,48},{64,72... | collective-permute-start | bytes 1769480 | tf_op jit(solution)/shard_map/ppermute | solution.py:300
  1.4 0.0 collective-permute-start.1
  1.4 2.2 %edges.1 = bf16[8,384,128]{2,1,0:T(8,128)(2,1)} custom-call(s32[2]{0:T(128)} %index_ref.5, bf16[3,3,128,256]{3,2,1,0:T(8,128)(2,1)} %own_ref.3, bf16[64,256]{1,0:T(8,128)(2,1)} %constant.22.clone.pick_ref), custom_call_target="tpu_custom_call" | custom-call | tf_op jit(solution)/shard_map/edges/pallas_call | solution.py:302
  3.7 0.0 collective-permute-done.1.halo_other_ref.halo_rows_other_ref
  3.7 0.0 collective-permute-done.other_ref
  3.7 7.7 %all-to-all-start = ((bf16[8,384,128]{2,1,0:T(8,128)(2,1)}), bf16[8,384,128]{2,1,0:T(8,128)(2,1)S(1)}, u32[]{:S(2)}, u32[]{:S(2)}) async-start(bf16[8,384,128]{2,1,0:T(8,128)(2,1)} %edges.1), calls=%async_computation | async-start | bytes 1572864 | tf_op jit(solution)/shard_map/all_to_all | solution.py:312
  11.3 0.1 pad_add_fusion.core_ref.place_ref
  11.4 0.0 copy-done
  11.4 0.0 copy-done.5
  11.4 0.0 copy-start.3
  11.4 0.0 copy-start.4
  11.4 9.4 %inner.1 = (f32[9,576,128]{2,1,0:T(8,128)}, f32[8,128]{1,0:T(8,128)S(1)}) custom-call(s32[3]{0:T(128)S(1)} %pad_add_fusion.core_ref.place_ref, s32[2]{0:T(128)S(1)} %copy-done.5, bf16[3,3,128,256]{3,2,1,0:T(8,128)(2,1)S(1)} %copy-done, bf16[3,3,128,256]{3,2,1,0:T(8,128)(2,1)S(1)} %collective-permute-done.other_ref), custom_call_target="tpu_custom_call" | custom-call | flops 6000000000 | bytes 5000000 | tf_op jit(solution)/shard_map/inner/pallas_call | solution.py:317
  20.9 0.0 copy-start.2
  20.9 3.4 %all-to-all-done.table_ref = bf16[8,384,128]{2,1,0:T(8,128)(2,1)S(1)} async-done(((bf16[8,384,128]{2,1,0:T(8,128)(2,1)}), bf16[8,384,128]{2,1,0:T(8,128)(2,1)S(1)}, u32[]{:S(2)}, u32[]{:S(2)}) %all-to-all-start) | async-done | bytes 786464 | tf_op jit(solution)/shard_map/all_to_all | solution.py:312
  24.3 0.0 copy-done.3
  24.3 1.7 %gather.1.tiles_own_ref = bf16[1536,128]{1,0:T(8,128)(2,1)S(1)} custom-call(s32[3]{0:T(128)S(1)} %pad_add_fusion.core_ref.place_ref, s32[3,68]{1,0:T(4,128)S(1)} %copy-done.3, s32[3,68]{1,0:T(4,128)S(1)} %collective-permute-done.1.halo_other_ref.halo_rows_other_ref, bf16[8,384,128]{2,1,0:T(8,128)(2,1)S(1)} %all-to-all-done.table_ref, ...), custom_call_target="tpu_custom_call" | custom-call | tf_op jit(solution)/shard_map/gather/pallas_call | solution.py:333
  26.1 1.2 %collective-permute-start.2 = (bf16[1536,128]{1,0:T(8,128)(2,1)S(1)}, bf16[1536,128]{1,0:T(8,128)(2,1)S(1)}, u32[]{:S(2)}, u32[]{:S(2)}) collective-permute-start(bf16[1536,128]{1,0:T(8,128)(2,1)S(1)} %gather.1.tiles_own_ref), channel_id=1, source_target_pairs={{0,8},{8,0},{16,24},{24,16},{32,40},{40,32},{48,56},{56,48},{64,72... | collective-permute-start | bytes 1179656 | tf_op jit(solution)/shard_map/ppermute | solution.py:341
  27.2 1.3 %collective-permute-done.2.tiles_other_ref = bf16[1536,128]{1,0:T(8,128)(2,1)S(1)} collective-permute-done((bf16[1536,128]{1,0:T(8,128)(2,1)S(1)}, bf16[1536,128]{1,0:T(8,128)(2,1)S(1)}, u32[]{:S(2)}, u32[]{:S(2)}) %collective-permute-start.2) | collective-permute-done | bytes 393248 | tf_op jit(solution)/shard_map/ppermute | solution.py:341
  28.6 0.0 copy-done.4
  28.6 0.0 copy-done.2
  28.6 5.6 %outer.1 = s16[64,88,128]{2,1,0:T(8,128)(2,1)S(1)} custom-call(s32[3]{0:T(128)S(1)} %pad_add_fusion.core_ref.place_ref, s32[2]{0:T(128)S(1)} %copy-done.5, bf16[3,3,128,256]{3,2,1,0:T(8,128)(2,1)S(1)} %copy-done, bf16[3,3,128,256]{3,2,1,0:T(8,128)(2,1)S(1)} %collective-permute-done.other_ref, bf16[1536,128]{1,0:T(8,128)(2,1)S(1)} %gather.1.tiles_own_ref, ...), custom_call_target="tpu_custom_call" | custom-call | tf_op jit(solution)/shard_map/outer/pallas_call | solution.py:343
  34.2 0.0 copy-start.1
  34.2 29.9 %all_to_all.10.landed_ref = s16[64,88,128]{2,1,0:T(8,128)(2,1)S(1)} all-to-all(s16[64,88,128]{2,1,0:T(8,128)(2,1)S(1)} %outer.1), channel_id=1, replica_groups={{0,1,2,3,4,5,6,7,16,17,18,19,20,21,22,23,32,33,34,35,36,37,38,39,48,49,..., dimensions={0} | all-to-all | bytes 2883584 | tf_op jit(solution)/shard_map/all_to_all | solution.py:375
  64.1 0.0 copy-done.1
  64.1 2.0 %rows.1 = f32[9,1408]{1,0:T(8,128)} custom-call(s32[3]{0:T(128)S(1)} %pad_add_fusion.core_ref.place_ref, s32[128]{0:T(128)S(1)} %copy-done.4, s16[64,88,128]{2,1,0:T(8,128)(2,1)S(1)} %all_to_all.10.landed_ref, bf16[1152,256]{1,0:T(8,128)(2,1)S(1)} %copy-done.1, s32[1,128]{1,0:T(1,128)S(1)} %bitcast.4), custom_call_target="tpu_custom_call" | custom-call | tf_op jit(solution)/shard_map/rows/pallas_call | solution.py:376
Async XLA Ops:
  0.0 11.4 %copy-start = (bf16[3,3,128,256]{3,2,1,0:T(8,128)(2,1)S(1)}, bf16[3,3,128,256]{3,2,1,0:T(8,128)(2,1)}, u32[]{:S(2)}) copy-start(bf16[3,3,128,256]{3,2,1,0:T(8,128)(2,1)} %own_ref.3) | copy-start | bytes 1769476
  0.0 11.4 %copy-start.5 = (s32[2]{0:T(128)S(1)}, s32[2]{0:T(128)}, u32[]{:S(2)}) copy-start(s32[2]{0:T(128)} %index_ref.5) | copy-start | bytes 28
  0.0 3.7 %collective-permute-start = (bf16[3,3,128,256]{3,2,1,0:T(8,128)(2,1)}, bf16[3,3,128,256]{3,2,1,0:T(8,128)(2,1)S(1)}, u32[]{:S(2)}, u32[]{:S(2)}) collective-permute-start(bf16[3,3,128,256]{3,2,1,0:T(8,128)(2,1)} %own_ref.3), channel_id=1, source_target_pairs={{0,8},{8,0},{16,24},{24,16},{32,40},{40,32},{48,56},{56,48},{64,72... | collective-permute-start | bytes 1769480 | tf_op jit(solution)/shard_map/ppermute | solution.py:300
  1.4 2.2 %collective-permute-start.1 = (s32[3,68]{1,0:T(4,128)}, s32[3,68]{1,0:T(4,128)S(1)}, u32[]{:S(2)}, u32[]{:S(2)}) collective-permute-start(s32[3,68]{1,0:T(4,128)} %halo_rows_own_ref.1), channel_id=1, source_target_pairs={{0,8},{8,0},{16,24},{24,16},{32,40},{40,32},{48,56},{56,48},{64,72... | collective-permute-start | bytes 2456 | tf_op jit(solution)/shard_map/ppermute | solution.py:301
  3.7 20.6 %all-to-all-start = ((bf16[8,384,128]{2,1,0:T(8,128)(2,1)}), bf16[8,384,128]{2,1,0:T(8,128)(2,1)S(1)}, u32[]{:S(2)}, u32[]{:S(2)}) async-start(bf16[8,384,128]{2,1,0:T(8,128)(2,1)} %edges.1), calls=%async_computation | async-start | bytes 1572864 | tf_op jit(solution)/shard_map/all_to_all | solution.py:312
  11.4 12.9 %copy-start.3 = (s32[3,68]{1,0:T(4,128)S(1)}, s32[3,68]{1,0:T(4,128)}, u32[]{:S(2)}) copy-start(s32[3,68]{1,0:T(4,128)} %halo_rows_own_ref.1) | copy-start | bytes 2452
  11.4 17.2 %copy-start.4 = (s32[128]{0:T(128)S(1)}, s32[128]{0:T(128)}, u32[]{:S(2)}) copy-start(s32[128]{0:T(128)} %mask_ref.1) | copy-start | bytes 1540
  20.9 7.7 %copy-start.2 = (bf16[384,640]{1,0:T(8,128)(2,1)S(1)}, bf16[384,640]{1,0:T(8,128)(2,1)}, u32[]{:S(2)}) copy-start(bf16[384,640]{1,0:T(8,128)(2,1)} %constant.23.clone.taps_ref) | copy-start | bytes 1474564
  26.1 2.5 %collective-permute-start.2 = (bf16[1536,128]{1,0:T(8,128)(2,1)S(1)}, bf16[1536,128]{1,0:T(8,128)(2,1)S(1)}, u32[]{:S(2)}, u32[]{:S(2)}) collective-permute-start(bf16[1536,128]{1,0:T(8,128)(2,1)S(1)} %gather.1.tiles_own_ref), channel_id=1, source_target_pairs={{0,8},{8,0},{16,24},{24,16},{32,40},{40,32},{48,56},{56,48},{64,72... | collective-permute-start | bytes 1179656 | tf_op jit(solution)/shard_map/ppermute | solution.py:341
  34.2 29.9 %copy-start.1 = (bf16[1152,256]{1,0:T(8,128)(2,1)S(1)}, bf16[1152,256]{1,0:T(8,128)(2,1)}, u32[]{:S(2)}) copy-start(bf16[1152,256]{1,0:T(8,128)(2,1)} %weight_ref.1) | copy-start | bytes 1769476

commit v6 on v5

v6 whole, which is shorter than its diff:
```python
import functools

import jax
import jax.numpy as jnp
import ml_dtypes
import numpy as np
from jax import lax
from jax.experimental import pallas as pl
from jax.experimental.pallas import tpu as pltpu
from jax.sharding import PartitionSpec as P

SIDE = 16
PIX = SIDE * SIDE
CH = 128
TAPS = 9
K = TAPS * CH
HALF = K // 2
CYCLE = 4 * SIDE + 4
RIM = 64
INNER = PIX - RIM
ROWS = 88
STEPS = 16
TOP = 32700.0
THIRD = 43
AXES = ("face", "sample")
NT = (((1,), (1,)), ((), ()))
SIDE_AT = (1, 19, 36, 52)
CORNER_AT = (0, 17, 18, 35)


def edge_picker():
    out = np.zeros((4 * SIDE, PIX), np.float32)
    for i in range(SIDE):
        out[i, i] = 1
        out[SIDE + i, (SIDE - 1) * SIDE + i] = 1
        out[2 * SIDE + i, i * SIDE] = 1
        out[3 * SIDE + i, i * SIDE + SIDE - 1] = 1
    return out.astype(ml_dtypes.bfloat16)


def rim_sources(tap):
    lane = lax.broadcasted_iota(jnp.int32, (8, CH), 1)
    second = lane >= RIM
    place = lax.rem(lane, RIM)
    along = lax.rem(place, SIDE)
    side = place // SIDE
    y = jnp.where(side == 0, 0, jnp.where(side == 1, SIDE - 1, along))
    x = jnp.where(side == 2, 0, jnp.where(side == 3, SIDE - 1, along))
    corner = (side >= 2) & ((along == 0) | (along == SIDE - 1))
    y = jnp.where(corner, jnp.clip(along, 1, SIDE - 2), y)
    x = jnp.where(corner, jnp.where(side == 2, 1, SIDE - 2), x)
    u, v = y + tap // 3 - 1, x + tap % 3 - 1
    inside = (u >= 0) & (u < SIDE) & (v >= 0) & (v < SIDE)
    entry = jnp.where(v < 0, 2 * SIDE + 4 + u, 3 * SIDE + 4 + u)
    entry = jnp.where(u < 0, v + 1, jnp.where(u >= SIDE, SIDE + 3 + v, entry))
    pixel = jnp.where(inside, u * SIDE + v + jnp.where(second, PIX, 0), -1)
    cycle = jnp.where(inside, -1, entry + jnp.where(second, CH, 0))
    return pixel[0:1, :], cycle[0:1, :]


def inner_pixels(place):
    rest = place - 2 * (SIDE - 4)
    row = lax.shift_right_logical(jnp.maximum(rest, 0) * 147, 11)
    y = jnp.where(place < SIDE - 4, 1, jnp.where(rest < 0, SIDE - 2, row + 2))
    x = jnp.where(place < SIDE - 4, place + 2, jnp.where(rest < 0, place - SIDE + 6, rest - row * (SIDE - 2) + 1))
    return jnp.where((place >= 0) & (place < INNER), y * SIDE + x, -PIX)


def one_hot(rows, source):
    at = lax.broadcasted_iota(jnp.int32, (rows, CH), 0)
    return jnp.where(at == source, 1.0, 0.0).astype(jnp.bfloat16)


def edges_kernel(index_ref, fields_ref, pick_ref, copies_ref):
    subs = fields_ref.shape[1]
    for s in range(2):
        for f in range(subs):
            x = fields_ref[index_ref[s], f]
            u = s * subs + f
            edges = lax.dot_general(pick_ref[...], x, NT, preferred_element_type=jnp.float32)
            edges = edges.astype(jnp.bfloat16)
            for d in range(copies_ref.shape[0]):
                copies_ref[d, u * 4 * SIDE : (u + 1) * 4 * SIDE, :] = edges


def owned_rows(core, patches, owned):
    for c in range(2):

        @pl.when(core == c)
        def _():
            for g in range(K // 144):
                owned[g * 72 : (g + 1) * 72, :] = patches[g * 144 + c * 72 : g * 144 + c * 72 + 72, :]


def tap_blocks():
    return [slice(0, 4), slice(4, 8), slice(8, TAPS)]


def core_index():
    return lax.axis_index("face") & 1


def inner_kernel(
    index_ref,
    halo_own_ref,
    halo_other_ref,
    own_ref,
    other_ref,
    gram_ref,
    pairs_ref,
    plan_ref,
    patches,
    owned,
    gram,
    sems,
):
    subs = own_ref.shape[1]
    core = core_index()

    for side, halo_ref in enumerate((halo_own_ref, halo_other_ref)):
        for f in range(subs):
            for n, at in enumerate(SIDE_AT + CORNER_AT):
                index = halo_ref[f, at]
                sub = lax.shift_right_logical(index, 6)
                device = lax.shift_right_logical(sub * THIRD, 7)
                row = (lax.shift_right_logical(device, 1) * 2 * subs + sub - device * subs) * 4 * SIDE
                row += index & (3 * SIDE)
                plan_ref[(side * subs + f) * 8 + n] = jnp.where((device & 1) == core, row, -SIDE)

    for s in range(2):
        for n, ref in enumerate((own_ref, other_ref)):
            rows = slice(s * subs * CH, (s + 1) * subs * CH)
            pairs_ref[rows, n * PIX : (n + 1) * PIX] = ref[index_ref[s]].reshape(subs * CH, PIX)

    row_at = lax.broadcasted_iota(jnp.int32, (PIX, PIX), 0)
    place = lax.broadcasted_iota(jnp.int32, (8, PIX), 1)
    ahead = [row_at - inner_pixels(place + d)[0:1, :] for d in (0, INNER - PIX)]
    for t in range(TAPS):
        shift = (t // 3 - 1) * SIDE + t % 3 - 1
        taps = [jnp.where(d == shift, 1.0, 0.0).astype(jnp.bfloat16) for d in ahead]
        for s in range(2):
            first, second = (
                jnp.dot(ref[index_ref[s]].reshape(subs * CH, PIX), tap, preferred_element_type=jnp.float32)
                for ref, tap in zip((own_ref, other_ref), taps)
            )
            columns = (first[:, :CH], first[:, CH:] + second[:, :CH], second[:, CH:])
            for n, values in enumerate(columns):
                values = values.astype(jnp.bfloat16)
                for f in range(subs):
                    at = (s * subs + f) * 2 * INNER + n * CH
                    patches[t * CH : (t + 1) * CH, at : at + CH] = values[f * CH : (f + 1) * CH, :]
    owned_rows(core, patches, owned)
    copies = []
    for n, taps in enumerate(tap_blocks()):
        right = patches[taps.start * CH : taps.stop * CH, :]
        block = lax.dot_general(owned[...], right, NT, preferred_element_type=jnp.float32)
        for l in range(taps.stop - taps.start):
            gram[taps.start + l, :, :] = block[:, l * CH : (l + 1) * CH]
        copies.append(pltpu.make_async_copy(gram.at[taps], gram_ref.at[taps], sems.at[n]))
        copies[-1].start()
    for copy in copies:
        copy.wait()


def gather_kernel(subs, plan_ref, table_ref, tiles_ref):
    zero = jnp.zeros((SIDE, CH), jnp.bfloat16)
    for f in range(2 * subs):
        for n in range(8):
            row = plan_ref[f * 8 + n]
            near = row >= 0
            row = jnp.maximum(row, 0)
            for s in range(2):
                at = pl.multiple_of(row + s * subs * 4 * SIDE, SIDE)
                u = (f // subs * 2 + s) * subs + f % subs
                tiles_ref[u * CH + n * SIDE : u * CH + (n + 1) * SIDE, :] = jnp.where(near, table_ref[pl.ds(at, SIDE), :], zero)


def rim_kernel(subs, pairs_ref, after_ref, inner_ref, rim_ref, matrix_ref, energy_ref, gram_ref, pixels, sems):
    copies = []
    for n, taps in enumerate(tap_blocks()):
        copies.append(pltpu.make_async_copy(inner_ref.at[taps], gram_ref.at[taps], sems.at[n]))
        copies[-1].start()
    for t in range(TAPS):
        pixel, cycle = rim_sources(t)
        pixels[:, t * CH : (t + 1) * CH] = one_hot(2 * PIX, pixel)
        matrix_ref[:, t * CH : (t + 1) * CH] = one_hot(2 * CH, cycle)
    energy = jnp.zeros((CH, CH), jnp.float32)
    for p in range(2 * subs):
        x = pairs_ref[p * CH : (p + 1) * CH, :].astype(jnp.float32)
        for n in range(4):
            energy += x[:, n * CH : (n + 1) * CH] * x[:, n * CH : (n + 1) * CH]
    energy_ref[...] = energy
    values = jnp.dot(pairs_ref[...], pixels[...], preferred_element_type=jnp.float32).astype(jnp.bfloat16)
    for p in range(2 * subs):
        for t in range(TAPS):
            part = values[p * CH : (p + 1) * CH, t * CH : (t + 1) * CH]
            rim_ref[t * CH : (t + 1) * CH, p * CH : (p + 1) * CH] = part
    for copy in copies:
        copy.wait()


def outer_kernel(
    subs,
    tiles_own_ref,
    tiles_other_ref,
    halo_rows_own_ref,
    halo_rows_other_ref,
    matrix_ref,
    energy_ref,
    mask_ref,
    rim_ref,
    inner_ref,
    message_ref,
    patches,
    owned,
    gram,
    stage,
    position,
    cycles,
):
    core = core_index()
    units = 4 * subs
    half = units // 2
    lane = lax.broadcasted_iota(jnp.int32, (8, CH), 1)
    base = jnp.full((8, CH), -1000, jnp.int32)
    for e, at in enumerate(SIDE_AT):
        base = jnp.where((lane >= at) & (lane < at + SIDE), e * SIDE, base)
    for e, at in enumerate(CORNER_AT):
        base = jnp.where(lane == at, (4 + e) * SIDE, base)
    position[...] = jnp.zeros((8, CH), jnp.int32)
    position[0:subs, 0:CYCLE] = lax.rem(halo_rows_own_ref[...], SIDE)
    position[subs : 2 * subs, 0:CYCLE] = lax.rem(halo_rows_other_ref[...], SIDE)
    source = position[...] + base

    row_at = lax.broadcasted_iota(jnp.int32, (CH, CH), 0)
    col_at = lax.broadcasted_iota(jnp.int32, (CH, CH), 1)
    diagonal = row_at == col_at
    eye = jnp.where(diagonal, 1.0, 0.0).astype(jnp.bfloat16)
    split = units * CH // 2
    energy = energy_ref[...]
    for side, (mine, theirs) in enumerate(((0, split), (split, 0))):
        tiles = tiles_own_ref[mine : mine + split, :] + tiles_other_ref[theirs : theirs + split, :]
        tiles = lax.dot_general(eye, tiles, NT, preferred_element_type=jnp.float32).astype(jnp.bfloat16)
        for p in range(half):
            at = side * subs + p % subs
            pick = jnp.where(row_at == source[at : at + 1, :], 1.0, 0.0).astype(jnp.bfloat16)
            cycle = jnp.dot(tiles[:, p * CH : (p + 1) * CH], pick, preferred_element_type=jnp.float32)
            energy += cycle * cycle
            cycles[p * CH : (p + 1) * CH, side * CH : (side + 1) * CH] = cycle.astype(jnp.bfloat16)

    values = jnp.dot(cycles[...], matrix_ref[...], preferred_element_type=jnp.float32).astype(jnp.bfloat16)
    for p in range(half):
        for t in range(TAPS):
            part = values[p * CH : (p + 1) * CH, t * CH : (t + 1) * CH]
            place = (slice(t * CH, (t + 1) * CH), slice(p * CH, (p + 1) * CH))
            patches[place] = rim_ref[place] + part

    kept = mask_ref[...].astype(jnp.float32)
    kept_row = jnp.sum(jnp.where(diagonal, kept, 0.0), axis=1, keepdims=True)
    energy = jnp.sum(energy, axis=1, keepdims=True)

    def exponent(values):
        top = jnp.full((8, CH), jnp.maximum(jnp.max(values), 2.0**-120), jnp.float32)
        return jnp.ceil(jnp.log2(top) * (STEPS / 2) + 0.1)

    kept_exp = exponent(jnp.where(kept_row > 0, energy, 0.0))
    any_exp = exponent(energy)
    lane_exps = jnp.where(kept > 0, kept_exp, any_exp) + kept_exp
    scale = jnp.exp2(lane_exps * (-1 / STEPS))

    def coded(values):
        return jnp.round(TOP * values * lax.rsqrt(jnp.maximum(jnp.abs(values), 1e-30)))

    owned_rows(core, patches, owned)
    for n, taps in enumerate(tap_blocks()):
        right = patches[taps.start * CH : taps.stop * CH, :]
        block = lax.dot_general(owned[...], right, NT, preferred_element_type=jnp.float32)
        for l in range(taps.stop - taps.start):
            part = block[:, l * CH : (l + 1) * CH] + inner_ref[taps.start + l, :, :]
            gram[taps.start + l, :, :] = coded(part * scale[0:1, :])

    for j in range(message_ref.shape[0]):
        block = stage.at[j % 4]
        for l in range(TAPS):
            block[l * 9 : (l + 1) * 9, :] = gram[l, j * 9 : (j + 1) * 9, :]
        block[81:88, :] = lane_exps[0:7, :]
        message_ref[j] = block[...].astype(jnp.int32).astype(jnp.int16)


def rows_kernel(count, landed_ref, weight_ref, kept_ref, out_ref, rows, split):
    owner = lax.axis_index("face") * lax.axis_size("sample") + lax.axis_index("sample")
    total = jnp.zeros((ROWS, CH), jnp.float32)
    for j in range(landed_ref.shape[0]):
        codes = landed_ref[j].astype(jnp.int32).astype(jnp.float32)
        scale = jnp.exp2(codes[80:88, :] * (1 / STEPS))
        total += codes * jnp.abs(codes) * scale[1:2, :]
    total = total * TOP**-2
    rows[...] = jnp.zeros_like(rows)
    for l in range(TAPS):
        rows[0:9, l * CH : (l + 1) * CH] = total[l * 9 : (l + 1) * 9, :]

    channel = lax.rem(owner * 9 + lax.broadcasted_iota(jnp.int32, (16, CH), 0), CH)
    own = lax.broadcasted_iota(jnp.int32, (16, CH), 1) == channel
    keep = jnp.sum(jnp.where(own, kept_ref[...].astype(jnp.float32), 0.0), axis=1, keepdims=True)
    whole = rows[...]
    head = whole.astype(jnp.bfloat16)
    left = whole - head.astype(jnp.float32)
    tail = left.astype(jnp.bfloat16)
    split[0:16, :] = head
    split[16:32, :] = tail
    split[32:48, :] = (left - tail.astype(jnp.float32)).astype(jnp.bfloat16)
    product = jnp.dot(split[...], weight_ref[...], preferred_element_type=jnp.float32)
    product = product[32:48, :] + product[16:32, :] + product[0:16, :]
    kept = kept_ref[...] > 0
    for t in range(TAPS):
        part = whole[:, t * CH : (t + 1) * CH]
        part = jnp.where((keep > 0) & kept, part / count, 0.0)
        out_ref[:, t * CH : (t + 1) * CH] = part[0:9, :]
    for n in range(2):
        part = product[:, n * CH : (n + 1) * CH]
        part = jnp.where(keep > 0, part / count, 0.0)
        out_ref[:, K + n * CH : K + (n + 1) * CH] = part[0:9, :]


VMEM = pl.BlockSpec(memory_space=pltpu.VMEM)
SMEM = pl.BlockSpec(memory_space=pltpu.SMEM)
HBM = pl.BlockSpec(memory_space=pltpu.HBM)


def shape(dims, kind):
    return jax.ShapeDtypeStruct(dims, kind)


def per_device(fields, sample_index, halo_index, channel_mask, weight):
    faces, samples = lax.axis_size("face"), lax.axis_size("sample")
    subs = fields.shape[1]
    units = 4 * subs
    swap = [(f, f ^ 1) for f in range(faces)]
    bf16, f32 = jnp.bfloat16, jnp.float32

    other = lax.ppermute(fields, "face", swap)
    halo_other = lax.ppermute(halo_index, "face", swap)
    copies = pl.pallas_call(
        edges_kernel,
        out_shape=shape((faces // 2, 8 * subs * SIDE, CH), bf16),
        in_specs=[SMEM, VMEM, VMEM],
        out_specs=VMEM,
        name="edges",
    )(sample_index, fields, jnp.asarray(edge_picker()))

    copies, other, halo_other = lax.optimization_barrier((copies, other, halo_other))
    same_core = [[f for f in range(c, faces, 2)] for c in range(2)]
    table = lax.all_to_all(copies, "face", 0, 0, axis_index_groups=same_core)

    mask_row = channel_mask[None]
    inner, pairs, plan = pl.pallas_call(
        inner_kernel,
        out_shape=(
            pltpu.HBM((TAPS, HALF, CH), f32),
            shape((units * CH // 2, 2 * PIX), bf16),
            shape((2 * subs * 8,), jnp.int32),
        ),
        in_specs=[SMEM] * 3 + [VMEM] * 2,
        out_specs=(HBM, VMEM, SMEM),
        scratch_shapes=[
            pltpu.VMEM((K, units * INNER), bf16),
            pltpu.VMEM((HALF, units * INNER), bf16),
            pltpu.VMEM((TAPS, HALF, CH), f32),
            pltpu.SemaphoreType.DMA((3,)),
        ],
        compiler_params=pltpu.CompilerParams(vmem_limit_bytes=32 * 2**20),
        cost_estimate=pl.CostEstimate(flops=6 * 10**9, bytes_accessed=5 * 10**6, transcendentals=0),
        name="inner",
    )(sample_index, halo_index, halo_other, fields, other)

    tiles = pl.pallas_call(
        functools.partial(gather_kernel, subs),
        out_shape=shape((units * CH, CH), bf16),
        in_specs=[SMEM, VMEM],
        out_specs=VMEM,
        compiler_params=pltpu.CompilerParams(vmem_limit_bytes=4 * 2**20),
        name="gather",
    )(plan, table.reshape(-1, CH))
    tiles_other = lax.ppermute(tiles, "face", swap)

    rim, matrix, energy, inner = pl.pallas_call(
        functools.partial(rim_kernel, subs),
        out_shape=(
            shape((K, units * RIM), bf16),
            shape((2 * CH, K), bf16),
            shape((CH, CH), f32),
            shape((TAPS, HALF, CH), f32),
        ),
        in_specs=[VMEM, pl.BlockSpec(memory_space=pl.ANY), HBM],
        out_specs=(VMEM, VMEM, VMEM, VMEM),
        scratch_shapes=[pltpu.VMEM((2 * PIX, K), bf16), pltpu.SemaphoreType.DMA((3,))],
        compiler_params=pltpu.CompilerParams(vmem_limit_bytes=16 * 2**20),
        cost_estimate=pl.CostEstimate(flops=10**9, bytes_accessed=6 * 10**6, transcendentals=0),
        name="rim",
    )(pairs, tiles, pltpu.with_memory_space_constraint(inner, pltpu.HBM))

    message = pl.pallas_call(
        functools.partial(outer_kernel, subs),
        out_shape=shape((64, ROWS, CH), jnp.int16),
        in_specs=[VMEM] * 9,
        out_specs=VMEM,
        scratch_shapes=[
            pltpu.VMEM((K, units * RIM), bf16),
            pltpu.VMEM((HALF, units * RIM), bf16),
            pltpu.VMEM((TAPS, HALF, CH), f32),
            pltpu.VMEM((4, ROWS, CH), f32),
            pltpu.VMEM((8, CH), jnp.int32),
            pltpu.VMEM((units * CH // 2, 2 * CH), bf16),
        ],
        compiler_params=pltpu.CompilerParams(vmem_limit_bytes=28 * 2**20),
        name="outer",
    )(
        tiles,
        tiles_other,
        halo_index,
        halo_other,
        matrix,
        energy,
        mask_row,
        rim,
        inner,
    )

    groups = [[f * samples + s for f in range(c, faces, 2) for s in range(samples)] for c in range(2)]
    landed = lax.all_to_all(message, AXES, 0, 0, axis_index_groups=groups)
    count = 2 * subs * PIX * faces * samples
    return pl.pallas_call(
        functools.partial(rows_kernel, count),
        out_shape=shape((9, K + weight.shape[1]), f32),
        in_specs=[VMEM] * 3,
        out_specs=VMEM,
        scratch_shapes=[pltpu.VMEM((16, K), f32), pltpu.VMEM((48, K), bf16)],
        compiler_params=pltpu.CompilerParams(vmem_limit_bytes=8 * 2**20),
        name="rows",
    )(landed, weight, mask_row)


def solution(mesh):
    placed = (P("sample", "face", None, None), P("sample"), P("face", None), P(), P())
    return jax.shard_map(
        per_device,
        mesh=mesh,
        in_specs=placed,
        out_specs=P(("face", "sample"), None),
        check_vma=False,
    )
```

time: 66.4 us -> 64.7 us (0.974)
  Pallas kernels: 21 us -> 19.6 us
    pallas_call x1 -> x2, Pallas kernels: 1.97 us -> 4.23 us  [the longest x1 2.8 us: per_device(): pl.pallas_call(functools.partial(rim_kernel, subs), out_shape=(shape((K,...]
    pallas_call x1, Pallas kernels: 5.59 us -> 3.83 us  [per_device(): pl.pallas_call(functools.partial(outer_kernel, subs), out_shape=shape((64...]
    ppermute x1, waiting for transfers between devices: 1.35 us -> 0.01 us  [per_device(): tiles_other = lax.ppermute(tiles, 'face', swap)]
    pallas_call x1, Pallas kernels: 1.74 us -> 0.76 us  [per_device(): pl.pallas_call(functools.partial(gather_kernel, subs), out_shape=shape((u...]
    all_to_all x1, waiting for transfers between devices: 3.42 us -> 4.37 us  [per_device(): table = lax.all_to_all(copies, 'face', 0, 0, axis_index_groups=same_core)]
    pallas_call x1, Pallas kernels: 9.43 us -> 8.57 us  [per_device(): pl.pallas_call(inner_kernel, out_shape=(pltpu.HBM((TAPS, HALF, CH), f32),...]
  transfers between devices with their start and end apart: 4 -> 4, of which waited for: 2 -> 1; matrix products, arithmetic and copies ran while one was open for 0% -> 0% of each run, Pallas kernels for 18% -> 21%
where the time goes in v6:
time: 64.7 us; the launch traced here: 64.5 us
  blocking collectives  30 us (46%)
  Pallas kernels  19.6 us (30%)
  starting transfers between devices  10.4 us (16%)
  waiting for transfers between devices  4.38 us (7%)
    all_to_all x1, blocking collectives, per_device(): landed = lax.all_to_all(message, AXES, 0, 0, axis_index_groups=groups)  30 us
    pallas_call x1, Pallas kernels, per_device(): pl.pallas_call(inner_kernel, out_shape=(pltpu.HBM((TAPS, HALF, CH), f32),...  8.57 us
    all_to_all x1, starting transfers between devices, per_device(): table = lax.all_to_all(copies, 'face', 0, 0, axis_index_groups=same_core)  7.69 us
    all_to_all x1, waiting for transfers between devices, per_device(): table = lax.all_to_all(copies, 'face', 0, 0, axis_index_groups=same_core)  4.37 us
    pallas_call x1, Pallas kernels, per_device(): pl.pallas_call(functools.partial(outer_kernel, subs), out_shape=shape((64...  3.83 us
    pallas_call x1, Pallas kernels, per_device(): pl.pallas_call(functools.partial(rim_kernel, subs), out_shape=(shape((K,...  2.8 us
    pallas_call x1, Pallas kernels, per_device(): pl.pallas_call(edges_kernel, out_shape=shape((faces // 2, 8 * subs * SIDE...  2.22 us
    pallas_call x1, Pallas kernels, per_device(): pl.pallas_call(functools.partial(rows_kernel, count), out_shape=shape((9,...  1.43 us
  transfers between devices with their start and end apart: 4, of which 1 were waited for; matrix products, arithmetic and copies ran while one was open for 0% of the time, Pallas kernels for 21%

profile of v6, /device:TPU:1, one launch (start us, length us, event | category | flops | bytes accessed | tf_op | source)
XLA Modules:
  0.0 64.5 jit_solution(7884920758408109132)
XLA Ops:
  0.0 0.0 copy-start
  0.0 0.0 copy-start.2
  0.0 0.0 copy-start.4
  0.0 1.4 %collective-permute-start = (bf16[3,3,128,256]{3,2,1,0:T(8,128)(2,1)}, bf16[3,3,128,256]{3,2,1,0:T(8,128)(2,1)S(1)}, u32[]{:S(2)}, u32[]{:S(2)}) collective-permute-start(bf16[3,3,128,256]{3,2,1,0:T(8,128)(2,1)} %own_ref.1), channel_id=1, source_target_pairs={{0,8},{8,0},{16,24},{24,16},{32,40},{40,32},{48,56},{56,48},{64,72... | collective-permute-start | bytes 1769480 | tf_op jit(solution)/shard_map/ppermute | solution.py:341
  1.4 0.1 collective-permute-start.1
  1.5 2.2 %edges.1 = bf16[8,384,128]{2,1,0:T(8,128)(2,1)} custom-call(s32[2]{0:T(128)} %index_ref.3, bf16[3,3,128,256]{3,2,1,0:T(8,128)(2,1)} %own_ref.1, bf16[64,256]{1,0:T(8,128)(2,1)} %constant.2.clone.pick_ref), custom_call_target="tpu_custom_call" | custom-call | tf_op jit(solution)/shard_map/edges/pallas_call | solution.py:343
  3.7 0.0 collective-permute-done.1.halo_other_ref.halo_rows_other_ref
  3.7 0.0 collective-permute-done.other_ref
  3.7 7.7 %all-to-all-start = ((bf16[8,384,128]{2,1,0:T(8,128)(2,1)}), bf16[8,384,128]{2,1,0:T(8,128)(2,1)S(1)}, u32[]{:S(2)}, u32[]{:S(2)}) async-start(bf16[8,384,128]{2,1,0:T(8,128)(2,1)} %edges.1), calls=%async_computation | async-start | bytes 1572864 | tf_op jit(solution)/shard_map/all_to_all | solution.py:353
  11.4 0.0 copy-done
  11.4 0.0 copy-done.2
  11.4 0.0 copy-done.4
  11.5 8.6 %inner.1 = (f32[9,576,128]{2,1,0:T(8,128)}, bf16[768,512]{1,0:T(8,128)(2,1)S(1)}, s32[48]{0:T(128)S(1)}) custom-call(s32[2]{0:T(128)S(1)} %copy-done.4, s32[3,68]{1,0:T(4,128)S(1)} %copy-done.2, s32[3,68]{1,0:T(4,128)S(1)} %collective-permute-done.1.halo_other_ref.halo_rows_other_ref, bf16[3,3,128,256]{3,2,1,0:T(8,128)(2,1)S(1)} %copy-done, ...), custom_call_target="tpu_custom_call" | custom-call | flops 6000000000 | bytes 5000000 | tf_op jit(solution)/shard_map/inner/pallas_call | solution.py:356
  20.0 4.4 %all-to-all-done = bf16[8,384,128]{2,1,0:T(8,128)(2,1)S(1)} async-done(((bf16[8,384,128]{2,1,0:T(8,128)(2,1)}), bf16[8,384,128]{2,1,0:T(8,128)(2,1)S(1)}, u32[]{:S(2)}, u32[]{:S(2)}) %all-to-all-start) | async-done | bytes 786464 | tf_op jit(solution)/shard_map/all_to_all | solution.py:353
  24.4 0.8 %gather.1.after_ref.tiles_own_ref = bf16[1536,128]{1,0:T(8,128)(2,1)S(1)} custom-call(s32[48]{0:T(128)S(1)} %get-tuple-element.17.plan_ref, bf16[3072,128]{1,0:T(8,128)(2,1)S(1)} %bitcast.2), custom_call_target="tpu_custom_call" | custom-call | tf_op jit(solution)/shard_map/gather/pallas_call | solution.py:376
  25.2 1.2 %collective-permute-start.2 = (bf16[1536,128]{1,0:T(8,128)(2,1)S(1)}, bf16[1536,128]{1,0:T(8,128)(2,1)S(1)}, u32[]{:S(2)}, u32[]{:S(2)}) collective-permute-start(bf16[1536,128]{1,0:T(8,128)(2,1)S(1)} %gather.1.after_ref.tiles_own_ref), channel_id=1, source_target_pairs={{0,8},{8,0},{16,24},{24,16},{32,40},{40,32},{48,56},{56,48},{64,72... | collective-permute-start | bytes 1179656 | tf_op jit(solution)/shard_map/ppermute | solution.py:384
  26.3 0.0 copy-start.3
  26.4 2.8 %rim.1 = (bf16[1152,768]{1,0:T(8,128)(2,1)S(1)}, bf16[256,1152]{1,0:T(8,128)(2,1)S(1)}, f32[128,128]{1,0:T(8,128)S(1)}, f32[9,576,128]{2,1,0:T(8,128)S(1)}) custom-call(bf16[768,512]{1,0:T(8,128)(2,1)S(1)} %get-tuple-element.19.pairs_ref, bf16[1536,128]{1,0:T(8,128)(2,1)S(1)} %gather.1.after_ref.tiles_own_ref, f32[9,576,128]{2,1,0:T(8,128)} %get-tuple-element.20.inner_ref), custom_call_target="tpu_custom_call" | custom-call | flops 1000000000 | bytes 6000000 | tf_op jit(solution)/shard_map/rim/pallas_call | solution.py:386
  29.2 0.0 collective-permute-done.2.tiles_other_ref
  29.2 0.0 copy-done.3
  29.2 3.8 %outer.1 = s16[64,88,128]{2,1,0:T(8,128)(2,1)S(1)} custom-call(bf16[1536,128]{1,0:T(8,128)(2,1)S(1)} %gather.1.after_ref.tiles_own_ref, bf16[1536,128]{1,0:T(8,128)(2,1)S(1)} %collective-permute-done.2.tiles_other_ref, s32[3,68]{1,0:T(4,128)S(1)} %copy-done.2, s32[3,68]{1,0:T(4,128)S(1)} %collective-permute-done.1.halo_other_ref.halo_rows_other_ref, ...), custom_call_target="tpu_custom_call" | custom-call | tf_op jit(solution)/shard_map/outer/pallas_call | solution.py:402
  33.0 0.0 copy-start.1
  33.0 30.0 %all_to_all.10.landed_ref = s16[64,88,128]{2,1,0:T(8,128)(2,1)S(1)} all-to-all(s16[64,88,128]{2,1,0:T(8,128)(2,1)S(1)} %outer.1), channel_id=1, replica_groups={{0,1,2,3,4,5,6,7,16,17,18,19,20,21,22,23,32,33,34,35,36,37,38,39,48,49,..., dimensions={0} | all-to-all | bytes 2883584 | tf_op jit(solution)/shard_map/all_to_all | solution.py:430
  63.0 0.0 copy-done.1
  63.0 1.4 %rows.1 = f32[9,1408]{1,0:T(8,128)} custom-call(s16[64,88,128]{2,1,0:T(8,128)(2,1)S(1)} %all_to_all.10.landed_ref, bf16[1152,256]{1,0:T(8,128)(2,1)S(1)} %copy-done.1, s32[1,128]{1,0:T(1,128)S(1)} %bitcast.4), custom_call_target="tpu_custom_call" | custom-call | tf_op jit(solution)/shard_map/rows/pallas_call | solution.py:432
Async XLA Ops:
  0.0 11.4 %copy-start = (bf16[3,3,128,256]{3,2,1,0:T(8,128)(2,1)S(1)}, bf16[3,3,128,256]{3,2,1,0:T(8,128)(2,1)}, u32[]{:S(2)}) copy-start(bf16[3,3,128,256]{3,2,1,0:T(8,128)(2,1)} %own_ref.1) | copy-start | bytes 1769476
  0.0 11.4 %copy-start.2 = (s32[3,68]{1,0:T(4,128)S(1)}, s32[3,68]{1,0:T(4,128)}, u32[]{:S(2)}) copy-start(s32[3,68]{1,0:T(4,128)} %halo_rows_own_ref.1) | copy-start | bytes 2452
  0.0 11.4 %copy-start.4 = (s32[2]{0:T(128)S(1)}, s32[2]{0:T(128)}, u32[]{:S(2)}) copy-start(s32[2]{0:T(128)} %index_ref.3) | copy-start | bytes 28
  0.0 3.7 %collective-permute-start = (bf16[3,3,128,256]{3,2,1,0:T(8,128)(2,1)}, bf16[3,3,128,256]{3,2,1,0:T(8,128)(2,1)S(1)}, u32[]{:S(2)}, u32[]{:S(2)}) collective-permute-start(bf16[3,3,128,256]{3,2,1,0:T(8,128)(2,1)} %own_ref.1), channel_id=1, source_target_pairs={{0,8},{8,0},{16,24},{24,16},{32,40},{40,32},{48,56},{56,48},{64,72... | collective-permute-start | bytes 1769480 | tf_op jit(solution)/shard_map/ppermute | solution.py:341
  1.4 2.3 %collective-permute-start.1 = (s32[3,68]{1,0:T(4,128)}, s32[3,68]{1,0:T(4,128)S(1)}, u32[]{:S(2)}, u32[]{:S(2)}) collective-permute-start(s32[3,68]{1,0:T(4,128)} %halo_rows_own_ref.1), channel_id=1, source_target_pairs={{0,8},{8,0},{16,24},{24,16},{32,40},{40,32},{48,56},{56,48},{64,72... | collective-permute-start | bytes 2456 | tf_op jit(solution)/shard_map/ppermute | solution.py:342
  3.7 20.7 %all-to-all-start = ((bf16[8,384,128]{2,1,0:T(8,128)(2,1)}), bf16[8,384,128]{2,1,0:T(8,128)(2,1)S(1)}, u32[]{:S(2)}, u32[]{:S(2)}) async-start(bf16[8,384,128]{2,1,0:T(8,128)(2,1)} %edges.1), calls=%async_computation | async-start | bytes 1572864 | tf_op jit(solution)/shard_map/all_to_all | solution.py:353
  25.2 4.0 %collective-permute-start.2 = (bf16[1536,128]{1,0:T(8,128)(2,1)S(1)}, bf16[1536,128]{1,0:T(8,128)(2,1)S(1)}, u32[]{:S(2)}, u32[]{:S(2)}) collective-permute-start(bf16[1536,128]{1,0:T(8,128)(2,1)S(1)} %gather.1.after_ref.tiles_own_ref), channel_id=1, source_target_pairs={{0,8},{8,0},{16,24},{24,16},{32,40},{40,32},{48,56},{56,48},{64,72... | collective-permute-start | bytes 1179656 | tf_op jit(solution)/shard_map/ppermute | solution.py:384
  26.3 2.8 %copy-start.3 = (s32[128]{0:T(128)S(1)}, s32[128]{0:T(128)}, u32[]{:S(2)}) copy-start(s32[128]{0:T(128)} %param.9) | copy-start | bytes 1540
  33.0 30.0 %copy-start.1 = (bf16[1152,256]{1,0:T(8,128)(2,1)S(1)}, bf16[1152,256]{1,0:T(8,128)(2,1)}, u32[]{:S(2)}) copy-start(bf16[1152,256]{1,0:T(8,128)(2,1)} %weight_ref.1) | copy-start | bytes 1769476

commit v7 on v6

--- a/solution.py
+++ b/solution.py
@@ -26,16 +26,6 @@
 NT = (((1,), (1,)), ((), ()))
 SIDE_AT = (1, 19, 36, 52)
 CORNER_AT = (0, 17, 18, 35)
-
-
-def edge_picker():
-    out = np.zeros((4 * SIDE, PIX), np.float32)
-    for i in range(SIDE):
-        out[i, i] = 1
-        out[SIDE + i, (SIDE - 1) * SIDE + i] = 1
-        out[2 * SIDE + i, i * SIDE] = 1
-        out[3 * SIDE + i, i * SIDE + SIDE - 1] = 1
-    return out.astype(ml_dtypes.bfloat16)
 
 
 def rim_sources(tap):
@@ -71,13 +61,20 @@
     return jnp.where(at == source, 1.0, 0.0).astype(jnp.bfloat16)
 
 
-def edges_kernel(index_ref, fields_ref, pick_ref, copies_ref):
+def edges_kernel(index_ref, fields_ref, copies_ref):
     subs = fields_ref.shape[1]
+    row = lax.broadcasted_iota(jnp.int32, (4 * SIDE, PIX), 0)
+    pixel = lax.broadcasted_iota(jnp.int32, (4 * SIDE, PIX), 1)
+    along = row & (SIDE - 1)
+    wanted = jnp.where(row < SIDE, along, (SIDE - 1) * SIDE + along)
+    wanted = jnp.where(row >= 2 * SIDE, along * SIDE, wanted)
+    wanted = jnp.where(row >= 3 * SIDE, along * SIDE + SIDE - 1, wanted)
+    pick = jnp.where(pixel == wanted, 1.0, 0.0).astype(jnp.bfloat16)
     for s in range(2):
         for f in range(subs):
             x = fields_ref[index_ref[s], f]
             u = s * subs + f
-            edges = lax.dot_general(pick_ref[...], x, NT, preferred_element_type=jnp.float32)
+            edges = lax.dot_general(pick, x, NT, preferred_element_type=jnp.float32)
             edges = edges.astype(jnp.bfloat16)
             for d in range(copies_ref.shape[0]):
                 copies_ref[d, u * 4 * SIDE : (u + 1) * 4 * SIDE, :] = edges
@@ -175,11 +172,9 @@
                 tiles_ref[u * CH + n * SIDE : u * CH + (n + 1) * SIDE, :] = jnp.where(near, table_ref[pl.ds(at, SIDE), :], zero)
 
 
-def rim_kernel(subs, pairs_ref, after_ref, inner_ref, rim_ref, matrix_ref, energy_ref, gram_ref, pixels, sems):
-    copies = []
-    for n, taps in enumerate(tap_blocks()):
-        copies.append(pltpu.make_async_copy(inner_ref.at[taps], gram_ref.at[taps], sems.at[n]))
-        copies[-1].start()
+def rim_kernel(subs, pairs_ref, after_ref, inner_ref, rim_ref, matrix_ref, energy_ref, gram_ref, pixels, sem):
+    copy = pltpu.make_async_copy(inner_ref.at[tap_blocks()[0]], gram_ref, sem)
+    copy.start()
     for t in range(TAPS):
         pixel, cycle = rim_sources(t)
         pixels[:, t * CH : (t + 1) * CH] = one_hot(2 * PIX, pixel)
@@ -195,8 +190,7 @@
         for t in range(TAPS):
             part = values[p * CH : (p + 1) * CH, t * CH : (t + 1) * CH]
             rim_ref[t * CH : (t + 1) * CH, p * CH : (p + 1) * CH] = part
-    for copy in copies:
-        copy.wait()
+    copy.wait()
 
 
 def outer_kernel(
@@ -209,6 +203,7 @@
     energy_ref,
     mask_ref,
     rim_ref,
+    first_ref,
     inner_ref,
     message_ref,
     patches,
@@ -217,10 +212,17 @@
     stage,
     position,
     cycles,
+    inner,
+    sems,
 ):
     core = core_index()
     units = 4 * subs
     half = units // 2
+    copies = []
+    for n, taps in enumerate(tap_blocks()[1:]):
+        copies.append(pltpu.make_async_copy(inner_ref.at[taps], inner.at[taps], sems.at[n]))
+        copies[-1].start()
+
     lane = lax.broadcasted_iota(jnp.int32, (8, CH), 1)
     base = jnp.full((8, CH), -1000, jnp.int32)
     for e, at in enumerate(SIDE_AT):
@@ -275,8 +277,10 @@
     for n, taps in enumerate(tap_blocks()):
         right = patches[taps.start * CH : taps.stop * CH, :]
         block = lax.dot_general(owned[...], right, NT, preferred_element_type=jnp.float32)
+        if n > 0:
+            copies[n - 1].wait()
         for l in range(taps.stop - taps.start):
-            part = block[:, l * CH : (l + 1) * CH] + inner_ref[taps.start + l, :, :]
+            part = block[:, l * CH : (l + 1) * CH] + (inner if n > 0 else first_ref)[taps.start + l, :, :]
             gram[taps.start + l, :, :] = coded(part * scale[0:1, :])
 
     for j in range(message_ref.shape[0]):
@@ -343,12 +347,12 @@
     copies = pl.pallas_call(
         edges_kernel,
         out_shape=shape((faces // 2, 8 * subs * SIDE, CH), bf16),
-        in_specs=[SMEM, VMEM, VMEM],
+        in_specs=[SMEM, VMEM],
         out_specs=VMEM,
+        compiler_params=pltpu.CompilerParams(vmem_limit_bytes=8 * 2**20),
         name="edges",
-    )(sample_index, fields, jnp.asarray(edge_picker()))
-
-    copies, other, halo_other = lax.optimization_barrier((copies, other, halo_other))
+    )(*(pltpu.with_memory_space_constraint(a, pltpu.HBM) for a in (sample_index, fields)))
+
     same_core = [[f for f in range(c, faces, 2)] for c in range(2)]
     table = lax.all_to_all(copies, "face", 0, 0, axis_index_groups=same_core)
 
@@ -383,26 +387,27 @@
     )(plan, table.reshape(-1, CH))
     tiles_other = lax.ppermute(tiles, "face", swap)
 
-    rim, matrix, energy, inner = pl.pallas_call(
+    inner = pltpu.with_memory_space_constraint(inner, pltpu.HBM)
+    rim, matrix, energy, first = pl.pallas_call(
         functools.partial(rim_kernel, subs),
         out_shape=(
             shape((K, units * RIM), bf16),
             shape((2 * CH, K), bf16),
             shape((CH, CH), f32),
-            shape((TAPS, HALF, CH), f32),
+            shape((tap_blocks()[0].stop, HALF, CH), f32),
         ),
         in_specs=[VMEM, pl.BlockSpec(memory_space=pl.ANY), HBM],
         out_specs=(VMEM, VMEM, VMEM, VMEM),
-        scratch_shapes=[pltpu.VMEM((2 * PIX, K), bf16), pltpu.SemaphoreType.DMA((3,))],
+        scratch_shapes=[pltpu.VMEM((2 * PIX, K), bf16), pltpu.SemaphoreType.DMA],
         compiler_params=pltpu.CompilerParams(vmem_limit_bytes=16 * 2**20),
         cost_estimate=pl.CostEstimate(flops=10**9, bytes_accessed=6 * 10**6, transcendentals=0),
         name="rim",
-    )(pairs, tiles, pltpu.with_memory_space_constraint(inner, pltpu.HBM))
+    )(pairs, tiles, inner)
 
     message = pl.pallas_call(
         functools.partial(outer_kernel, subs),
         out_shape=shape((64, ROWS, CH), jnp.int16),
-        in_specs=[VMEM] * 9,
+        in_specs=[VMEM] * 9 + [HBM],
         out_specs=VMEM,
         scratch_shapes=[
             pltpu.VMEM((K, units * RIM), bf16),
@@ -411,6 +416,8 @@
             pltpu.VMEM((4, ROWS, CH), f32),
             pltpu.VMEM((8, CH), jnp.int32),
             pltpu.VMEM((units * CH // 2, 2 * CH), bf16),
+            pltpu.VMEM((TAPS, HALF, CH), f32),
+            pltpu.SemaphoreType.DMA((2,)),
         ],
         compiler_params=pltpu.CompilerParams(vmem_limit_bytes=28 * 2**20),
         name="outer",
@@ -423,6 +430,7 @@
         energy,
         mask_row,
         rim,
+        first,
         inner,
     )
 

time: 64.7 us -> 63.7 us (0.985)
  Pallas kernels: 19.6 us -> 18.6 us
    pallas_call x1, Pallas kernels: 2.8 us -> 1.55 us  [per_device(): pl.pallas_call(functools.partial(rim_kernel, subs), out_shape=(shape((K,...]
    all_to_all x1, waiting for transfers between devices: 4.37 us -> 3.33 us  [per_device(): table = lax.all_to_all(copies, 'face', 0, 0, axis_index_groups=same_core)]
    ppermute x1, waiting for transfers between devices: 0.01 us -> 0.82 us  [per_device(): halo_other = lax.ppermute(halo_index, 'face', swap)]
  transfers between devices with their start and end apart: 4 -> 4, of which waited for: 1 -> 2; matrix products, arithmetic and copies ran while one was open for 0% -> 0% of each run, Pallas kernels for 21% -> 19%
where the time goes in v7:
time: 63.7 us; the launch traced here: 63.4 us
  blocking collectives  29.9 us (47%)
  Pallas kernels  18.6 us (29%)
  starting transfers between devices  10.7 us (17%)
  waiting for transfers between devices  4.16 us (7%)
    all_to_all x1, blocking collectives, per_device(): landed = lax.all_to_all(message, AXES, 0, 0, axis_index_groups=groups)  29.9 us
    pallas_call x1, Pallas kernels, per_device(): pl.pallas_call(inner_kernel, out_shape=(pltpu.HBM((TAPS, HALF, CH), f32),...  8.52 us
    all_to_all x1, starting transfers between devices, per_device(): table = lax.all_to_all(copies, 'face', 0, 0, axis_index_groups=same_core)  7.68 us
    pallas_call x1, Pallas kernels, per_device(): pl.pallas_call(functools.partial(outer_kernel, subs), out_shape=shape((64...  4.16 us
    all_to_all x1, waiting for transfers between devices, per_device(): table = lax.all_to_all(copies, 'face', 0, 0, axis_index_groups=same_core)  3.33 us
    pallas_call x1, Pallas kernels, per_device(): pl.pallas_call(edges_kernel, out_shape=shape((faces // 2, 8 * subs * SIDE...  2.22 us
    pallas_call x1, Pallas kernels, per_device(): pl.pallas_call(functools.partial(rim_kernel, subs), out_shape=(shape((K,...  1.55 us
    pallas_call x1, Pallas kernels, per_device(): pl.pallas_call(functools.partial(rows_kernel, count), out_shape=shape((9,...  1.42 us
  transfers between devices with their start and end apart: 4, of which 2 were waited for; matrix products, arithmetic and copies ran while one was open for 0% of the time, Pallas kernels for 19%

profile of v7, /device:TPU:1, one launch (start us, length us, event | category | flops | bytes accessed | tf_op | source)
XLA Modules:
  0.0 63.4 jit_solution(4870472405260814992)
XLA Ops:
  0.0 0.0 copy-start
  0.0 0.0 copy-start.4
  0.0 0.0 copy-start.3
  0.0 1.4 %collective-permute-start.1 = (bf16[3,3,128,256]{3,2,1,0:T(8,128)(2,1)}, bf16[3,3,128,256]{3,2,1,0:T(8,128)(2,1)S(1)}, u32[]{:S(2)}, u32[]{:S(2)}) collective-permute-start(bf16[3,3,128,256]{3,2,1,0:T(8,128)(2,1)} %fields_ref.1), channel_id=1, source_target_pairs={{0,8},{8,0},{16,24},{24,16},{32,40},{40,32},{48,56},{56,48},{64,72... | collective-permute-start | bytes 1769480 | tf_op jit(solution)/shard_map/ppermute | solution.py:345
  1.4 2.2 %edges.1 = bf16[8,384,128]{2,1,0:T(8,128)(2,1)} custom-call(s32[2]{0:T(128)} %index_ref.3, bf16[3,3,128,256]{3,2,1,0:T(8,128)(2,1)} %fields_ref.1), custom_call_target="tpu_custom_call" | custom-call | tf_op jit(solution)/shard_map/edges/pallas_call | solution.py:347
  3.7 7.7 %all-to-all-start = ((bf16[8,384,128]{2,1,0:T(8,128)(2,1)}), bf16[8,384,128]{2,1,0:T(8,128)(2,1)S(1)}, u32[]{:S(2)}, u32[]{:S(2)}) async-start(bf16[8,384,128]{2,1,0:T(8,128)(2,1)} %edges.1), calls=%async_computation | async-start | bytes 1572864 | tf_op jit(solution)/shard_map/all_to_all | solution.py:357
  11.3 0.0 copy-done.3
  11.3 0.4 collective-permute-start
  11.8 0.8 %collective-permute-done.halo_other_ref.halo_rows_other_ref = s32[3,68]{1,0:T(4,128)S(1)} collective-permute-done((s32[3,68]{1,0:T(4,128)S(1)}, s32[3,68]{1,0:T(4,128)S(1)}, u32[]{:S(2)}, u32[]{:S(2)}) %collective-permute-start) | collective-permute-done | bytes 848 | tf_op jit(solution)/shard_map/ppermute | solution.py:346
  12.6 0.0 collective-permute-done.1.other_ref
  12.6 0.0 copy-done
  12.6 0.0 copy-done.4
  12.6 8.5 %inner.1 = (f32[9,576,128]{2,1,0:T(8,128)}, bf16[768,512]{1,0:T(8,128)(2,1)S(1)}, s32[48]{0:T(128)S(1)}) custom-call(s32[2]{0:T(128)S(1)} %copy-done.4, s32[3,68]{1,0:T(4,128)S(1)} %copy-done.3, s32[3,68]{1,0:T(4,128)S(1)} %collective-permute-done.halo_other_ref.halo_rows_other_ref, bf16[3,3,128,256]{3,2,1,0:T(8,128)(2,1)S(1)} %copy-done, ...), custom_call_target="tpu_custom_call" | custom-call | flops 6000000000 | bytes 5000000 | tf_op jit(solution)/shard_map/inner/pallas_call | solution.py:360
  21.1 3.3 %all-to-all-done = bf16[8,384,128]{2,1,0:T(8,128)(2,1)S(1)} async-done(((bf16[8,384,128]{2,1,0:T(8,128)(2,1)}), bf16[8,384,128]{2,1,0:T(8,128)(2,1)S(1)}, u32[]{:S(2)}, u32[]{:S(2)}) %all-to-all-start) | async-done | bytes 786464 | tf_op jit(solution)/shard_map/all_to_all | solution.py:357
  24.5 0.8 %gather.1.after_ref.tiles_own_ref = bf16[1536,128]{1,0:T(8,128)(2,1)S(1)} custom-call(s32[48]{0:T(128)S(1)} %get-tuple-element.12.plan_ref, bf16[3072,128]{1,0:T(8,128)(2,1)S(1)} %bitcast.2), custom_call_target="tpu_custom_call" | custom-call | tf_op jit(solution)/shard_map/gather/pallas_call | solution.py:380
  25.2 1.1 %collective-permute-start.2 = (bf16[1536,128]{1,0:T(8,128)(2,1)S(1)}, bf16[1536,128]{1,0:T(8,128)(2,1)S(1)}, u32[]{:S(2)}, u32[]{:S(2)}) collective-permute-start(bf16[1536,128]{1,0:T(8,128)(2,1)S(1)} %gather.1.after_ref.tiles_own_ref), channel_id=1, source_target_pairs={{0,8},{8,0},{16,24},{24,16},{32,40},{40,32},{48,56},{56,48},{64,72... | collective-permute-start | bytes 1179656 | tf_op jit(solution)/shard_map/ppermute | solution.py:388
  26.4 0.0 copy-start.2
  26.4 1.5 %rim.1 = (bf16[1152,768]{1,0:T(8,128)(2,1)S(1)}, bf16[256,1152]{1,0:T(8,128)(2,1)S(1)}, f32[128,128]{1,0:T(8,128)S(1)}, f32[4,576,128]{2,1,0:T(8,128)S(1)}) custom-call(bf16[768,512]{1,0:T(8,128)(2,1)S(1)} %get-tuple-element.13.pairs_ref, bf16[1536,128]{1,0:T(8,128)(2,1)S(1)} %gather.1.after_ref.tiles_own_ref, f32[9,576,128]{2,1,0:T(8,128)} %get-tuple-element.14.inner_ref), custom_call_target="tpu_custom_call" | custom-call | flops 1000000000 | bytes 6000000 | tf_op jit(solution)/shard_map/rim/pallas_call | solution.py:391
  27.9 0.0 collective-permute-done.2.tiles_other_ref
  27.9 0.0 copy-done.2
  27.9 4.2 %outer.1 = s16[64,88,128]{2,1,0:T(8,128)(2,1)S(1)} custom-call(bf16[1536,128]{1,0:T(8,128)(2,1)S(1)} %gather.1.after_ref.tiles_own_ref, bf16[1536,128]{1,0:T(8,128)(2,1)S(1)} %collective-permute-done.2.tiles_other_ref, s32[3,68]{1,0:T(4,128)S(1)} %copy-done.3, s32[3,68]{1,0:T(4,128)S(1)} %collective-permute-done.halo_other_ref.halo_rows_other_ref, ...), custom_call_target="tpu_custom_call" | custom-call | tf_op jit(solution)/shard_map/outer/pallas_call | solution.py:407
  32.1 0.0 copy-start.1
  32.1 29.9 %all_to_all.10.landed_ref = s16[64,88,128]{2,1,0:T(8,128)(2,1)S(1)} all-to-all(s16[64,88,128]{2,1,0:T(8,128)(2,1)S(1)} %outer.1), channel_id=1, replica_groups={{0,1,2,3,4,5,6,7,16,17,18,19,20,21,22,23,32,33,34,35,36,37,38,39,48,49,..., dimensions={0} | all-to-all | bytes 2883584 | tf_op jit(solution)/shard_map/all_to_all | solution.py:438
  62.0 0.0 copy-done.1
  62.0 1.4 %rows.1 = f32[9,1408]{1,0:T(8,128)} custom-call(s16[64,88,128]{2,1,0:T(8,128)(2,1)S(1)} %all_to_all.10.landed_ref, bf16[1152,256]{1,0:T(8,128)(2,1)S(1)} %copy-done.1, s32[1,128]{1,0:T(1,128)S(1)} %bitcast.4), custom_call_target="tpu_custom_call" | custom-call | tf_op jit(solution)/shard_map/rows/pallas_call | solution.py:440
Async XLA Ops:
  0.0 12.6 %copy-start = (bf16[3,3,128,256]{3,2,1,0:T(8,128)(2,1)S(1)}, bf16[3,3,128,256]{3,2,1,0:T(8,128)(2,1)}, u32[]{:S(2)}) copy-start(bf16[3,3,128,256]{3,2,1,0:T(8,128)(2,1)} %fields_ref.1) | copy-start | bytes 1769476
  0.0 12.6 %copy-start.4 = (s32[2]{0:T(128)S(1)}, s32[2]{0:T(128)}, u32[]{:S(2)}) copy-start(s32[2]{0:T(128)} %index_ref.3) | copy-start | bytes 28
  0.0 11.3 %copy-start.3 = (s32[3,68]{1,0:T(4,128)S(1)}, s32[3,68]{1,0:T(4,128)}, u32[]{:S(2)}) copy-start(s32[3,68]{1,0:T(4,128)} %halo_rows_own_ref.1) | copy-start | bytes 2452
  0.0 12.6 %collective-permute-start.1 = (bf16[3,3,128,256]{3,2,1,0:T(8,128)(2,1)}, bf16[3,3,128,256]{3,2,1,0:T(8,128)(2,1)S(1)}, u32[]{:S(2)}, u32[]{:S(2)}) collective-permute-start(bf16[3,3,128,256]{3,2,1,0:T(8,128)(2,1)} %fields_ref.1), channel_id=1, source_target_pairs={{0,8},{8,0},{16,24},{24,16},{32,40},{40,32},{48,56},{56,48},{64,72... | collective-permute-start | bytes 1769480 | tf_op jit(solution)/shard_map/ppermute | solution.py:345
  3.7 20.8 %all-to-all-start = ((bf16[8,384,128]{2,1,0:T(8,128)(2,1)}), bf16[8,384,128]{2,1,0:T(8,128)(2,1)S(1)}, u32[]{:S(2)}, u32[]{:S(2)}) async-start(bf16[8,384,128]{2,1,0:T(8,128)(2,1)} %edges.1), calls=%async_computation | async-start | bytes 1572864 | tf_op jit(solution)/shard_map/all_to_all | solution.py:357
  11.3 1.2 %collective-permute-start = (s32[3,68]{1,0:T(4,128)S(1)}, s32[3,68]{1,0:T(4,128)S(1)}, u32[]{:S(2)}, u32[]{:S(2)}) collective-permute-start(s32[3,68]{1,0:T(4,128)S(1)} %copy-done.3), channel_id=1, source_target_pairs={{0,8},{8,0},{16,24},{24,16},{32,40},{40,32},{48,56},{56,48},{64,72... | collective-permute-start | bytes 2456 | tf_op jit(solution)/shard_map/ppermute | solution.py:346
  25.2 2.7 %collective-permute-start.2 = (bf16[1536,128]{1,0:T(8,128)(2,1)S(1)}, bf16[1536,128]{1,0:T(8,128)(2,1)S(1)}, u32[]{:S(2)}, u32[]{:S(2)}) collective-permute-start(bf16[1536,128]{1,0:T(8,128)(2,1)S(1)} %gather.1.after_ref.tiles_own_ref), channel_id=1, source_target_pairs={{0,8},{8,0},{16,24},{24,16},{32,40},{40,32},{48,56},{56,48},{64,72... | collective-permute-start | bytes 1179656 | tf_op jit(solution)/shard_map/ppermute | solution.py:388
  26.4 1.6 %copy-start.2 = (s32[128]{0:T(128)S(1)}, s32[128]{0:T(128)}, u32[]{:S(2)}) copy-start(s32[128]{0:T(128)} %param.8) | copy-start | bytes 1540
  32.1 29.9 %copy-start.1 = (bf16[1152,256]{1,0:T(8,128)(2,1)S(1)}, bf16[1152,256]{1,0:T(8,128)(2,1)}, u32[]{:S(2)}) copy-start(bf16[1152,256]{1,0:T(8,128)(2,1)} %weight_ref.1) | copy-start | bytes 1769476

commit v8 on v7

--- a/solution.py
+++ b/solution.py
@@ -18,7 +18,7 @@
 CYCLE = 4 * SIDE + 4
 RIM = 64
 INNER = PIX - RIM
-ROWS = 88
+ROWS = 82
 STEPS = 16
 TOP = 32700.0
 THIRD = 43
@@ -283,20 +283,20 @@
             part = block[:, l * CH : (l + 1) * CH] + (inner if n > 0 else first_ref)[taps.start + l, :, :]
             gram[taps.start + l, :, :] = coded(part * scale[0:1, :])
 
-    for j in range(message_ref.shape[0]):
+    for j in range(message_ref.shape[0] // ROWS):
         block = stage.at[j % 4]
         for l in range(TAPS):
             block[l * 9 : (l + 1) * 9, :] = gram[l, j * 9 : (j + 1) * 9, :]
         block[81:88, :] = lane_exps[0:7, :]
-        message_ref[j] = block[...].astype(jnp.int32).astype(jnp.int16)
+        message_ref[j * ROWS : (j + 1) * ROWS, :] = block[:ROWS, :].astype(jnp.int32).astype(jnp.int16)
 
 
 def rows_kernel(count, landed_ref, weight_ref, kept_ref, out_ref, rows, split):
     owner = lax.axis_index("face") * lax.axis_size("sample") + lax.axis_index("sample")
     total = jnp.zeros((ROWS, CH), jnp.float32)
-    for j in range(landed_ref.shape[0]):
-        codes = landed_ref[j].astype(jnp.int32).astype(jnp.float32)
-        scale = jnp.exp2(codes[80:88, :] * (1 / STEPS))
+    for j in range(landed_ref.shape[0] // ROWS):
+        codes = landed_ref[j * ROWS : (j + 1) * ROWS, :].astype(jnp.int32).astype(jnp.float32)
+        scale = jnp.exp2(codes[80:82, :] * (1 / STEPS))
         total += codes * jnp.abs(codes) * scale[1:2, :]
     total = total * TOP**-2
     rows[...] = jnp.zeros_like(rows)
@@ -406,14 +406,14 @@
 
     message = pl.pallas_call(
         functools.partial(outer_kernel, subs),
-        out_shape=shape((64, ROWS, CH), jnp.int16),
+        out_shape=shape((64 * ROWS, CH), jnp.int16),
         in_specs=[VMEM] * 9 + [HBM],
         out_specs=VMEM,
         scratch_shapes=[
             pltpu.VMEM((K, units * RIM), bf16),
             pltpu.VMEM((HALF, units * RIM), bf16),
             pltpu.VMEM((TAPS, HALF, CH), f32),
-            pltpu.VMEM((4, ROWS, CH), f32),
+            pltpu.VMEM((4, 88, CH), f32),
             pltpu.VMEM((8, CH), jnp.int32),
             pltpu.VMEM((units * CH // 2, 2 * CH), bf16),
             pltpu.VMEM((TAPS, HALF, CH), f32),
@@ -435,7 +435,7 @@
     )
 
     groups = [[f * samples + s for f in range(c, faces, 2) for s in range(samples)] for c in range(2)]
-    landed = lax.all_to_all(message, AXES, 0, 0, axis_index_groups=groups)
+    landed = lax.all_to_all(message.reshape(64, -1, 2, CH), AXES, 0, 0, axis_index_groups=groups).reshape(-1, CH)
     count = 2 * subs * PIX * faces * samples
     return pl.pallas_call(
         functools.partial(rows_kernel, count),

time: 63.7 us -> 63.1 us (level)
  blocking collectives: 29.9 us -> 28.9 us
    all_to_all x1, blocking collectives: 29.9 us -> 28.9 us  [per_device(): lax.all_to_all(message.reshape(64, -1, 2, CH), AXES, 0, 0, axis_index_gro...]
  transfers between devices with their start and end apart: 4 -> 4, of which waited for: 2 -> 2; matrix products, arithmetic and copies ran while one was open for 0% -> 0% of each run, Pallas kernels for 19% -> 20%
where the time goes in v8:
time: 63.1 us; the launch traced here: 62.8 us
  blocking collectives  28.9 us (46%)
  Pallas kernels  19 us (30%)
  starting transfers between devices  10.7 us (17%)
  waiting for transfers between devices  4.16 us (7%)
    all_to_all x1, blocking collectives, per_device(): lax.all_to_all(message.reshape(64, -1, 2, CH), AXES, 0, 0, axis_index_gro...  28.9 us
    pallas_call x1, Pallas kernels, per_device(): pl.pallas_call(inner_kernel, out_shape=(pltpu.HBM((TAPS, HALF, CH), f32),...  8.52 us
    all_to_all x1, starting transfers between devices, per_device(): table = lax.all_to_all(copies, 'face', 0, 0, axis_index_groups=same_core)  7.68 us
    pallas_call x1, Pallas kernels, per_device(): pl.pallas_call(functools.partial(outer_kernel, subs), out_shape=shape((64...  4.34 us
    all_to_all x1, waiting for transfers between devices, per_device(): table = lax.all_to_all(copies, 'face', 0, 0, axis_index_groups=same_core)  3.33 us
    pallas_call x1, Pallas kernels, per_device(): pl.pallas_call(edges_kernel, out_shape=shape((faces // 2, 8 * subs * SIDE...  2.22 us
    pallas_call x1, Pallas kernels, per_device(): pl.pallas_call(functools.partial(rows_kernel, count), out_shape=shape((9,...  1.62 us
    pallas_call x1, Pallas kernels, per_device(): pl.pallas_call(functools.partial(rim_kernel, subs), out_shape=(shape((K,...  1.55 us
  transfers between devices with their start and end apart: 4, of which 2 were waited for; matrix products, arithmetic and copies ran while one was open for 0% of the time, Pallas kernels for 20%

profile of v8, /device:TPU:1, one launch (start us, length us, event | category | flops | bytes accessed | tf_op | source)
XLA Modules:
  0.0 62.8 jit_solution(11578501907276935627)
XLA Ops:
  0.0 0.0 copy-start
  0.0 0.0 copy-start.4
  0.0 0.0 copy-start.3
  0.0 1.4 %collective-permute-start.1 = (bf16[3,3,128,256]{3,2,1,0:T(8,128)(2,1)}, bf16[3,3,128,256]{3,2,1,0:T(8,128)(2,1)S(1)}, u32[]{:S(2)}, u32[]{:S(2)}) collective-permute-start(bf16[3,3,128,256]{3,2,1,0:T(8,128)(2,1)} %fields_ref.1), channel_id=1, source_target_pairs={{0,8},{8,0},{16,24},{24,16},{32,40},{40,32},{48,56},{56,48},{64,72... | collective-permute-start | bytes 1769480 | tf_op jit(solution)/shard_map/ppermute | solution.py:345
  1.4 2.2 %edges.1 = bf16[8,384,128]{2,1,0:T(8,128)(2,1)} custom-call(s32[2]{0:T(128)} %index_ref.3, bf16[3,3,128,256]{3,2,1,0:T(8,128)(2,1)} %fields_ref.1), custom_call_target="tpu_custom_call" | custom-call | tf_op jit(solution)/shard_map/edges/pallas_call | solution.py:347
  3.7 7.7 %all-to-all-start = ((bf16[8,384,128]{2,1,0:T(8,128)(2,1)}), bf16[8,384,128]{2,1,0:T(8,128)(2,1)S(1)}, u32[]{:S(2)}, u32[]{:S(2)}) async-start(bf16[8,384,128]{2,1,0:T(8,128)(2,1)} %edges.1), calls=%async_computation | async-start | bytes 1572864 | tf_op jit(solution)/shard_map/all_to_all | solution.py:357
  11.3 0.0 copy-done.3
  11.3 0.4 collective-permute-start
  11.8 0.8 %collective-permute-done.halo_other_ref.halo_rows_other_ref = s32[3,68]{1,0:T(4,128)S(1)} collective-permute-done((s32[3,68]{1,0:T(4,128)S(1)}, s32[3,68]{1,0:T(4,128)S(1)}, u32[]{:S(2)}, u32[]{:S(2)}) %collective-permute-start) | collective-permute-done | bytes 848 | tf_op jit(solution)/shard_map/ppermute | solution.py:346
  12.6 0.0 collective-permute-done.1.other_ref
  12.6 0.0 copy-done
  12.6 0.0 copy-done.4
  12.6 8.5 %inner.1 = (f32[9,576,128]{2,1,0:T(8,128)}, bf16[768,512]{1,0:T(8,128)(2,1)S(1)}, s32[48]{0:T(128)S(1)}) custom-call(s32[2]{0:T(128)S(1)} %copy-done.4, s32[3,68]{1,0:T(4,128)S(1)} %copy-done.3, s32[3,68]{1,0:T(4,128)S(1)} %collective-permute-done.halo_other_ref.halo_rows_other_ref, bf16[3,3,128,256]{3,2,1,0:T(8,128)(2,1)S(1)} %copy-done, ...), custom_call_target="tpu_custom_call" | custom-call | flops 6000000000 | bytes 5000000 | tf_op jit(solution)/shard_map/inner/pallas_call | solution.py:360
  21.1 3.3 %all-to-all-done = bf16[8,384,128]{2,1,0:T(8,128)(2,1)S(1)} async-done(((bf16[8,384,128]{2,1,0:T(8,128)(2,1)}), bf16[8,384,128]{2,1,0:T(8,128)(2,1)S(1)}, u32[]{:S(2)}, u32[]{:S(2)}) %all-to-all-start) | async-done | bytes 786464 | tf_op jit(solution)/shard_map/all_to_all | solution.py:357
  24.5 0.8 %gather.1.after_ref.tiles_own_ref = bf16[1536,128]{1,0:T(8,128)(2,1)S(1)} custom-call(s32[48]{0:T(128)S(1)} %get-tuple-element.12.plan_ref, bf16[3072,128]{1,0:T(8,128)(2,1)S(1)} %bitcast.6), custom_call_target="tpu_custom_call" | custom-call | tf_op jit(solution)/shard_map/gather/pallas_call | solution.py:380
  25.2 1.1 %collective-permute-start.2 = (bf16[1536,128]{1,0:T(8,128)(2,1)S(1)}, bf16[1536,128]{1,0:T(8,128)(2,1)S(1)}, u32[]{:S(2)}, u32[]{:S(2)}) collective-permute-start(bf16[1536,128]{1,0:T(8,128)(2,1)S(1)} %gather.1.after_ref.tiles_own_ref), channel_id=1, source_target_pairs={{0,8},{8,0},{16,24},{24,16},{32,40},{40,32},{48,56},{56,48},{64,72... | collective-permute-start | bytes 1179656 | tf_op jit(solution)/shard_map/ppermute | solution.py:388
  26.4 0.0 copy-start.2
  26.4 1.5 %rim.1 = (bf16[1152,768]{1,0:T(8,128)(2,1)S(1)}, bf16[256,1152]{1,0:T(8,128)(2,1)S(1)}, f32[128,128]{1,0:T(8,128)S(1)}, f32[4,576,128]{2,1,0:T(8,128)S(1)}) custom-call(bf16[768,512]{1,0:T(8,128)(2,1)S(1)} %get-tuple-element.13.pairs_ref, bf16[1536,128]{1,0:T(8,128)(2,1)S(1)} %gather.1.after_ref.tiles_own_ref, f32[9,576,128]{2,1,0:T(8,128)} %get-tuple-element.14.inner_ref), custom_call_target="tpu_custom_call" | custom-call | flops 1000000000 | bytes 6000000 | tf_op jit(solution)/shard_map/rim/pallas_call | solution.py:391
  27.9 0.0 collective-permute-done.2.tiles_other_ref
  27.9 0.0 copy-done.2
  27.9 4.3 %outer.1 = s16[5248,128]{1,0:T(8,128)(2,1)S(1)} custom-call(bf16[1536,128]{1,0:T(8,128)(2,1)S(1)} %gather.1.after_ref.tiles_own_ref, bf16[1536,128]{1,0:T(8,128)(2,1)S(1)} %collective-permute-done.2.tiles_other_ref, s32[3,68]{1,0:T(4,128)S(1)} %copy-done.3, s32[3,68]{1,0:T(4,128)S(1)} %collective-permute-done.halo_other_ref.halo_rows_other_ref, ...), custom_call_target="tpu_custom_call" | custom-call | tf_op jit(solution)/shard_map/outer/pallas_call | solution.py:407
  32.3 0.0 copy-start.1
  32.3 28.9 %all_to_all.10 = s16[64,41,2,128]{3,2,1,0:T(2,128)(2,1)S(1)} all-to-all(s16[64,41,2,128]{3,2,1,0:T(2,128)(2,1)S(1)} %bitcast.5), channel_id=1, replica_groups={{0,1,2,3,4,5,6,7,16,17,18,19,20,21,22,23,32,33,34,35,36,37,38,39,48,49,..., dimensions={0} | all-to-all | bytes 2686976 | tf_op jit(solution)/shard_map/all_to_all | solution.py:438
  61.2 0.0 copy-done.1
  61.2 1.6 %rows.1 = f32[9,1408]{1,0:T(8,128)} custom-call(s16[5248,128]{1,0:T(8,128)(2,1)S(1)} %bitcast.4, bf16[1152,256]{1,0:T(8,128)(2,1)S(1)} %copy-done.1, s32[1,128]{1,0:T(1,128)S(1)} %bitcast.8), custom_call_target="tpu_custom_call" | custom-call | tf_op jit(solution)/shard_map/rows/pallas_call | solution.py:440
Async XLA Ops:
  0.0 12.6 %copy-start = (bf16[3,3,128,256]{3,2,1,0:T(8,128)(2,1)S(1)}, bf16[3,3,128,256]{3,2,1,0:T(8,128)(2,1)}, u32[]{:S(2)}) copy-start(bf16[3,3,128,256]{3,2,1,0:T(8,128)(2,1)} %fields_ref.1) | copy-start | bytes 1769476
  0.0 12.6 %copy-start.4 = (s32[2]{0:T(128)S(1)}, s32[2]{0:T(128)}, u32[]{:S(2)}) copy-start(s32[2]{0:T(128)} %index_ref.3) | copy-start | bytes 28
  0.0 11.3 %copy-start.3 = (s32[3,68]{1,0:T(4,128)S(1)}, s32[3,68]{1,0:T(4,128)}, u32[]{:S(2)}) copy-start(s32[3,68]{1,0:T(4,128)} %halo_rows_own_ref.1) | copy-start | bytes 2452
  0.0 12.6 %collective-permute-start.1 = (bf16[3,3,128,256]{3,2,1,0:T(8,128)(2,1)}, bf16[3,3,128,256]{3,2,1,0:T(8,128)(2,1)S(1)}, u32[]{:S(2)}, u32[]{:S(2)}) collective-permute-start(bf16[3,3,128,256]{3,2,1,0:T(8,128)(2,1)} %fields_ref.1), channel_id=1, source_target_pairs={{0,8},{8,0},{16,24},{24,16},{32,40},{40,32},{48,56},{56,48},{64,72... | collective-permute-start | bytes 1769480 | tf_op jit(solution)/shard_map/ppermute | solution.py:345
  3.7 20.8 %all-to-all-start = ((bf16[8,384,128]{2,1,0:T(8,128)(2,1)}), bf16[8,384,128]{2,1,0:T(8,128)(2,1)S(1)}, u32[]{:S(2)}, u32[]{:S(2)}) async-start(bf16[8,384,128]{2,1,0:T(8,128)(2,1)} %edges.1), calls=%async_computation | async-start | bytes 1572864 | tf_op jit(solution)/shard_map/all_to_all | solution.py:357
  11.3 1.2 %collective-permute-start = (s32[3,68]{1,0:T(4,128)S(1)}, s32[3,68]{1,0:T(4,128)S(1)}, u32[]{:S(2)}, u32[]{:S(2)}) collective-permute-start(s32[3,68]{1,0:T(4,128)S(1)} %copy-done.3), channel_id=1, source_target_pairs={{0,8},{8,0},{16,24},{24,16},{32,40},{40,32},{48,56},{56,48},{64,72... | collective-permute-start | bytes 2456 | tf_op jit(solution)/shard_map/ppermute | solution.py:346
  25.2 2.7 %collective-permute-start.2 = (bf16[1536,128]{1,0:T(8,128)(2,1)S(1)}, bf16[1536,128]{1,0:T(8,128)(2,1)S(1)}, u32[]{:S(2)}, u32[]{:S(2)}) collective-permute-start(bf16[1536,128]{1,0:T(8,128)(2,1)S(1)} %gather.1.after_ref.tiles_own_ref), channel_id=1, source_target_pairs={{0,8},{8,0},{16,24},{24,16},{32,40},{40,32},{48,56},{56,48},{64,72... | collective-permute-start | bytes 1179656 | tf_op jit(solution)/shard_map/ppermute | solution.py:388
  26.4 1.6 %copy-start.2 = (s32[128]{0:T(128)S(1)}, s32[128]{0:T(128)}, u32[]{:S(2)}) copy-start(s32[128]{0:T(128)} %param.8) | copy-start | bytes 1540
  32.3 28.9 %copy-start.1 = (bf16[1152,256]{1,0:T(8,128)(2,1)S(1)}, bf16[1152,256]{1,0:T(8,128)(2,1)}, u32[]{:S(2)}) copy-start(bf16[1152,256]{1,0:T(8,128)(2,1)} %weight_ref.1) | copy-start | bytes 1769476

commit v9 on v8

--- a/solution.py
+++ b/solution.py
@@ -22,6 +22,7 @@
 STEPS = 16
 TOP = 32700.0
 THIRD = 43
+GROUP = 4
 AXES = ("face", "sample")
 NT = (((1,), (1,)), ((), ()))
 SIDE_AT = (1, 19, 36, 52)
@@ -99,13 +100,10 @@
 
 def inner_kernel(
     index_ref,
-    halo_own_ref,
-    halo_other_ref,
     own_ref,
     other_ref,
     gram_ref,
     pairs_ref,
-    plan_ref,
     patches,
     owned,
     gram,
@@ -114,20 +112,13 @@
     subs = own_ref.shape[1]
     core = core_index()
 
-    for side, halo_ref in enumerate((halo_own_ref, halo_other_ref)):
-        for f in range(subs):
-            for n, at in enumerate(SIDE_AT + CORNER_AT):
-                index = halo_ref[f, at]
-                sub = lax.shift_right_logical(index, 6)
-                device = lax.shift_right_logical(sub * THIRD, 7)
-                row = (lax.shift_right_logical(device, 1) * 2 * subs + sub - device * subs) * 4 * SIDE
-                row += index & (3 * SIDE)
-                plan_ref[(side * subs + f) * 8 + n] = jnp.where((device & 1) == core, row, -SIDE)
-
+    index = index_ref[...]
     for s in range(2):
+        rows = slice(s * subs * CH, (s + 1) * subs * CH)
+        chosen = [(index[:, s : s + 1] == n).astype(jnp.float32).astype(jnp.bfloat16) for n in range(own_ref.shape[0])]
         for n, ref in enumerate((own_ref, other_ref)):
-            rows = slice(s * subs * CH, (s + 1) * subs * CH)
-            pairs_ref[rows, n * PIX : (n + 1) * PIX] = ref[index_ref[s]].reshape(subs * CH, PIX)
+            parts = [ref[k].reshape(subs * CH, PIX) * one for k, one in enumerate(chosen)]
+            pairs_ref[rows, n * PIX : (n + 1) * PIX] = sum(parts[1:], parts[0])
 
     row_at = lax.broadcasted_iota(jnp.int32, (PIX, PIX), 0)
     place = lax.broadcasted_iota(jnp.int32, (8, PIX), 1)
@@ -137,8 +128,12 @@
         taps = [jnp.where(d == shift, 1.0, 0.0).astype(jnp.bfloat16) for d in ahead]
         for s in range(2):
             first, second = (
-                jnp.dot(ref[index_ref[s]].reshape(subs * CH, PIX), tap, preferred_element_type=jnp.float32)
-                for ref, tap in zip((own_ref, other_ref), taps)
+                jnp.dot(
+                    pairs_ref[s * subs * CH : (s + 1) * subs * CH, n * PIX : (n + 1) * PIX],
+                    tap,
+                    preferred_element_type=jnp.float32,
+                )
+                for n, tap in enumerate(taps)
             )
             columns = (first[:, :CH], first[:, CH:] + second[:, :CH], second[:, CH:])
             for n, values in enumerate(columns):
@@ -159,17 +154,21 @@
         copy.wait()
 
 
-def gather_kernel(subs, plan_ref, table_ref, tiles_ref):
+def gather_kernel(subs, halo_own_ref, halo_other_ref, table_ref, after_ref, tiles_ref):
+    core = core_index()
     zero = jnp.zeros((SIDE, CH), jnp.bfloat16)
-    for f in range(2 * subs):
-        for n in range(8):
-            row = plan_ref[f * 8 + n]
-            near = row >= 0
-            row = jnp.maximum(row, 0)
-            for s in range(2):
-                at = pl.multiple_of(row + s * subs * 4 * SIDE, SIDE)
-                u = (f // subs * 2 + s) * subs + f % subs
-                tiles_ref[u * CH + n * SIDE : u * CH + (n + 1) * SIDE, :] = jnp.where(near, table_ref[pl.ds(at, SIDE), :], zero)
+    for side, halo_ref in enumerate((halo_own_ref, halo_other_ref)):
+        for f in range(subs):
+            for n, at in enumerate(SIDE_AT + CORNER_AT):
+                index = halo_ref[f, at]
+                sub = lax.shift_right_logical(index, 6)
+                device = lax.shift_right_logical(sub * THIRD, 7)
+                row = (lax.shift_right_logical(device, 1) * 2 * subs + sub - device * subs) * 4 * SIDE
+                row = pl.multiple_of(row + (index & (3 * SIDE)), SIDE)
+                for s in range(2):
+                    u = (side * 2 + s) * subs + f
+                    tile = table_ref[pl.ds(pl.multiple_of(row + s * subs * 4 * SIDE, SIDE), SIDE), :]
+                    tiles_ref[u * CH + n * SIDE : u * CH + (n + 1) * SIDE, :] = jnp.where((device & 1) == core, tile, zero)
 
 
 def rim_kernel(subs, pairs_ref, after_ref, inner_ref, rim_ref, matrix_ref, energy_ref, gram_ref, pixels, sem):
@@ -268,36 +267,42 @@
     kept_exp = exponent(jnp.where(kept_row > 0, energy, 0.0))
     any_exp = exponent(energy)
     lane_exps = jnp.where(kept > 0, kept_exp, any_exp) + kept_exp
-    scale = jnp.exp2(lane_exps * (-1 / STEPS))
+    scale = jnp.exp2(lane_exps * (-1 / STEPS)) * TOP**2
 
     def coded(values):
-        return jnp.round(TOP * values * lax.rsqrt(jnp.maximum(jnp.abs(values), 1e-30)))
+        return jnp.round(values * lax.rsqrt(jnp.maximum(jnp.abs(values), 1e-30)))
 
     owned_rows(core, patches, owned)
-    for n, taps in enumerate(tap_blocks()):
-        right = patches[taps.start * CH : taps.stop * CH, :]
-        block = lax.dot_general(owned[...], right, NT, preferred_element_type=jnp.float32)
-        if n > 0:
-            copies[n - 1].wait()
-        for l in range(taps.stop - taps.start):
-            part = block[:, l * CH : (l + 1) * CH] + (inner if n > 0 else first_ref)[taps.start + l, :, :]
-            gram[taps.start + l, :, :] = coded(part * scale[0:1, :])
-
-    for j in range(message_ref.shape[0] // ROWS):
-        block = stage.at[j % 4]
-        for l in range(TAPS):
-            block[l * 9 : (l + 1) * 9, :] = gram[l, j * 9 : (j + 1) * 9, :]
-        block[81:88, :] = lane_exps[0:7, :]
-        message_ref[j * ROWS : (j + 1) * ROWS, :] = block[:ROWS, :].astype(jnp.int32).astype(jnp.int16)
-
-
-def rows_kernel(count, landed_ref, weight_ref, kept_ref, out_ref, rows, split):
+    for m in range(0, HALF, HALF // 2):
+        at = slice(m, m + HALF // 2)
+        for n, taps in enumerate(tap_blocks()):
+            right = patches[taps.start * CH : taps.stop * CH, :]
+            block = lax.dot_general(owned[at, :], right, NT, preferred_element_type=jnp.float32)
+            if n > 0 and m == 0:
+                copies[n - 1].wait()
+            for l in range(taps.stop - taps.start):
+                part = block[:, l * CH : (l + 1) * CH] + (inner if n > 0 else first_ref)[taps.start + l, at, :]
+                gram[taps.start + l, at, :] = coded(part * scale[0:1, :])
+
+        for j in range(m // 9, (m + HALF // 2) // 9, GROUP):
+            block = stage.at[j // GROUP % 4]
+            for i in range(GROUP):
+                for l in range(TAPS):
+                    to = i * ROWS + l * 9
+                    block[to : to + 9, :] = gram[l, (j + i) * 9 : (j + i + 1) * 9, :]
+                block[i * ROWS + 81 : (i + 1) * ROWS, :] = lane_exps[0:1, :]
+            message_ref[j * ROWS : (j + GROUP) * ROWS, :] = block[...].astype(jnp.int32).astype(jnp.int16)
+
+
+def rows_kernel(count, landed_ref, weight_ref, kept_ref, out_ref, rows, split, stage):
     owner = lax.axis_index("face") * lax.axis_size("sample") + lax.axis_index("sample")
     total = jnp.zeros((ROWS, CH), jnp.float32)
-    for j in range(landed_ref.shape[0] // ROWS):
-        codes = landed_ref[j * ROWS : (j + 1) * ROWS, :].astype(jnp.int32).astype(jnp.float32)
-        scale = jnp.exp2(codes[80:82, :] * (1 / STEPS))
-        total += codes * jnp.abs(codes) * scale[1:2, :]
+    for j in range(0, landed_ref.shape[0] // ROWS, 2 * GROUP):
+        block = stage.at[j // (2 * GROUP) % 4]
+        block[...] = landed_ref[j * ROWS : (j + 2 * GROUP) * ROWS, :].astype(jnp.int32).astype(jnp.float32)
+        for i in range(2 * GROUP):
+            codes = block[i * ROWS : (i + 1) * ROWS, :]
+            total += codes * jnp.abs(codes) * jnp.exp2(block[i * ROWS + 81 : (i + 1) * ROWS, :] * (1 / STEPS))
     total = total * TOP**-2
     rows[...] = jnp.zeros_like(rows)
     for l in range(TAPS):
@@ -329,6 +334,7 @@
 VMEM = pl.BlockSpec(memory_space=pltpu.VMEM)
 SMEM = pl.BlockSpec(memory_space=pltpu.SMEM)
 HBM = pl.BlockSpec(memory_space=pltpu.HBM)
+ANY = pl.BlockSpec(memory_space=pl.ANY)
 
 
 def shape(dims, kind):
@@ -357,15 +363,14 @@
     table = lax.all_to_all(copies, "face", 0, 0, axis_index_groups=same_core)
 
     mask_row = channel_mask[None]
-    inner, pairs, plan = pl.pallas_call(
+    inner, pairs = pl.pallas_call(
         inner_kernel,
         out_shape=(
             pltpu.HBM((TAPS, HALF, CH), f32),
             shape((units * CH // 2, 2 * PIX), bf16),
-            shape((2 * subs * 8,), jnp.int32),
         ),
-        in_specs=[SMEM] * 3 + [VMEM] * 2,
-        out_specs=(HBM, VMEM, SMEM),
+        in_specs=[VMEM] * 3,
+        out_specs=(HBM, VMEM),
         scratch_shapes=[
             pltpu.VMEM((K, units * INNER), bf16),
             pltpu.VMEM((HALF, units * INNER), bf16),
@@ -375,16 +380,16 @@
         compiler_params=pltpu.CompilerParams(vmem_limit_bytes=32 * 2**20),
         cost_estimate=pl.CostEstimate(flops=6 * 10**9, bytes_accessed=5 * 10**6, transcendentals=0),
         name="inner",
-    )(sample_index, halo_index, halo_other, fields, other)
+    )(sample_index[None], fields, other)
 
     tiles = pl.pallas_call(
         functools.partial(gather_kernel, subs),
         out_shape=shape((units * CH, CH), bf16),
-        in_specs=[SMEM, VMEM],
+        in_specs=[SMEM, SMEM, VMEM, ANY],
         out_specs=VMEM,
         compiler_params=pltpu.CompilerParams(vmem_limit_bytes=4 * 2**20),
         name="gather",
-    )(plan, table.reshape(-1, CH))
+    )(halo_index, halo_other, table.reshape(-1, CH), pairs)
     tiles_other = lax.ppermute(tiles, "face", swap)
 
     inner = pltpu.with_memory_space_constraint(inner, pltpu.HBM)
@@ -396,7 +401,7 @@
             shape((CH, CH), f32),
             shape((tap_blocks()[0].stop, HALF, CH), f32),
         ),
-        in_specs=[VMEM, pl.BlockSpec(memory_space=pl.ANY), HBM],
+        in_specs=[VMEM, ANY, HBM],
         out_specs=(VMEM, VMEM, VMEM, VMEM),
         scratch_shapes=[pltpu.VMEM((2 * PIX, K), bf16), pltpu.SemaphoreType.DMA],
         compiler_params=pltpu.CompilerParams(vmem_limit_bytes=16 * 2**20),
@@ -413,7 +418,7 @@
             pltpu.VMEM((K, units * RIM), bf16),
             pltpu.VMEM((HALF, units * RIM), bf16),
             pltpu.VMEM((TAPS, HALF, CH), f32),
-            pltpu.VMEM((4, 88, CH), f32),
+            pltpu.VMEM((4, GROUP * ROWS, CH), f32),
             pltpu.VMEM((8, CH), jnp.int32),
             pltpu.VMEM((units * CH // 2, 2 * CH), bf16),
             pltpu.VMEM((TAPS, HALF, CH), f32),
@@ -442,7 +447,7 @@
         out_shape=shape((9, K + weight.shape[1]), f32),
         in_specs=[VMEM] * 3,
         out_specs=VMEM,
-        scratch_shapes=[pltpu.VMEM((16, K), f32), pltpu.VMEM((48, K), bf16)],
+        scratch_shapes=[pltpu.VMEM((16, K), f32), pltpu.VMEM((48, K), bf16), pltpu.VMEM((4, 2 * GROUP * ROWS, CH), f32)],
         compiler_params=pltpu.CompilerParams(vmem_limit_bytes=8 * 2**20),
         name="rows",
     )(landed, weight, mask_row)

time: 63.1 us -> 62.5 us (level)
  Pallas kernels: 19 us -> 17.1 us
  waiting for transfers between devices: 4.16 us -> 5.51 us
    all_to_all x1, waiting for transfers between devices: 3.33 us -> 5.5 us  [per_device(): table = lax.all_to_all(copies, 'face', 0, 0, axis_index_groups=same_core)]
    pallas_call x1, Pallas kernels: 8.52 us -> 7.16 us  [per_device(): pl.pallas_call(inner_kernel, out_shape=(pltpu.HBM((TAPS, HALF, CH), f32),...]
    ppermute x1, waiting for transfers between devices: 0.82 us -> 0.01 us  [per_device(): halo_other = lax.ppermute(halo_index, 'face', swap)]
  transfers between devices with their start and end apart: 4 -> 4, of which waited for: 2 -> 1; matrix products, arithmetic and copies ran while one was open for 0% -> 0% of each run, Pallas kernels for 20% -> 18%
where the time goes in v9:
time: 62.5 us; the launch traced here: 62.3 us
  blocking collectives  28.9 us (46%)
  Pallas kernels  17.1 us (27%)
  starting transfers between devices  10.7 us (17%)
  waiting for transfers between devices  5.51 us (9%)
    all_to_all x1, blocking collectives, per_device(): lax.all_to_all(message.reshape(64, -1, 2, CH), AXES, 0, 0, axis_index_gro...  28.9 us
    all_to_all x1, starting transfers between devices, per_device(): table = lax.all_to_all(copies, 'face', 0, 0, axis_index_groups=same_core)  7.68 us
    pallas_call x1, Pallas kernels, per_device(): pl.pallas_call(inner_kernel, out_shape=(pltpu.HBM((TAPS, HALF, CH), f32),...  7.16 us
    all_to_all x1, waiting for transfers between devices, per_device(): table = lax.all_to_all(copies, 'face', 0, 0, axis_index_groups=same_core)  5.5 us
    pallas_call x1, Pallas kernels, per_device(): pl.pallas_call(functools.partial(outer_kernel, subs), out_shape=shape((64...  3.76 us
    pallas_call x1, Pallas kernels, per_device(): pl.pallas_call(edges_kernel, out_shape=shape((faces // 2, 8 * subs * SIDE...  2.22 us
    pallas_call x1, Pallas kernels, per_device(): pl.pallas_call(functools.partial(rim_kernel, subs), out_shape=(shape((K,...  1.55 us
    pallas_call x1, Pallas kernels, per_device(): pl.pallas_call(functools.partial(rows_kernel, count), out_shape=shape((9,...  1.48 us
  transfers between devices with their start and end apart: 4, of which 1 were waited for; matrix products, arithmetic and copies ran while one was open for 0% of the time, Pallas kernels for 18%

profile of v9, /device:TPU:1, one launch (start us, length us, event | category | flops | bytes accessed | tf_op | source)
XLA Modules:
  0.0 62.3 jit_solution(6140385337257555304)
XLA Ops:
  0.0 0.0 copy-start
  0.0 0.0 copy-start.4
  0.0 0.0 copy-start.2
  0.0 1.4 %collective-permute-start.1 = (bf16[3,3,128,256]{3,2,1,0:T(8,128)(2,1)}, bf16[3,3,128,256]{3,2,1,0:T(8,128)(2,1)S(1)}, u32[]{:S(2)}, u32[]{:S(2)}) collective-permute-start(bf16[3,3,128,256]{3,2,1,0:T(8,128)(2,1)} %own_ref.1), channel_id=1, source_target_pairs={{0,8},{8,0},{16,24},{24,16},{32,40},{40,32},{48,56},{56,48},{64,72... | collective-permute-start | bytes 1769480 | tf_op jit(solution)/shard_map/ppermute | solution.py:351
  1.4 2.2 %edges.1 = bf16[8,384,128]{2,1,0:T(8,128)(2,1)} custom-call(s32[2]{0:T(128)} %index_ref.1, bf16[3,3,128,256]{3,2,1,0:T(8,128)(2,1)} %own_ref.1), custom_call_target="tpu_custom_call" | custom-call | tf_op jit(solution)/shard_map/edges/pallas_call | solution.py:353
  3.7 7.7 %all-to-all-start = ((bf16[8,384,128]{2,1,0:T(8,128)(2,1)}), bf16[8,384,128]{2,1,0:T(8,128)(2,1)S(1)}, u32[]{:S(2)}, u32[]{:S(2)}) async-start(bf16[8,384,128]{2,1,0:T(8,128)(2,1)} %edges.1), calls=%async_computation | async-start | bytes 1572864 | tf_op jit(solution)/shard_map/all_to_all | solution.py:363
  11.3 0.0 copy-done.2
  11.3 0.4 collective-permute-start
  11.8 0.0 collective-permute-done.1.other_ref
  11.8 0.0 copy-done
  11.8 0.0 copy-done.4
  11.8 7.2 %inner.1 = (f32[9,576,128]{2,1,0:T(8,128)}, bf16[768,512]{1,0:T(8,128)(2,1)S(1)}) custom-call(s32[1,2]{1,0:T(1,128)S(1)} %bitcast.10, bf16[3,3,128,256]{3,2,1,0:T(8,128)(2,1)S(1)} %copy-done, bf16[3,3,128,256]{3,2,1,0:T(8,128)(2,1)S(1)} %collective-permute-done.1.other_ref), custom_call_target="tpu_custom_call" | custom-call | flops 6000000000 | bytes 5000000 | tf_op jit(solution)/shard_map/inner/pallas_call | solution.py:366
  18.9 0.0 collective-permute-done.halo_other_ref.halo_rows_other_ref
  19.0 5.5 %all-to-all-done = bf16[8,384,128]{2,1,0:T(8,128)(2,1)S(1)} async-done(((bf16[8,384,128]{2,1,0:T(8,128)(2,1)}), bf16[8,384,128]{2,1,0:T(8,128)(2,1)S(1)}, u32[]{:S(2)}, u32[]{:S(2)}) %all-to-all-start) | async-done | bytes 786464 | tf_op jit(solution)/shard_map/all_to_all | solution.py:363
  24.5 0.9 %gather.1.after_ref.tiles_own_ref = bf16[1536,128]{1,0:T(8,128)(2,1)S(1)} custom-call(s32[3,68]{1,0:T(4,128)S(1)} %copy-done.2, s32[3,68]{1,0:T(4,128)S(1)} %collective-permute-done.halo_other_ref.halo_rows_other_ref, bf16[3072,128]{1,0:T(8,128)(2,1)S(1)} %bitcast.7, bf16[768,512]{1,0:T(8,128)(2,1)S(1)} %get-tuple-element.11.after_ref.pairs_ref), custom_call_target="tpu_custom_call" | custom-call | tf_op jit(solution)/shard_map/gather/pallas_call | solution.py:385
  25.4 1.1 %collective-permute-start.2 = (bf16[1536,128]{1,0:T(8,128)(2,1)S(1)}, bf16[1536,128]{1,0:T(8,128)(2,1)S(1)}, u32[]{:S(2)}, u32[]{:S(2)}) collective-permute-start(bf16[1536,128]{1,0:T(8,128)(2,1)S(1)} %gather.1.after_ref.tiles_own_ref), channel_id=1, source_target_pairs={{0,8},{8,0},{16,24},{24,16},{32,40},{40,32},{48,56},{56,48},{64,72... | collective-permute-start | bytes 1179656 | tf_op jit(solution)/shard_map/ppermute | solution.py:393
  26.5 0.0 copy-start.3
  26.5 1.5 %rim.1 = (bf16[1152,768]{1,0:T(8,128)(2,1)S(1)}, bf16[256,1152]{1,0:T(8,128)(2,1)S(1)}, f32[128,128]{1,0:T(8,128)S(1)}, f32[4,576,128]{2,1,0:T(8,128)S(1)}) custom-call(bf16[768,512]{1,0:T(8,128)(2,1)S(1)} %get-tuple-element.11.after_ref.pairs_ref, bf16[1536,128]{1,0:T(8,128)(2,1)S(1)} %gather.1.after_ref.tiles_own_ref, ...), custom_call_target="tpu_custom_call" | custom-call | flops 1000000000 | bytes 6000000 | tf_op jit(solution)/shard_map/rim/pallas_call | solution.py:396
  28.1 0.0 collective-permute-done.2.tiles_other_ref
  28.1 0.0 copy-done.3
  28.1 3.8 %outer.1 = s16[5248,128]{1,0:T(8,128)(2,1)S(1)} custom-call(bf16[1536,128]{1,0:T(8,128)(2,1)S(1)} %gather.1.after_ref.tiles_own_ref, bf16[1536,128]{1,0:T(8,128)(2,1)S(1)} %collective-permute-done.2.tiles_other_ref, s32[3,68]{1,0:T(4,128)S(1)} %copy-done.2, s32[3,68]{1,0:T(4,128)S(1)} %collective-permute-done.halo_other_ref.halo_rows_other_ref, ...), custom_call_target="tpu_custom_call" | custom-call | tf_op jit(solution)/shard_map/outer/pallas_call | solution.py:412
  31.9 0.0 copy-start.1
  31.9 28.9 %all_to_all.10 = s16[64,41,2,128]{3,2,1,0:T(2,128)(2,1)S(1)} all-to-all(s16[64,41,2,128]{3,2,1,0:T(2,128)(2,1)S(1)} %bitcast.6), channel_id=1, replica_groups={{0,1,2,3,4,5,6,7,16,17,18,19,20,21,22,23,32,33,34,35,36,37,38,39,48,49,..., dimensions={0} | all-to-all | bytes 2686976 | tf_op jit(solution)/shard_map/all_to_all | solution.py:443
  60.8 0.0 copy-done.1
  60.8 1.5 %rows.1 = f32[9,1408]{1,0:T(8,128)} custom-call(s16[5248,128]{1,0:T(8,128)(2,1)S(1)} %bitcast.5, bf16[1152,256]{1,0:T(8,128)(2,1)S(1)} %copy-done.1, s32[1,128]{1,0:T(1,128)S(1)} %bitcast.9), custom_call_target="tpu_custom_call" | custom-call | tf_op jit(solution)/shard_map/rows/pallas_call | solution.py:445
Async XLA Ops:
  0.0 11.8 %copy-start = (bf16[3,3,128,256]{3,2,1,0:T(8,128)(2,1)S(1)}, bf16[3,3,128,256]{3,2,1,0:T(8,128)(2,1)}, u32[]{:S(2)}) copy-start(bf16[3,3,128,256]{3,2,1,0:T(8,128)(2,1)} %own_ref.1) | copy-start | bytes 1769476
  0.0 11.8 %copy-start.4 = (s32[2]{0:T(128)S(1)}, s32[2]{0:T(128)}, u32[]{:S(2)}) copy-start(s32[2]{0:T(128)} %index_ref.1) | copy-start | bytes 28
  0.0 11.3 %copy-start.2 = (s32[3,68]{1,0:T(4,128)S(1)}, s32[3,68]{1,0:T(4,128)}, u32[]{:S(2)}) copy-start(s32[3,68]{1,0:T(4,128)} %halo_rows_own_ref.1) | copy-start | bytes 2452
  0.0 11.8 %collective-permute-start.1 = (bf16[3,3,128,256]{3,2,1,0:T(8,128)(2,1)}, bf16[3,3,128,256]{3,2,1,0:T(8,128)(2,1)S(1)}, u32[]{:S(2)}, u32[]{:S(2)}) collective-permute-start(bf16[3,3,128,256]{3,2,1,0:T(8,128)(2,1)} %own_ref.1), channel_id=1, source_target_pairs={{0,8},{8,0},{16,24},{24,16},{32,40},{40,32},{48,56},{56,48},{64,72... | collective-permute-start | bytes 1769480 | tf_op jit(solution)/shard_map/ppermute | solution.py:351
  3.7 20.8 %all-to-all-start = ((bf16[8,384,128]{2,1,0:T(8,128)(2,1)}), bf16[8,384,128]{2,1,0:T(8,128)(2,1)S(1)}, u32[]{:S(2)}, u32[]{:S(2)}) async-start(bf16[8,384,128]{2,1,0:T(8,128)(2,1)} %edges.1), calls=%async_computation | async-start | bytes 1572864 | tf_op jit(solution)/shard_map/all_to_all | solution.py:363
  11.3 7.6 %collective-permute-start = (s32[3,68]{1,0:T(4,128)S(1)}, s32[3,68]{1,0:T(4,128)S(1)}, u32[]{:S(2)}, u32[]{:S(2)}) collective-permute-start(s32[3,68]{1,0:T(4,128)S(1)} %copy-done.2), channel_id=1, source_target_pairs={{0,8},{8,0},{16,24},{24,16},{32,40},{40,32},{48,56},{56,48},{64,72... | collective-permute-start | bytes 2456 | tf_op jit(solution)/shard_map/ppermute | solution.py:352
  25.4 2.7 %collective-permute-start.2 = (bf16[1536,128]{1,0:T(8,128)(2,1)S(1)}, bf16[1536,128]{1,0:T(8,128)(2,1)S(1)}, u32[]{:S(2)}, u32[]{:S(2)}) collective-permute-start(bf16[1536,128]{1,0:T(8,128)(2,1)S(1)} %gather.1.after_ref.tiles_own_ref), channel_id=1, source_target_pairs={{0,8},{8,0},{16,24},{24,16},{32,40},{40,32},{48,56},{56,48},{64,72... | collective-permute-start | bytes 1179656 | tf_op jit(solution)/shard_map/ppermute | solution.py:393
  26.5 1.6 %copy-start.3 = (s32[128]{0:T(128)S(1)}, s32[128]{0:T(128)}, u32[]{:S(2)}) copy-start(s32[128]{0:T(128)} %param.8) | copy-start | bytes 1540
  31.9 28.9 %copy-start.1 = (bf16[1152,256]{1,0:T(8,128)(2,1)S(1)}, bf16[1152,256]{1,0:T(8,128)(2,1)}, u32[]{:S(2)}) copy-start(bf16[1152,256]{1,0:T(8,128)(2,1)} %weight_ref.1) | copy-start | bytes 1769476

commit v10 on v9

--- a/solution.py
+++ b/solution.py
@@ -273,16 +273,21 @@
         return jnp.round(values * lax.rsqrt(jnp.maximum(jnp.abs(values), 1e-30)))
 
     owned_rows(core, patches, owned)
+
+    def add_block(n, at):
+        taps = tap_blocks()[n]
+        right = patches[taps.start * CH : taps.stop * CH, :]
+        block = lax.dot_general(owned[at, :], right, NT, preferred_element_type=jnp.float32)
+        if n > 0 and at.start == 0:
+            copies[n - 1].wait()
+        for l in range(taps.stop - taps.start):
+            part = block[:, l * CH : (l + 1) * CH] + (inner if n > 0 else first_ref)[taps.start + l, at, :]
+            gram[taps.start + l, at, :] = coded(part * scale[0:1, :])
+
+    add_block(0, slice(0, HALF))
     for m in range(0, HALF, HALF // 2):
-        at = slice(m, m + HALF // 2)
-        for n, taps in enumerate(tap_blocks()):
-            right = patches[taps.start * CH : taps.stop * CH, :]
-            block = lax.dot_general(owned[at, :], right, NT, preferred_element_type=jnp.float32)
-            if n > 0 and m == 0:
-                copies[n - 1].wait()
-            for l in range(taps.stop - taps.start):
-                part = block[:, l * CH : (l + 1) * CH] + (inner if n > 0 else first_ref)[taps.start + l, at, :]
-                gram[taps.start + l, at, :] = coded(part * scale[0:1, :])
+        add_block(1, slice(m, m + HALF // 2))
+        add_block(2, slice(m, m + HALF // 2))
 
         for j in range(m // 9, (m + HALF // 2) // 9, GROUP):
             block = stage.at[j // GROUP % 4]

time: 62.5 us -> 62.4 us (level)
  no operation moved by 1% of the time
where the time goes in v10:
time: 62.4 us; the launch traced here: 62.1 us
  blocking collectives  28.9 us (46%)
  Pallas kernels  17 us (27%)
  starting transfers between devices  10.7 us (17%)
  waiting for transfers between devices  5.51 us (9%)
    all_to_all x1, blocking collectives, per_device(): lax.all_to_all(message.reshape(64, -1, 2, CH), AXES, 0, 0, axis_index_gro...  28.9 us
    all_to_all x1, starting transfers between devices, per_device(): table = lax.all_to_all(copies, 'face', 0, 0, axis_index_groups=same_core)  7.68 us
    pallas_call x1, Pallas kernels, per_device(): pl.pallas_call(inner_kernel, out_shape=(pltpu.HBM((TAPS, HALF, CH), f32),...  7.16 us
    all_to_all x1, waiting for transfers between devices, per_device(): table = lax.all_to_all(copies, 'face', 0, 0, axis_index_groups=same_core)  5.5 us
    pallas_call x1, Pallas kernels, per_device(): pl.pallas_call(functools.partial(outer_kernel, subs), out_shape=shape((64...  3.64 us
    pallas_call x1, Pallas kernels, per_device(): pl.pallas_call(edges_kernel, out_shape=shape((faces // 2, 8 * subs * SIDE...  2.22 us
    pallas_call x1, Pallas kernels, per_device(): pl.pallas_call(functools.partial(rim_kernel, subs), out_shape=(shape((K,...  1.55 us
    pallas_call x1, Pallas kernels, per_device(): pl.pallas_call(functools.partial(rows_kernel, count), out_shape=shape((9,...  1.48 us
  transfers between devices with their start and end apart: 4, of which 1 were waited for; matrix products, arithmetic and copies ran while one was open for 0% of the time, Pallas kernels for 18%

profile of v10, /device:TPU:1, one launch (start us, length us, event | category | flops | bytes accessed | tf_op | source)
XLA Modules:
  0.0 62.1 jit_solution(10756190211351728552)
XLA Ops:
  0.0 0.0 copy-start
  0.0 0.0 copy-start.4
  0.0 0.0 copy-start.2
  0.0 1.4 %collective-permute-start.1 = (bf16[3,3,128,256]{3,2,1,0:T(8,128)(2,1)}, bf16[3,3,128,256]{3,2,1,0:T(8,128)(2,1)S(1)}, u32[]{:S(2)}, u32[]{:S(2)}) collective-permute-start(bf16[3,3,128,256]{3,2,1,0:T(8,128)(2,1)} %own_ref.1), channel_id=1, source_target_pairs={{0,8},{8,0},{16,24},{24,16},{32,40},{40,32},{48,56},{56,48},{64,72... | collective-permute-start | bytes 1769480 | tf_op jit(solution)/shard_map/ppermute | solution.py:356
  1.4 2.2 %edges.1 = bf16[8,384,128]{2,1,0:T(8,128)(2,1)} custom-call(s32[2]{0:T(128)} %index_ref.1, bf16[3,3,128,256]{3,2,1,0:T(8,128)(2,1)} %own_ref.1), custom_call_target="tpu_custom_call" | custom-call | tf_op jit(solution)/shard_map/edges/pallas_call | solution.py:358
  3.7 7.7 %all-to-all-start = ((bf16[8,384,128]{2,1,0:T(8,128)(2,1)}), bf16[8,384,128]{2,1,0:T(8,128)(2,1)S(1)}, u32[]{:S(2)}, u32[]{:S(2)}) async-start(bf16[8,384,128]{2,1,0:T(8,128)(2,1)} %edges.1), calls=%async_computation | async-start | bytes 1572864 | tf_op jit(solution)/shard_map/all_to_all | solution.py:368
  11.3 0.0 copy-done.2
  11.3 0.4 collective-permute-start
  11.8 0.0 collective-permute-done.1.other_ref
  11.8 0.0 copy-done
  11.8 0.0 copy-done.4
  11.8 7.2 %inner.1 = (f32[9,576,128]{2,1,0:T(8,128)}, bf16[768,512]{1,0:T(8,128)(2,1)S(1)}) custom-call(s32[1,2]{1,0:T(1,128)S(1)} %bitcast.10, bf16[3,3,128,256]{3,2,1,0:T(8,128)(2,1)S(1)} %copy-done, bf16[3,3,128,256]{3,2,1,0:T(8,128)(2,1)S(1)} %collective-permute-done.1.other_ref), custom_call_target="tpu_custom_call" | custom-call | flops 6000000000 | bytes 5000000 | tf_op jit(solution)/shard_map/inner/pallas_call | solution.py:371
  18.9 0.0 collective-permute-done.halo_other_ref.halo_rows_other_ref
  19.0 5.5 %all-to-all-done = bf16[8,384,128]{2,1,0:T(8,128)(2,1)S(1)} async-done(((bf16[8,384,128]{2,1,0:T(8,128)(2,1)}), bf16[8,384,128]{2,1,0:T(8,128)(2,1)S(1)}, u32[]{:S(2)}, u32[]{:S(2)}) %all-to-all-start) | async-done | bytes 786464 | tf_op jit(solution)/shard_map/all_to_all | solution.py:368
  24.5 0.9 %gather.1.after_ref.tiles_own_ref = bf16[1536,128]{1,0:T(8,128)(2,1)S(1)} custom-call(s32[3,68]{1,0:T(4,128)S(1)} %copy-done.2, s32[3,68]{1,0:T(4,128)S(1)} %collective-permute-done.halo_other_ref.halo_rows_other_ref, bf16[3072,128]{1,0:T(8,128)(2,1)S(1)} %bitcast.7, bf16[768,512]{1,0:T(8,128)(2,1)S(1)} %get-tuple-element.11.after_ref.pairs_ref), custom_call_target="tpu_custom_call" | custom-call | tf_op jit(solution)/shard_map/gather/pallas_call | solution.py:390
  25.4 1.1 %collective-permute-start.2 = (bf16[1536,128]{1,0:T(8,128)(2,1)S(1)}, bf16[1536,128]{1,0:T(8,128)(2,1)S(1)}, u32[]{:S(2)}, u32[]{:S(2)}) collective-permute-start(bf16[1536,128]{1,0:T(8,128)(2,1)S(1)} %gather.1.after_ref.tiles_own_ref), channel_id=1, source_target_pairs={{0,8},{8,0},{16,24},{24,16},{32,40},{40,32},{48,56},{56,48},{64,72... | collective-permute-start | bytes 1179656 | tf_op jit(solution)/shard_map/ppermute | solution.py:398
  26.5 0.0 copy-start.3
  26.5 1.5 %rim.1 = (bf16[1152,768]{1,0:T(8,128)(2,1)S(1)}, bf16[256,1152]{1,0:T(8,128)(2,1)S(1)}, f32[128,128]{1,0:T(8,128)S(1)}, f32[4,576,128]{2,1,0:T(8,128)S(1)}) custom-call(bf16[768,512]{1,0:T(8,128)(2,1)S(1)} %get-tuple-element.11.after_ref.pairs_ref, bf16[1536,128]{1,0:T(8,128)(2,1)S(1)} %gather.1.after_ref.tiles_own_ref, ...), custom_call_target="tpu_custom_call" | custom-call | flops 1000000000 | bytes 6000000 | tf_op jit(solution)/shard_map/rim/pallas_call | solution.py:401
  28.1 0.0 collective-permute-done.2.tiles_other_ref
  28.1 0.0 copy-done.3
  28.1 3.6 %outer.1 = s16[5248,128]{1,0:T(8,128)(2,1)S(1)} custom-call(bf16[1536,128]{1,0:T(8,128)(2,1)S(1)} %gather.1.after_ref.tiles_own_ref, bf16[1536,128]{1,0:T(8,128)(2,1)S(1)} %collective-permute-done.2.tiles_other_ref, s32[3,68]{1,0:T(4,128)S(1)} %copy-done.2, s32[3,68]{1,0:T(4,128)S(1)} %collective-permute-done.halo_other_ref.halo_rows_other_ref, ...), custom_call_target="tpu_custom_call" | custom-call | tf_op jit(solution)/shard_map/outer/pallas_call | solution.py:417
  31.7 0.0 copy-start.1
  31.8 28.9 %all_to_all.10 = s16[64,41,2,128]{3,2,1,0:T(2,128)(2,1)S(1)} all-to-all(s16[64,41,2,128]{3,2,1,0:T(2,128)(2,1)S(1)} %bitcast.6), channel_id=1, replica_groups={{0,1,2,3,4,5,6,7,16,17,18,19,20,21,22,23,32,33,34,35,36,37,38,39,48,49,..., dimensions={0} | all-to-all | bytes 2686976 | tf_op jit(solution)/shard_map/all_to_all | solution.py:448
  60.7 0.0 copy-done.1
  60.7 1.5 %rows.1 = f32[9,1408]{1,0:T(8,128)} custom-call(s16[5248,128]{1,0:T(8,128)(2,1)S(1)} %bitcast.5, bf16[1152,256]{1,0:T(8,128)(2,1)S(1)} %copy-done.1, s32[1,128]{1,0:T(1,128)S(1)} %bitcast.9), custom_call_target="tpu_custom_call" | custom-call | tf_op jit(solution)/shard_map/rows/pallas_call | solution.py:450
Async XLA Ops:
  0.0 11.8 %copy-start = (bf16[3,3,128,256]{3,2,1,0:T(8,128)(2,1)S(1)}, bf16[3,3,128,256]{3,2,1,0:T(8,128)(2,1)}, u32[]{:S(2)}) copy-start(bf16[3,3,128,256]{3,2,1,0:T(8,128)(2,1)} %own_ref.1) | copy-start | bytes 1769476
  0.0 11.8 %copy-start.4 = (s32[2]{0:T(128)S(1)}, s32[2]{0:T(128)}, u32[]{:S(2)}) copy-start(s32[2]{0:T(128)} %index_ref.1) | copy-start | bytes 28
  0.0 11.3 %copy-start.2 = (s32[3,68]{1,0:T(4,128)S(1)}, s32[3,68]{1,0:T(4,128)}, u32[]{:S(2)}) copy-start(s32[3,68]{1,0:T(4,128)} %halo_rows_own_ref.1) | copy-start | bytes 2452
  0.0 11.8 %collective-permute-start.1 = (bf16[3,3,128,256]{3,2,1,0:T(8,128)(2,1)}, bf16[3,3,128,256]{3,2,1,0:T(8,128)(2,1)S(1)}, u32[]{:S(2)}, u32[]{:S(2)}) collective-permute-start(bf16[3,3,128,256]{3,2,1,0:T(8,128)(2,1)} %own_ref.1), channel_id=1, source_target_pairs={{0,8},{8,0},{16,24},{24,16},{32,40},{40,32},{48,56},{56,48},{64,72... | collective-permute-start | bytes 1769480 | tf_op jit(solution)/shard_map/ppermute | solution.py:356
  3.7 20.8 %all-to-all-start = ((bf16[8,384,128]{2,1,0:T(8,128)(2,1)}), bf16[8,384,128]{2,1,0:T(8,128)(2,1)S(1)}, u32[]{:S(2)}, u32[]{:S(2)}) async-start(bf16[8,384,128]{2,1,0:T(8,128)(2,1)} %edges.1), calls=%async_computation | async-start | bytes 1572864 | tf_op jit(solution)/shard_map/all_to_all | solution.py:368
  11.3 7.6 %collective-permute-start = (s32[3,68]{1,0:T(4,128)S(1)}, s32[3,68]{1,0:T(4,128)S(1)}, u32[]{:S(2)}, u32[]{:S(2)}) collective-permute-start(s32[3,68]{1,0:T(4,128)S(1)} %copy-done.2), channel_id=1, source_target_pairs={{0,8},{8,0},{16,24},{24,16},{32,40},{40,32},{48,56},{56,48},{64,72... | collective-permute-start | bytes 2456 | tf_op jit(solution)/shard_map/ppermute | solution.py:357
  25.4 2.7 %collective-permute-start.2 = (bf16[1536,128]{1,0:T(8,128)(2,1)S(1)}, bf16[1536,128]{1,0:T(8,128)(2,1)S(1)}, u32[]{:S(2)}, u32[]{:S(2)}) collective-permute-start(bf16[1536,128]{1,0:T(8,128)(2,1)S(1)} %gather.1.after_ref.tiles_own_ref), channel_id=1, source_target_pairs={{0,8},{8,0},{16,24},{24,16},{32,40},{40,32},{48,56},{56,48},{64,72... | collective-permute-start | bytes 1179656 | tf_op jit(solution)/shard_map/ppermute | solution.py:398
  26.5 1.6 %copy-start.3 = (s32[128]{0:T(128)S(1)}, s32[128]{0:T(128)}, u32[]{:S(2)}) copy-start(s32[128]{0:T(128)} %param.8) | copy-start | bytes 1540
  31.7 28.9 %copy-start.1 = (bf16[1152,256]{1,0:T(8,128)(2,1)S(1)}, bf16[1152,256]{1,0:T(8,128)(2,1)}, u32[]{:S(2)}) copy-start(bf16[1152,256]{1,0:T(8,128)(2,1)} %weight_ref.1) | copy-start | bytes 1769476

commit v11 on v10

--- a/solution.py
+++ b/solution.py
@@ -91,7 +91,7 @@
 
 
 def tap_blocks():
-    return [slice(0, 4), slice(4, 8), slice(8, TAPS)]
+    return [slice(0, 4), slice(4, 5), slice(5, TAPS)]
 
 
 def core_index():

time: 62.4 us -> 62.7 us (level)
  transfers between devices with their start and end apart: 4 -> 4, of which waited for: 1 -> 1; matrix products, arithmetic and copies ran while one was open for 0% -> 0% of each run, Pallas kernels for 18% -> 17%
where the time goes in v11:
time: 62.7 us; the launch traced here: 62.4 us
  blocking collectives  28.9 us (46%)
  Pallas kernels  17.1 us (27%)
  starting transfers between devices  10.7 us (17%)
  waiting for transfers between devices  5.65 us (9%)
    all_to_all x1, blocking collectives, per_device(): lax.all_to_all(message.reshape(64, -1, 2, CH), AXES, 0, 0, axis_index_gro...  28.9 us
    all_to_all x1, starting transfers between devices, per_device(): table = lax.all_to_all(copies, 'face', 0, 0, axis_index_groups=same_core)  7.68 us
    pallas_call x1, Pallas kernels, per_device(): pl.pallas_call(inner_kernel, out_shape=(pltpu.HBM((TAPS, HALF, CH), f32),...  7.03 us
    all_to_all x1, waiting for transfers between devices, per_device(): table = lax.all_to_all(copies, 'face', 0, 0, axis_index_groups=same_core)  5.64 us
    pallas_call x1, Pallas kernels, per_device(): pl.pallas_call(functools.partial(outer_kernel, subs), out_shape=shape((64...  3.94 us
    pallas_call x1, Pallas kernels, per_device(): pl.pallas_call(edges_kernel, out_shape=shape((faces // 2, 8 * subs * SIDE...  2.22 us
    pallas_call x1, Pallas kernels, per_device(): pl.pallas_call(functools.partial(rim_kernel, subs), out_shape=(shape((K,...  1.55 us
    pallas_call x1, Pallas kernels, per_device(): pl.pallas_call(functools.partial(rows_kernel, count), out_shape=shape((9,...  1.48 us
  transfers between devices with their start and end apart: 4, of which 1 were waited for; matrix products, arithmetic and copies ran while one was open for 0% of the time, Pallas kernels for 17%

profile of v11, /device:TPU:1, one launch (start us, length us, event | category | flops | bytes accessed | tf_op | source)
XLA Modules:
  0.0 62.4 jit_solution(11000576790246428616)
XLA Ops:
  0.0 0.0 copy-start
  0.0 0.0 copy-start.4
  0.0 0.0 copy-start.2
  0.0 1.4 %collective-permute-start.1 = (bf16[3,3,128,256]{3,2,1,0:T(8,128)(2,1)}, bf16[3,3,128,256]{3,2,1,0:T(8,128)(2,1)S(1)}, u32[]{:S(2)}, u32[]{:S(2)}) collective-permute-start(bf16[3,3,128,256]{3,2,1,0:T(8,128)(2,1)} %own_ref.1), channel_id=1, source_target_pairs={{0,8},{8,0},{16,24},{24,16},{32,40},{40,32},{48,56},{56,48},{64,72... | collective-permute-start | bytes 1769480 | tf_op jit(solution)/shard_map/ppermute | solution.py:356
  1.4 2.2 %edges.1 = bf16[8,384,128]{2,1,0:T(8,128)(2,1)} custom-call(s32[2]{0:T(128)} %index_ref.1, bf16[3,3,128,256]{3,2,1,0:T(8,128)(2,1)} %own_ref.1), custom_call_target="tpu_custom_call" | custom-call | tf_op jit(solution)/shard_map/edges/pallas_call | solution.py:358
  3.7 7.7 %all-to-all-start = ((bf16[8,384,128]{2,1,0:T(8,128)(2,1)}), bf16[8,384,128]{2,1,0:T(8,128)(2,1)S(1)}, u32[]{:S(2)}, u32[]{:S(2)}) async-start(bf16[8,384,128]{2,1,0:T(8,128)(2,1)} %edges.1), calls=%async_computation | async-start | bytes 1572864 | tf_op jit(solution)/shard_map/all_to_all | solution.py:368
  11.3 0.0 copy-done.2
  11.3 0.4 collective-permute-start
  11.8 0.0 collective-permute-done.1.other_ref
  11.8 0.0 copy-done
  11.8 0.0 copy-done.4
  11.8 7.0 %inner.1 = (f32[9,576,128]{2,1,0:T(8,128)}, bf16[768,512]{1,0:T(8,128)(2,1)S(1)}) custom-call(s32[1,2]{1,0:T(1,128)S(1)} %bitcast.10, bf16[3,3,128,256]{3,2,1,0:T(8,128)(2,1)S(1)} %copy-done, bf16[3,3,128,256]{3,2,1,0:T(8,128)(2,1)S(1)} %collective-permute-done.1.other_ref), custom_call_target="tpu_custom_call" | custom-call | flops 6000000000 | bytes 5000000 | tf_op jit(solution)/shard_map/inner/pallas_call | solution.py:371
  18.8 0.0 collective-permute-done.halo_other_ref.halo_rows_other_ref
  18.8 5.6 %all-to-all-done = bf16[8,384,128]{2,1,0:T(8,128)(2,1)S(1)} async-done(((bf16[8,384,128]{2,1,0:T(8,128)(2,1)}), bf16[8,384,128]{2,1,0:T(8,128)(2,1)S(1)}, u32[]{:S(2)}, u32[]{:S(2)}) %all-to-all-start) | async-done | bytes 786464 | tf_op jit(solution)/shard_map/all_to_all | solution.py:368
  24.5 0.9 %gather.1.after_ref.tiles_own_ref = bf16[1536,128]{1,0:T(8,128)(2,1)S(1)} custom-call(s32[3,68]{1,0:T(4,128)S(1)} %copy-done.2, s32[3,68]{1,0:T(4,128)S(1)} %collective-permute-done.halo_other_ref.halo_rows_other_ref, bf16[3072,128]{1,0:T(8,128)(2,1)S(1)} %bitcast.7, bf16[768,512]{1,0:T(8,128)(2,1)S(1)} %get-tuple-element.11.after_ref.pairs_ref), custom_call_target="tpu_custom_call" | custom-call | tf_op jit(solution)/shard_map/gather/pallas_call | solution.py:390
  25.4 1.1 %collective-permute-start.2 = (bf16[1536,128]{1,0:T(8,128)(2,1)S(1)}, bf16[1536,128]{1,0:T(8,128)(2,1)S(1)}, u32[]{:S(2)}, u32[]{:S(2)}) collective-permute-start(bf16[1536,128]{1,0:T(8,128)(2,1)S(1)} %gather.1.after_ref.tiles_own_ref), channel_id=1, source_target_pairs={{0,8},{8,0},{16,24},{24,16},{32,40},{40,32},{48,56},{56,48},{64,72... | collective-permute-start | bytes 1179656 | tf_op jit(solution)/shard_map/ppermute | solution.py:398
  26.5 0.0 copy-start.3
  26.5 1.5 %rim.1 = (bf16[1152,768]{1,0:T(8,128)(2,1)S(1)}, bf16[256,1152]{1,0:T(8,128)(2,1)S(1)}, f32[128,128]{1,0:T(8,128)S(1)}, f32[4,576,128]{2,1,0:T(8,128)S(1)}) custom-call(bf16[768,512]{1,0:T(8,128)(2,1)S(1)} %get-tuple-element.11.after_ref.pairs_ref, bf16[1536,128]{1,0:T(8,128)(2,1)S(1)} %gather.1.after_ref.tiles_own_ref, ...), custom_call_target="tpu_custom_call" | custom-call | flops 1000000000 | bytes 6000000 | tf_op jit(solution)/shard_map/rim/pallas_call | solution.py:401
  28.1 0.0 collective-permute-done.2.tiles_other_ref
  28.1 0.0 copy-done.3
  28.1 3.9 %outer.1 = s16[5248,128]{1,0:T(8,128)(2,1)S(1)} custom-call(bf16[1536,128]{1,0:T(8,128)(2,1)S(1)} %gather.1.after_ref.tiles_own_ref, bf16[1536,128]{1,0:T(8,128)(2,1)S(1)} %collective-permute-done.2.tiles_other_ref, s32[3,68]{1,0:T(4,128)S(1)} %copy-done.2, s32[3,68]{1,0:T(4,128)S(1)} %collective-permute-done.halo_other_ref.halo_rows_other_ref, ...), custom_call_target="tpu_custom_call" | custom-call | tf_op jit(solution)/shard_map/outer/pallas_call | solution.py:417
  32.0 0.0 copy-start.1
  32.1 28.9 %all_to_all.10 = s16[64,41,2,128]{3,2,1,0:T(2,128)(2,1)S(1)} all-to-all(s16[64,41,2,128]{3,2,1,0:T(2,128)(2,1)S(1)} %bitcast.6), channel_id=1, replica_groups={{0,1,2,3,4,5,6,7,16,17,18,19,20,21,22,23,32,33,34,35,36,37,38,39,48,49,..., dimensions={0} | all-to-all | bytes 2686976 | tf_op jit(solution)/shard_map/all_to_all | solution.py:448
  61.0 0.0 copy-done.1
  61.0 1.5 %rows.1 = f32[9,1408]{1,0:T(8,128)} custom-call(s16[5248,128]{1,0:T(8,128)(2,1)S(1)} %bitcast.5, bf16[1152,256]{1,0:T(8,128)(2,1)S(1)} %copy-done.1, s32[1,128]{1,0:T(1,128)S(1)} %bitcast.9), custom_call_target="tpu_custom_call" | custom-call | tf_op jit(solution)/shard_map/rows/pallas_call | solution.py:450
Async XLA Ops:
  0.0 11.8 %copy-start = (bf16[3,3,128,256]{3,2,1,0:T(8,128)(2,1)S(1)}, bf16[3,3,128,256]{3,2,1,0:T(8,128)(2,1)}, u32[]{:S(2)}) copy-start(bf16[3,3,128,256]{3,2,1,0:T(8,128)(2,1)} %own_ref.1) | copy-start | bytes 1769476
  0.0 11.8 %copy-start.4 = (s32[2]{0:T(128)S(1)}, s32[2]{0:T(128)}, u32[]{:S(2)}) copy-start(s32[2]{0:T(128)} %index_ref.1) | copy-start | bytes 28
  0.0 11.3 %copy-start.2 = (s32[3,68]{1,0:T(4,128)S(1)}, s32[3,68]{1,0:T(4,128)}, u32[]{:S(2)}) copy-start(s32[3,68]{1,0:T(4,128)} %halo_rows_own_ref.1) | copy-start | bytes 2452
  0.0 11.8 %collective-permute-start.1 = (bf16[3,3,128,256]{3,2,1,0:T(8,128)(2,1)}, bf16[3,3,128,256]{3,2,1,0:T(8,128)(2,1)S(1)}, u32[]{:S(2)}, u32[]{:S(2)}) collective-permute-start(bf16[3,3,128,256]{3,2,1,0:T(8,128)(2,1)} %own_ref.1), channel_id=1, source_target_pairs={{0,8},{8,0},{16,24},{24,16},{32,40},{40,32},{48,56},{56,48},{64,72... | collective-permute-start | bytes 1769480 | tf_op jit(solution)/shard_map/ppermute | solution.py:356
  3.7 20.8 %all-to-all-start = ((bf16[8,384,128]{2,1,0:T(8,128)(2,1)}), bf16[8,384,128]{2,1,0:T(8,128)(2,1)S(1)}, u32[]{:S(2)}, u32[]{:S(2)}) async-start(bf16[8,384,128]{2,1,0:T(8,128)(2,1)} %edges.1), calls=%async_computation | async-start | bytes 1572864 | tf_op jit(solution)/shard_map/all_to_all | solution.py:368
  11.3 7.5 %collective-permute-start = (s32[3,68]{1,0:T(4,128)S(1)}, s32[3,68]{1,0:T(4,128)S(1)}, u32[]{:S(2)}, u32[]{:S(2)}) collective-permute-start(s32[3,68]{1,0:T(4,128)S(1)} %copy-done.2), channel_id=1, source_target_pairs={{0,8},{8,0},{16,24},{24,16},{32,40},{40,32},{48,56},{56,48},{64,72... | collective-permute-start | bytes 2456 | tf_op jit(solution)/shard_map/ppermute | solution.py:357
  25.4 2.7 %collective-permute-start.2 = (bf16[1536,128]{1,0:T(8,128)(2,1)S(1)}, bf16[1536,128]{1,0:T(8,128)(2,1)S(1)}, u32[]{:S(2)}, u32[]{:S(2)}) collective-permute-start(bf16[1536,128]{1,0:T(8,128)(2,1)S(1)} %gather.1.after_ref.tiles_own_ref), channel_id=1, source_target_pairs={{0,8},{8,0},{16,24},{24,16},{32,40},{40,32},{48,56},{56,48},{64,72... | collective-permute-start | bytes 1179656 | tf_op jit(solution)/shard_map/ppermute | solution.py:398
  26.5 1.6 %copy-start.3 = (s32[128]{0:T(128)S(1)}, s32[128]{0:T(128)}, u32[]{:S(2)}) copy-start(s32[128]{0:T(128)} %param.8) | copy-start | bytes 1540
  32.0 28.9 %copy-start.1 = (bf16[1152,256]{1,0:T(8,128)(2,1)S(1)}, bf16[1152,256]{1,0:T(8,128)(2,1)}, u32[]{:S(2)}) copy-start(bf16[1152,256]{1,0:T(8,128)(2,1)} %weight_ref.1) | copy-start | bytes 1769476

commit v12 on v10

--- a/solution.py
+++ b/solution.py
@@ -22,7 +22,7 @@
 STEPS = 16
 TOP = 32700.0
 THIRD = 43
-GROUP = 4
+GROUP = 8
 AXES = ("face", "sample")
 NT = (((1,), (1,)), ((), ()))
 SIDE_AT = (1, 19, 36, 52)

time: 62.4 us -> 62.3 us (level)
  no operation moved by 1% of the time
where the time goes in v12:
time: 62.3 us; the launch traced here: 62.1 us
  blocking collectives  28.9 us (46%)
  Pallas kernels  16.9 us (27%)
  starting transfers between devices  10.7 us (17%)
  waiting for transfers between devices  5.51 us (9%)
    all_to_all x1, blocking collectives, per_device(): lax.all_to_all(message.reshape(64, -1, 2, CH), AXES, 0, 0, axis_index_gro...  28.9 us
    all_to_all x1, starting transfers between devices, per_device(): table = lax.all_to_all(copies, 'face', 0, 0, axis_index_groups=same_core)  7.68 us
    pallas_call x1, Pallas kernels, per_device(): pl.pallas_call(inner_kernel, out_shape=(pltpu.HBM((TAPS, HALF, CH), f32),...  7.16 us
    all_to_all x1, waiting for transfers between devices, per_device(): table = lax.all_to_all(copies, 'face', 0, 0, axis_index_groups=same_core)  5.5 us
    pallas_call x1, Pallas kernels, per_device(): pl.pallas_call(functools.partial(outer_kernel, subs), out_shape=shape((64...  3.63 us
    pallas_call x1, Pallas kernels, per_device(): pl.pallas_call(edges_kernel, out_shape=shape((faces // 2, 8 * subs * SIDE...  2.22 us
    pallas_call x1, Pallas kernels, per_device(): pl.pallas_call(functools.partial(rim_kernel, subs), out_shape=(shape((K,...  1.55 us
    pallas_call x1, Pallas kernels, per_device(): pl.pallas_call(functools.partial(rows_kernel, count), out_shape=shape((9,...  1.43 us
  transfers between devices with their start and end apart: 4, of which 1 were waited for; matrix products, arithmetic and copies ran while one was open for 0% of the time, Pallas kernels for 18%

profile of v12, /device:TPU:1, one launch (start us, length us, event | category | flops | bytes accessed | tf_op | source)
XLA Modules:
  0.0 62.1 jit_solution(12812706041714727658)
XLA Ops:
  0.0 0.0 copy-start
  0.0 0.0 copy-start.4
  0.0 0.0 copy-start.2
  0.0 1.4 %collective-permute-start.1 = (bf16[3,3,128,256]{3,2,1,0:T(8,128)(2,1)}, bf16[3,3,128,256]{3,2,1,0:T(8,128)(2,1)S(1)}, u32[]{:S(2)}, u32[]{:S(2)}) collective-permute-start(bf16[3,3,128,256]{3,2,1,0:T(8,128)(2,1)} %own_ref.1), channel_id=1, source_target_pairs={{0,8},{8,0},{16,24},{24,16},{32,40},{40,32},{48,56},{56,48},{64,72... | collective-permute-start | bytes 1769480 | tf_op jit(solution)/shard_map/ppermute | solution.py:356
  1.4 2.2 %edges.1 = bf16[8,384,128]{2,1,0:T(8,128)(2,1)} custom-call(s32[2]{0:T(128)} %index_ref.1, bf16[3,3,128,256]{3,2,1,0:T(8,128)(2,1)} %own_ref.1), custom_call_target="tpu_custom_call" | custom-call | tf_op jit(solution)/shard_map/edges/pallas_call | solution.py:358
  3.7 7.7 %all-to-all-start = ((bf16[8,384,128]{2,1,0:T(8,128)(2,1)}), bf16[8,384,128]{2,1,0:T(8,128)(2,1)S(1)}, u32[]{:S(2)}, u32[]{:S(2)}) async-start(bf16[8,384,128]{2,1,0:T(8,128)(2,1)} %edges.1), calls=%async_computation | async-start | bytes 1572864 | tf_op jit(solution)/shard_map/all_to_all | solution.py:368
  11.3 0.0 copy-done.2
  11.3 0.4 collective-permute-start
  11.8 0.0 collective-permute-done.1.other_ref
  11.8 0.0 copy-done
  11.8 0.0 copy-done.4
  11.8 7.2 %inner.1 = (f32[9,576,128]{2,1,0:T(8,128)}, bf16[768,512]{1,0:T(8,128)(2,1)S(1)}) custom-call(s32[1,2]{1,0:T(1,128)S(1)} %bitcast.10, bf16[3,3,128,256]{3,2,1,0:T(8,128)(2,1)S(1)} %copy-done, bf16[3,3,128,256]{3,2,1,0:T(8,128)(2,1)S(1)} %collective-permute-done.1.other_ref), custom_call_target="tpu_custom_call" | custom-call | flops 6000000000 | bytes 5000000 | tf_op jit(solution)/shard_map/inner/pallas_call | solution.py:371
  18.9 0.0 collective-permute-done.halo_other_ref.halo_rows_other_ref
  19.0 5.5 %all-to-all-done = bf16[8,384,128]{2,1,0:T(8,128)(2,1)S(1)} async-done(((bf16[8,384,128]{2,1,0:T(8,128)(2,1)}), bf16[8,384,128]{2,1,0:T(8,128)(2,1)S(1)}, u32[]{:S(2)}, u32[]{:S(2)}) %all-to-all-start) | async-done | bytes 786464 | tf_op jit(solution)/shard_map/all_to_all | solution.py:368
  24.5 0.9 %gather.1.after_ref.tiles_own_ref = bf16[1536,128]{1,0:T(8,128)(2,1)S(1)} custom-call(s32[3,68]{1,0:T(4,128)S(1)} %copy-done.2, s32[3,68]{1,0:T(4,128)S(1)} %collective-permute-done.halo_other_ref.halo_rows_other_ref, bf16[3072,128]{1,0:T(8,128)(2,1)S(1)} %bitcast.7, bf16[768,512]{1,0:T(8,128)(2,1)S(1)} %get-tuple-element.11.after_ref.pairs_ref), custom_call_target="tpu_custom_call" | custom-call | tf_op jit(solution)/shard_map/gather/pallas_call | solution.py:390
  25.4 1.1 %collective-permute-start.2 = (bf16[1536,128]{1,0:T(8,128)(2,1)S(1)}, bf16[1536,128]{1,0:T(8,128)(2,1)S(1)}, u32[]{:S(2)}, u32[]{:S(2)}) collective-permute-start(bf16[1536,128]{1,0:T(8,128)(2,1)S(1)} %gather.1.after_ref.tiles_own_ref), channel_id=1, source_target_pairs={{0,8},{8,0},{16,24},{24,16},{32,40},{40,32},{48,56},{56,48},{64,72... | collective-permute-start | bytes 1179656 | tf_op jit(solution)/shard_map/ppermute | solution.py:398
  26.5 0.0 copy-start.3
  26.5 1.5 %rim.1 = (bf16[1152,768]{1,0:T(8,128)(2,1)S(1)}, bf16[256,1152]{1,0:T(8,128)(2,1)S(1)}, f32[128,128]{1,0:T(8,128)S(1)}, f32[4,576,128]{2,1,0:T(8,128)S(1)}) custom-call(bf16[768,512]{1,0:T(8,128)(2,1)S(1)} %get-tuple-element.11.after_ref.pairs_ref, bf16[1536,128]{1,0:T(8,128)(2,1)S(1)} %gather.1.after_ref.tiles_own_ref, ...), custom_call_target="tpu_custom_call" | custom-call | flops 1000000000 | bytes 6000000 | tf_op jit(solution)/shard_map/rim/pallas_call | solution.py:401
  28.1 0.0 collective-permute-done.2.tiles_other_ref
  28.1 0.0 copy-done.3
  28.1 3.6 %outer.1 = s16[5248,128]{1,0:T(8,128)(2,1)S(1)} custom-call(bf16[1536,128]{1,0:T(8,128)(2,1)S(1)} %gather.1.after_ref.tiles_own_ref, bf16[1536,128]{1,0:T(8,128)(2,1)S(1)} %collective-permute-done.2.tiles_other_ref, s32[3,68]{1,0:T(4,128)S(1)} %copy-done.2, s32[3,68]{1,0:T(4,128)S(1)} %collective-permute-done.halo_other_ref.halo_rows_other_ref, ...), custom_call_target="tpu_custom_call" | custom-call | tf_op jit(solution)/shard_map/outer/pallas_call | solution.py:417
  31.7 0.0 copy-start.1
  31.7 28.9 %all_to_all.10 = s16[64,41,2,128]{3,2,1,0:T(2,128)(2,1)S(1)} all-to-all(s16[64,41,2,128]{3,2,1,0:T(2,128)(2,1)S(1)} %bitcast.6), channel_id=1, replica_groups={{0,1,2,3,4,5,6,7,16,17,18,19,20,21,22,23,32,33,34,35,36,37,38,39,48,49,..., dimensions={0} | all-to-all | bytes 2686976 | tf_op jit(solution)/shard_map/all_to_all | solution.py:448
  60.6 0.0 copy-done.1
  60.7 1.4 %rows.1 = f32[9,1408]{1,0:T(8,128)} custom-call(s16[5248,128]{1,0:T(8,128)(2,1)S(1)} %bitcast.5, bf16[1152,256]{1,0:T(8,128)(2,1)S(1)} %copy-done.1, s32[1,128]{1,0:T(1,128)S(1)} %bitcast.9), custom_call_target="tpu_custom_call" | custom-call | tf_op jit(solution)/shard_map/rows/pallas_call | solution.py:450
Async XLA Ops:
  0.0 11.8 %copy-start = (bf16[3,3,128,256]{3,2,1,0:T(8,128)(2,1)S(1)}, bf16[3,3,128,256]{3,2,1,0:T(8,128)(2,1)}, u32[]{:S(2)}) copy-start(bf16[3,3,128,256]{3,2,1,0:T(8,128)(2,1)} %own_ref.1) | copy-start | bytes 1769476
  0.0 11.8 %copy-start.4 = (s32[2]{0:T(128)S(1)}, s32[2]{0:T(128)}, u32[]{:S(2)}) copy-start(s32[2]{0:T(128)} %index_ref.1) | copy-start | bytes 28
  0.0 11.3 %copy-start.2 = (s32[3,68]{1,0:T(4,128)S(1)}, s32[3,68]{1,0:T(4,128)}, u32[]{:S(2)}) copy-start(s32[3,68]{1,0:T(4,128)} %halo_rows_own_ref.1) | copy-start | bytes 2452
  0.0 11.8 %collective-permute-start.1 = (bf16[3,3,128,256]{3,2,1,0:T(8,128)(2,1)}, bf16[3,3,128,256]{3,2,1,0:T(8,128)(2,1)S(1)}, u32[]{:S(2)}, u32[]{:S(2)}) collective-permute-start(bf16[3,3,128,256]{3,2,1,0:T(8,128)(2,1)} %own_ref.1), channel_id=1, source_target_pairs={{0,8},{8,0},{16,24},{24,16},{32,40},{40,32},{48,56},{56,48},{64,72... | collective-permute-start | bytes 1769480 | tf_op jit(solution)/shard_map/ppermute | solution.py:356
  3.7 20.8 %all-to-all-start = ((bf16[8,384,128]{2,1,0:T(8,128)(2,1)}), bf16[8,384,128]{2,1,0:T(8,128)(2,1)S(1)}, u32[]{:S(2)}, u32[]{:S(2)}) async-start(bf16[8,384,128]{2,1,0:T(8,128)(2,1)} %edges.1), calls=%async_computation | async-start | bytes 1572864 | tf_op jit(solution)/shard_map/all_to_all | solution.py:368
  11.3 7.6 %collective-permute-start = (s32[3,68]{1,0:T(4,128)S(1)}, s32[3,68]{1,0:T(4,128)S(1)}, u32[]{:S(2)}, u32[]{:S(2)}) collective-permute-start(s32[3,68]{1,0:T(4,128)S(1)} %copy-done.2), channel_id=1, source_target_pairs={{0,8},{8,0},{16,24},{24,16},{32,40},{40,32},{48,56},{56,48},{64,72... | collective-permute-start | bytes 2456 | tf_op jit(solution)/shard_map/ppermute | solution.py:357
  25.4 2.7 %collective-permute-start.2 = (bf16[1536,128]{1,0:T(8,128)(2,1)S(1)}, bf16[1536,128]{1,0:T(8,128)(2,1)S(1)}, u32[]{:S(2)}, u32[]{:S(2)}) collective-permute-start(bf16[1536,128]{1,0:T(8,128)(2,1)S(1)} %gather.1.after_ref.tiles_own_ref), channel_id=1, source_target_pairs={{0,8},{8,0},{16,24},{24,16},{32,40},{40,32},{48,56},{56,48},{64,72... | collective-permute-start | bytes 1179656 | tf_op jit(solution)/shard_map/ppermute | solution.py:398
  26.5 1.6 %copy-start.3 = (s32[128]{0:T(128)S(1)}, s32[128]{0:T(128)}, u32[]{:S(2)}) copy-start(s32[128]{0:T(128)} %param.8) | copy-start | bytes 1540
  31.7 28.9 %copy-start.1 = (bf16[1152,256]{1,0:T(8,128)(2,1)S(1)}, bf16[1152,256]{1,0:T(8,128)(2,1)}, u32[]{:S(2)}) copy-start(bf16[1152,256]{1,0:T(8,128)(2,1)} %weight_ref.1) | copy-start | bytes 1769476

commit v13 on v12

--- a/solution.py
+++ b/solution.py
@@ -22,7 +22,7 @@
 STEPS = 16
 TOP = 32700.0
 THIRD = 43
-GROUP = 8
+GROUP = 16
 AXES = ("face", "sample")
 NT = (((1,), (1,)), ((), ()))
 SIDE_AT = (1, 19, 36, 52)
@@ -302,10 +302,10 @@
 def rows_kernel(count, landed_ref, weight_ref, kept_ref, out_ref, rows, split, stage):
     owner = lax.axis_index("face") * lax.axis_size("sample") + lax.axis_index("sample")
     total = jnp.zeros((ROWS, CH), jnp.float32)
-    for j in range(0, landed_ref.shape[0] // ROWS, 2 * GROUP):
-        block = stage.at[j // (2 * GROUP) % 4]
-        block[...] = landed_ref[j * ROWS : (j + 2 * GROUP) * ROWS, :].astype(jnp.int32).astype(jnp.float32)
-        for i in range(2 * GROUP):
+    for j in range(0, landed_ref.shape[0] // ROWS, GROUP):
+        block = stage.at[j // (GROUP) % 4]
+        block[...] = landed_ref[j * ROWS : (j + GROUP) * ROWS, :].astype(jnp.int32).astype(jnp.float32)
+        for i in range(GROUP):
             codes = block[i * ROWS : (i + 1) * ROWS, :]
             total += codes * jnp.abs(codes) * jnp.exp2(block[i * ROWS + 81 : (i + 1) * ROWS, :] * (1 / STEPS))
     total = total * TOP**-2
@@ -452,7 +452,7 @@
         out_shape=shape((9, K + weight.shape[1]), f32),
         in_specs=[VMEM] * 3,
         out_specs=VMEM,
-        scratch_shapes=[pltpu.VMEM((16, K), f32), pltpu.VMEM((48, K), bf16), pltpu.VMEM((4, 2 * GROUP * ROWS, CH), f32)],
+        scratch_shapes=[pltpu.VMEM((16, K), f32), pltpu.VMEM((48, K), bf16), pltpu.VMEM((4, GROUP * ROWS, CH), f32)],
         compiler_params=pltpu.CompilerParams(vmem_limit_bytes=8 * 2**20),
         name="rows",
     )(landed, weight, mask_row)

time: 62.3 us -> 62.3 us (level)
  no operation moved by 1% of the time
where the time goes in v13:
time: 62.3 us; the launch traced here: 62.1 us
  blocking collectives  28.9 us (46%)
  Pallas kernels  16.9 us (27%)
  starting transfers between devices  10.7 us (17%)
  waiting for transfers between devices  5.51 us (9%)
    all_to_all x1, blocking collectives, per_device(): lax.all_to_all(message.reshape(64, -1, 2, CH), AXES, 0, 0, axis_index_gro...  28.9 us
    all_to_all x1, starting transfers between devices, per_device(): table = lax.all_to_all(copies, 'face', 0, 0, axis_index_groups=same_core)  7.68 us
    pallas_call x1, Pallas kernels, per_device(): pl.pallas_call(inner_kernel, out_shape=(pltpu.HBM((TAPS, HALF, CH), f32),...  7.16 us
    all_to_all x1, waiting for transfers between devices, per_device(): table = lax.all_to_all(copies, 'face', 0, 0, axis_index_groups=same_core)  5.5 us
    pallas_call x1, Pallas kernels, per_device(): pl.pallas_call(functools.partial(outer_kernel, subs), out_shape=shape((64...  3.61 us
    pallas_call x1, Pallas kernels, per_device(): pl.pallas_call(edges_kernel, out_shape=shape((faces // 2, 8 * subs * SIDE...  2.22 us
    pallas_call x1, Pallas kernels, per_device(): pl.pallas_call(functools.partial(rim_kernel, subs), out_shape=(shape((K,...  1.55 us
    pallas_call x1, Pallas kernels, per_device(): pl.pallas_call(functools.partial(rows_kernel, count), out_shape=shape((9,...  1.43 us
  transfers between devices with their start and end apart: 4, of which 1 were waited for; matrix products, arithmetic and copies ran while one was open for 0% of the time, Pallas kernels for 18%

profile of v13, /device:TPU:1, one launch (start us, length us, event | category | flops | bytes accessed | tf_op | source)
XLA Modules:
  0.0 62.1 jit_solution(3466115523545760141)
XLA Ops:
  0.0 0.0 copy-start
  0.0 0.0 copy-start.4
  0.0 0.0 copy-start.2
  0.0 1.4 %collective-permute-start.1 = (bf16[3,3,128,256]{3,2,1,0:T(8,128)(2,1)}, bf16[3,3,128,256]{3,2,1,0:T(8,128)(2,1)S(1)}, u32[]{:S(2)}, u32[]{:S(2)}) collective-permute-start(bf16[3,3,128,256]{3,2,1,0:T(8,128)(2,1)} %own_ref.1), channel_id=1, source_target_pairs={{0,8},{8,0},{16,24},{24,16},{32,40},{40,32},{48,56},{56,48},{64,72... | collective-permute-start | bytes 1769480 | tf_op jit(solution)/shard_map/ppermute | solution.py:356
  1.4 2.2 %edges.1 = bf16[8,384,128]{2,1,0:T(8,128)(2,1)} custom-call(s32[2]{0:T(128)} %index_ref.1, bf16[3,3,128,256]{3,2,1,0:T(8,128)(2,1)} %own_ref.1), custom_call_target="tpu_custom_call" | custom-call | tf_op jit(solution)/shard_map/edges/pallas_call | solution.py:358
  3.7 7.7 %all-to-all-start = ((bf16[8,384,128]{2,1,0:T(8,128)(2,1)}), bf16[8,384,128]{2,1,0:T(8,128)(2,1)S(1)}, u32[]{:S(2)}, u32[]{:S(2)}) async-start(bf16[8,384,128]{2,1,0:T(8,128)(2,1)} %edges.1), calls=%async_computation | async-start | bytes 1572864 | tf_op jit(solution)/shard_map/all_to_all | solution.py:368
  11.3 0.0 copy-done.2
  11.3 0.4 collective-permute-start
  11.8 0.0 collective-permute-done.1.other_ref
  11.8 0.0 copy-done
  11.8 0.0 copy-done.4
  11.8 7.2 %inner.1 = (f32[9,576,128]{2,1,0:T(8,128)}, bf16[768,512]{1,0:T(8,128)(2,1)S(1)}) custom-call(s32[1,2]{1,0:T(1,128)S(1)} %bitcast.10, bf16[3,3,128,256]{3,2,1,0:T(8,128)(2,1)S(1)} %copy-done, bf16[3,3,128,256]{3,2,1,0:T(8,128)(2,1)S(1)} %collective-permute-done.1.other_ref), custom_call_target="tpu_custom_call" | custom-call | flops 6000000000 | bytes 5000000 | tf_op jit(solution)/shard_map/inner/pallas_call | solution.py:371
  18.9 0.0 collective-permute-done.halo_other_ref.halo_rows_other_ref
  19.0 5.5 %all-to-all-done = bf16[8,384,128]{2,1,0:T(8,128)(2,1)S(1)} async-done(((bf16[8,384,128]{2,1,0:T(8,128)(2,1)}), bf16[8,384,128]{2,1,0:T(8,128)(2,1)S(1)}, u32[]{:S(2)}, u32[]{:S(2)}) %all-to-all-start) | async-done | bytes 786464 | tf_op jit(solution)/shard_map/all_to_all | solution.py:368
  24.5 0.9 %gather.1.after_ref.tiles_own_ref = bf16[1536,128]{1,0:T(8,128)(2,1)S(1)} custom-call(s32[3,68]{1,0:T(4,128)S(1)} %copy-done.2, s32[3,68]{1,0:T(4,128)S(1)} %collective-permute-done.halo_other_ref.halo_rows_other_ref, bf16[3072,128]{1,0:T(8,128)(2,1)S(1)} %bitcast.7, bf16[768,512]{1,0:T(8,128)(2,1)S(1)} %get-tuple-element.11.after_ref.pairs_ref), custom_call_target="tpu_custom_call" | custom-call | tf_op jit(solution)/shard_map/gather/pallas_call | solution.py:390
  25.4 1.1 %collective-permute-start.2 = (bf16[1536,128]{1,0:T(8,128)(2,1)S(1)}, bf16[1536,128]{1,0:T(8,128)(2,1)S(1)}, u32[]{:S(2)}, u32[]{:S(2)}) collective-permute-start(bf16[1536,128]{1,0:T(8,128)(2,1)S(1)} %gather.1.after_ref.tiles_own_ref), channel_id=1, source_target_pairs={{0,8},{8,0},{16,24},{24,16},{32,40},{40,32},{48,56},{56,48},{64,72... | collective-permute-start | bytes 1179656 | tf_op jit(solution)/shard_map/ppermute | solution.py:398
  26.5 0.0 copy-start.3
  26.5 1.5 %rim.1 = (bf16[1152,768]{1,0:T(8,128)(2,1)S(1)}, bf16[256,1152]{1,0:T(8,128)(2,1)S(1)}, f32[128,128]{1,0:T(8,128)S(1)}, f32[4,576,128]{2,1,0:T(8,128)S(1)}) custom-call(bf16[768,512]{1,0:T(8,128)(2,1)S(1)} %get-tuple-element.11.after_ref.pairs_ref, bf16[1536,128]{1,0:T(8,128)(2,1)S(1)} %gather.1.after_ref.tiles_own_ref, ...), custom_call_target="tpu_custom_call" | custom-call | flops 1000000000 | bytes 6000000 | tf_op jit(solution)/shard_map/rim/pallas_call | solution.py:401
  28.1 0.0 collective-permute-done.2.tiles_other_ref
  28.1 0.0 copy-done.3
  28.1 3.6 %outer.1 = s16[5248,128]{1,0:T(8,128)(2,1)S(1)} custom-call(bf16[1536,128]{1,0:T(8,128)(2,1)S(1)} %gather.1.after_ref.tiles_own_ref, bf16[1536,128]{1,0:T(8,128)(2,1)S(1)} %collective-permute-done.2.tiles_other_ref, s32[3,68]{1,0:T(4,128)S(1)} %copy-done.2, s32[3,68]{1,0:T(4,128)S(1)} %collective-permute-done.halo_other_ref.halo_rows_other_ref, ...), custom_call_target="tpu_custom_call" | custom-call | tf_op jit(solution)/shard_map/outer/pallas_call | solution.py:417
  31.7 0.0 copy-start.1
  31.7 28.9 %all_to_all.10 = s16[64,41,2,128]{3,2,1,0:T(2,128)(2,1)S(1)} all-to-all(s16[64,41,2,128]{3,2,1,0:T(2,128)(2,1)S(1)} %bitcast.6), channel_id=1, replica_groups={{0,1,2,3,4,5,6,7,16,17,18,19,20,21,22,23,32,33,34,35,36,37,38,39,48,49,..., dimensions={0} | all-to-all | bytes 2686976 | tf_op jit(solution)/shard_map/all_to_all | solution.py:448
  60.6 0.0 copy-done.1
  60.6 1.4 %rows.1 = f32[9,1408]{1,0:T(8,128)} custom-call(s16[5248,128]{1,0:T(8,128)(2,1)S(1)} %bitcast.5, bf16[1152,256]{1,0:T(8,128)(2,1)S(1)} %copy-done.1, s32[1,128]{1,0:T(1,128)S(1)} %bitcast.9), custom_call_target="tpu_custom_call" | custom-call | tf_op jit(solution)/shard_map/rows/pallas_call | solution.py:450
Async XLA Ops:
  0.0 11.8 %copy-start = (bf16[3,3,128,256]{3,2,1,0:T(8,128)(2,1)S(1)}, bf16[3,3,128,256]{3,2,1,0:T(8,128)(2,1)}, u32[]{:S(2)}) copy-start(bf16[3,3,128,256]{3,2,1,0:T(8,128)(2,1)} %own_ref.1) | copy-start | bytes 1769476
  0.0 11.8 %copy-start.4 = (s32[2]{0:T(128)S(1)}, s32[2]{0:T(128)}, u32[]{:S(2)}) copy-start(s32[2]{0:T(128)} %index_ref.1) | copy-start | bytes 28
  0.0 11.3 %copy-start.2 = (s32[3,68]{1,0:T(4,128)S(1)}, s32[3,68]{1,0:T(4,128)}, u32[]{:S(2)}) copy-start(s32[3,68]{1,0:T(4,128)} %halo_rows_own_ref.1) | copy-start | bytes 2452
  0.0 11.8 %collective-permute-start.1 = (bf16[3,3,128,256]{3,2,1,0:T(8,128)(2,1)}, bf16[3,3,128,256]{3,2,1,0:T(8,128)(2,1)S(1)}, u32[]{:S(2)}, u32[]{:S(2)}) collective-permute-start(bf16[3,3,128,256]{3,2,1,0:T(8,128)(2,1)} %own_ref.1), channel_id=1, source_target_pairs={{0,8},{8,0},{16,24},{24,16},{32,40},{40,32},{48,56},{56,48},{64,72... | collective-permute-start | bytes 1769480 | tf_op jit(solution)/shard_map/ppermute | solution.py:356
  3.7 20.8 %all-to-all-start = ((bf16[8,384,128]{2,1,0:T(8,128)(2,1)}), bf16[8,384,128]{2,1,0:T(8,128)(2,1)S(1)}, u32[]{:S(2)}, u32[]{:S(2)}) async-start(bf16[8,384,128]{2,1,0:T(8,128)(2,1)} %edges.1), calls=%async_computation | async-start | bytes 1572864 | tf_op jit(solution)/shard_map/all_to_all | solution.py:368
  11.3 7.6 %collective-permute-start = (s32[3,68]{1,0:T(4,128)S(1)}, s32[3,68]{1,0:T(4,128)S(1)}, u32[]{:S(2)}, u32[]{:S(2)}) collective-permute-start(s32[3,68]{1,0:T(4,128)S(1)} %copy-done.2), channel_id=1, source_target_pairs={{0,8},{8,0},{16,24},{24,16},{32,40},{40,32},{48,56},{56,48},{64,72... | collective-permute-start | bytes 2456 | tf_op jit(solution)/shard_map/ppermute | solution.py:357
  25.4 2.7 %collective-permute-start.2 = (bf16[1536,128]{1,0:T(8,128)(2,1)S(1)}, bf16[1536,128]{1,0:T(8,128)(2,1)S(1)}, u32[]{:S(2)}, u32[]{:S(2)}) collective-permute-start(bf16[1536,128]{1,0:T(8,128)(2,1)S(1)} %gather.1.after_ref.tiles_own_ref), channel_id=1, source_target_pairs={{0,8},{8,0},{16,24},{24,16},{32,40},{40,32},{48,56},{56,48},{64,72... | collective-permute-start | bytes 1179656 | tf_op jit(solution)/shard_map/ppermute | solution.py:398
  26.5 1.6 %copy-start.3 = (s32[128]{0:T(128)S(1)}, s32[128]{0:T(128)}, u32[]{:S(2)}) copy-start(s32[128]{0:T(128)} %param.8) | copy-start | bytes 1540
  31.7 28.9 %copy-start.1 = (bf16[1152,256]{1,0:T(8,128)(2,1)S(1)}, bf16[1152,256]{1,0:T(8,128)(2,1)}, u32[]{:S(2)}) copy-start(bf16[1152,256]{1,0:T(8,128)(2,1)} %weight_ref.1) | copy-start | bytes 1769476
